TPU v7x, 128 devices: a whole 4x4x4 slice. The times are simulated.
128 devices in a mesh: dp: 16 (over y_lo, x, core), tensor: 8 (over z, y_hi).
Axes of the slice: x: 4, y: 4 (y_hi: 2, y_lo: 2; y = y_hi * 2 + y_lo), z: 4, core: 2. Of those that a mesh axis runs over, the one named last changes fastest.
Arguments:
- hidden: bfloat16 [128, 16384], P('dp'), may hold values from -6 to 6
- norm_gain: bfloat16 [16384], replicated, may hold values from 0.099609375 to 1.8984375
- query_weight: bfloat16 [16384, 16384], P('dp', 'tensor'), may hold values from -0.046875 to 0.046875
- keyval_weight: bfloat16 [16384, 8, 256], P('dp', 'tensor'), may hold values from -0.046875 to 0.046875
- output_weight: bfloat16 [16384, 16384], P('tensor', 'dp'), may hold values from -0.046875 to 0.046875
- kv_cache: bfloat16 [128, 8, 1024, 256], P('dp', 'tensor')
- cache_lengths: int32 [128], P('dp'), may hold values from 128 to 1024, as said below
- next_source: bfloat16 [128, 128, 16384], P(('dp', 'tensor')), may hold values from -0.046875 to 0.046875
- block_ids: int32 [128], P('dp'), may hold values from 0 to 127, as said below
Outputs:
- mixed: bfloat16 [128, 16384], P('dp')
- next_weight: bfloat16 [16384, 16384], P('dp', 'tensor')
Inputs may be any that keep to these rules, and one draw needn't show every extreme that they name: `cache_lengths`: some row uses exactly 1024 positions. `block_ids`: a permutation; the 8 entries on one dp index name at most 1 block within the rows of any one dp index, and that many for some.
All inputs are finite; a program needn't handle non-finite values.
Results may differ from a plain program's by a relative error of at most 0.04.
Values may be sent and summed in bfloat16 or wider, within the bound.
No kernel may reach another device: no remote copies, remote signals or barrier semaphores. Data moves between devices by JAX's collectives and lax.ppermute only.
A program may use at most 128 MiB of HBM per device.

v0:
```python
import jax
import jax.numpy as jnp
from jax import lax
from jax.sharding import PartitionSpec as P


def attend(queries, new_keyval, kv_cache, cache_lengths):
    rows, groups, length, twice = kv_cache.shape
    head_dim = twice // 2
    score_scale = head_dim ** (-0.5)
    query_heads = queries.reshape(rows, groups, -1, head_dim)
    scores = (
        jnp.einsum(
            "rjhd,rjpd->rjhp",
            query_heads,
            kv_cache[..., :head_dim],
            preferred_element_type=jnp.float32,
        )
        * score_scale
    )
    visible = jnp.arange(length)[None, :] < cache_lengths[:, None]
    scores = jnp.where(visible[:, None, None, :], scores, -jnp.inf)
    self_score = (
        jnp.einsum(
            "rjhd,rjd->rjh",
            query_heads,
            new_keyval[..., :head_dim],
            preferred_element_type=jnp.float32,
        )
        * score_scale
    )
    highest = jnp.maximum(jnp.max(scores, axis=-1), self_score)
    expo = jnp.exp(scores - highest[..., None])
    self_expo = jnp.exp(self_score - highest)
    denominator = jnp.sum(expo, axis=-1) + self_expo
    weights = (expo / denominator[..., None]).astype(jnp.bfloat16)
    self_weight = (self_expo / denominator).astype(jnp.bfloat16)
    summed = jnp.einsum(
        "rjhp,rjpd->rjhd", weights, kv_cache[..., head_dim:], preferred_element_type=jnp.float32
    )
    summed = summed + self_weight.astype(jnp.float32)[..., None] * new_keyval[
        :, :, None, head_dim:
    ].astype(jnp.float32)
    return summed.astype(jnp.bfloat16).reshape(rows, -1)


def relayout(next_source, block_ids):
    dp_count = lax.axis_size("dp")
    columns = lax.all_to_all(next_source, "tensor", split_axis=2, concat_axis=0, tiled=True)
    group_size = columns.shape[0]
    capacity = max(1, group_size // dp_count)
    mine_dp = lax.axis_index("dp")
    target = block_ids // group_size
    onehot = (target[:, None] == jnp.arange(dp_count, dtype=jnp.int32)[None, :]).astype(jnp.int32)
    arrival = jnp.sum((jnp.cumsum(onehot, axis=0) - onehot) * onehot, axis=1)
    slot_index = target * capacity + arrival
    select = jnp.arange(dp_count * capacity, dtype=jnp.int32)[:, None] == slot_index[None, :]
    outgoing = jnp.einsum(
        "sb,brc->src", select.astype(jnp.bfloat16), columns, preferred_element_type=jnp.float32
    ).astype(jnp.bfloat16)
    outgoing_ids = jnp.sum(jnp.where(select, block_ids[None, :] + 1, 0), axis=1) - 1
    incoming, incoming_ids = (
        lax.all_to_all(outgoing, "dp", split_axis=0, concat_axis=0, tiled=True),
        lax.all_to_all(outgoing_ids, "dp", split_axis=0, concat_axis=0, tiled=True),
    )
    position = incoming_ids - mine_dp * group_size
    place_table = (jnp.arange(group_size, dtype=jnp.int32)[:, None] == position[None, :]).astype(
        jnp.bfloat16
    )
    placed = jnp.einsum(
        "gs,src->grc", place_table, incoming, preferred_element_type=jnp.float32
    ).astype(jnp.bfloat16)
    return placed.reshape(group_size * placed.shape[1], placed.shape[2])


def on_device(
    hidden,
    norm_gain,
    query_weight,
    keyval_weight,
    output_weight,
    kv_cache,
    cache_lengths,
    next_source,
    block_ids,
):
    rows_dev = hidden.shape[0]
    stream = hidden.astype(jnp.float32)
    meansq = jnp.mean(stream * stream, axis=-1, keepdims=True)
    normed = (stream * lax.rsqrt(meansq + 1e-05) * norm_gain.astype(jnp.float32)).astype(
        jnp.bfloat16
    )
    pieces = lax.all_to_all(normed, "dp", split_axis=1, concat_axis=0, tiled=True)
    flat_kv = keyval_weight.reshape(keyval_weight.shape[0], -1)
    query_cols = query_weight.shape[1]
    projected = lax.psum_scatter(
        jnp.concatenate(
            [
                jnp.dot(pieces, query_weight, preferred_element_type=jnp.float32),
                jnp.dot(pieces, flat_kv, preferred_element_type=jnp.float32),
            ],
            axis=1,
        ).astype(jnp.bfloat16),
        "dp",
        scatter_dimension=0,
        tiled=True,
    ).astype(jnp.float32)
    queries = projected[:, :query_cols].astype(jnp.bfloat16)
    new_keyval = (
        projected[:, query_cols:]
        .astype(jnp.bfloat16)
        .reshape(rows_dev, keyval_weight.shape[1], keyval_weight.shape[2])
    )
    heads_out = attend(queries, new_keyval, kv_cache, cache_lengths)
    next_weight = relayout(next_source, block_ids)
    partial_out = jnp.dot(
        lax.all_gather(heads_out, "dp", axis=0, tiled=True),
        output_weight,
        preferred_element_type=jnp.float32,
    )
    summed = lax.psum(partial_out.astype(jnp.bfloat16), "tensor")
    attention = lax.all_to_all(summed, "dp", split_axis=0, concat_axis=1, tiled=True)
    mixed = (stream + attention.astype(jnp.float32)).astype(jnp.bfloat16)
    return (mixed, next_weight)


def solution(mesh):
    return jax.shard_map(
        on_device,
        mesh=mesh,
        in_specs=(
            P("dp", None),
            P(),
            P("dp", "tensor"),
            P("dp", "tensor", None),
            P("tensor", "dp"),
            P("dp", "tensor", None, None),
            P("dp"),
            P(("dp", "tensor"), None, None),
            P("dp"),
        ),
        out_specs=(P("dp", None), P("dp", "tensor")),
        check_vma=False,
    )
```

profile of v0, /device:TPU:3, one launch (start us, length us, event | category | flops | bytes accessed | tf_op | source)
XLA Modules:
  0.0 429.1 jit_solution(10654132601360564867)
XLA Ops:
  7.2 0.0 copy-start
  7.2 0.0 reduce-scatter.2.cloned.1.call-start
  7.2 1.2 fusion.14
  8.5 0.8 convert_element_type.67
  9.3 1.1 fusion.16
  10.3 12.0 %all_to_all.61 = bf16[8,16,1024]{2,0,1:T(8,128)(2,1)S(1)} all-to-all(bf16[8,16,1024]{2,0,1:T(8,128)(2,1)S(1)} %bitcast.82), channel_id=1, replica_groups=mesh['dp'=16,'tensor'=8] {'dp'}, dimensions={1} | all-to-all | bytes 524288 | tf_op jit(solution)/shard_map/all_to_all | solution.py:93
  22.4 0.2 convolution_convert_fusion.3
  22.6 2.9 convolution_convert_fusion.1
  25.6 0.9 pad_maximum_fusion
  26.4 0.0 reduce-scatter.2.cloned.1.call-update
  26.5 17.7 %copy.40 = bf16[1,128,16384]{1,0,2:T(2,128)(2,1)} copy(bf16[1,128,16384]{2,1,0:T(8,128)(2,1)} %param.16) | data formatting | bytes 8388608 | tf_op args[7]
  44.2 0.5 broadcast.96
  44.7 90.7 %reduce.6 = bf16[16384,128]{1,0:T(8,128)(2,1)} reduce(bf16[16384,1,128]{2,1,0:T(2,128)(2,1)} %bitcast.75, bf16[]{:T(256)} %broadcast.96), dimensions={1}, to_apply=%bitcast.67.reduce_sub_computation | reduce | bytes 8388610
  135.5 7.0 %reshape.158 = bf16[8,2,131072]{2,1,0:T(2,128)(2,1)} reshape(bf16[16384,128]{1,0:T(8,128)(2,1)} %reduce.6) | data formatting | bytes 8388608
  142.5 7.5 %all-to-all-start.3 = ((bf16[8,2,131072]{2,1,0:T(2,128)(2,1)}), bf16[8,2,131072]{2,1,0:T(2,128)(2,1)}, u32[]{:S(2)}, u32[]{:S(2)}) async-start(bf16[8,2,131072]{2,1,0:T(2,128)(2,1)} %reshape.158), calls=%async_computation.4 | async-start | bytes 8388608 | tf_op jit(solution)/shard_map/all_to_all | solution.py:49
  150.0 0.0 all-reduce.2.cloned.1.call-start
  150.0 0.1 fusion.28
  150.1 0.2 select_reduce_fusion.1
  150.3 0.1 iota_compare_fusion
  150.4 0.8 slice_bitcast_fusion.15
  151.3 0.9 slice_bitcast_fusion.14
  152.2 0.1 fusion.24
  152.3 2.3 fusion.38
  154.7 0.2 fusion.19
  154.9 2.0 fusion.13
  157.0 20.0 %all_gather.3 = bf16[128,2048]{1,0:T(8,128)(2,1)S(1)} all-gather(bf16[8,2048]{1,0:T(8,128)(2,1)S(1)} %bitcast.83), channel_id=1, replica_groups=mesh['dp'=16,'tensor'=8] {'dp'}, dimensions={0}, use_global_device_ids=true | all-gather | bytes 557056 | tf_op jit(solution)/shard_map/all_gather | solution.py:117
  177.0 1.4 fusion.10
  178.5 0.0 all-reduce.2.cloned.1.call-update
  178.5 0.1 select_reduce_fusion
  178.6 0.7 copy.39
  179.3 23.7 %all-to-all-done.3 = bf16[8,2,131072]{2,1,0:T(2,128)(2,1)} async-done(((bf16[8,2,131072]{2,1,0:T(2,128)(2,1)}), bf16[8,2,131072]{2,1,0:T(2,128)(2,1)}, u32[]{:S(2)}, u32[]{:S(2)}) %all-to-all-start.3) | async-done | bytes 4194336 | tf_op jit(solution)/shard_map/all_to_all | solution.py:49
  203.0 8.9 %all-to-all-start.2 = ((s32[16,1,1]{2,1,0:T(1,128)}), s32[16,1,1]{2,1,0:T(1,128)S(1)}, u32[]{:S(2)}, u32[]{:S(2)}) async-start(s32[16,1,1]{2,1,0:T(1,128)} %copy.39), calls=%async_computation.3 | async-start | bytes 16384 | tf_op jit(solution)/shard_map/all_to_all | solution.py:64
  211.9 8.8 %reshape.159 = bf16[16384,1,128]{2,1,0:T(2,128)(2,1)} reshape(bf16[8,2,131072]{2,1,0:T(2,128)(2,1)} %all-to-all-done.3) | data formatting | bytes 8388608
  220.7 5.9 %copy.48 = bf16[1,128,16384]{1,2,0:T(8,128)(2,1)} copy(bf16[1,128,16384]{1,0,2:T(2,128)(2,1)} %bitcast.76) | data formatting | bytes 8388608
  226.5 6.8 %copy.47 = bf16[1,128,8,2048]{3,2,1,0:T(8,128)(2,1)} copy(bf16[1,128,8,2048]{1,3,2,0:T(8,128)(2,1)} %bitcast.77) | data formatting | bytes 8388608 | tf_op jit(solution)/shard_map/all_to_all | solution.py:49
  233.3 0.0 all-to-all-done.2
  233.3 24.9 %all-reduce.2.cloned.1.call-done = bf16[16,8,1024]{2,1,0:T(8,128)(2,1)} async-done(((bf16[16,8,1024]{2,1,0:T(8,128)(2,1)}), bf16[16,8,1024]{2,1,0:T(8,128)(2,1)}) %all-reduce.2.cloned.1.call-update) | async-done | bytes 262160 | tf_op jit(solution)/shard_map/psum | solution.py:121
  258.2 10.4 %all-to-all-start.1 = ((bf16[16,8,1024]{2,1,0:T(8,128)(2,1)}), bf16[16,8,1024]{2,1,0:T(8,128)(2,1)S(1)}, u32[]{:S(2)}, u32[]{:S(2)}) async-start(bf16[16,8,1024]{2,1,0:T(8,128)(2,1)} %all-reduce.2.cloned.1.call-done), calls=%async_computation.2 | async-start | bytes 524288 | tf_op jit(solution)/shard_map/all_to_all | solution.py:122
  268.6 6.4 %convolution_convert_fusion = bf16[16,128,2048]{2,0,1:T(8,128)(2,1)} fusion(bf16[1,128,8,2048]{3,2,1,0:T(8,128)(2,1)} %copy.47, s32[8]{0:T(128)S(1)} %add.44), kind=kOutput, calls=%fused_computation.2 | convolution fusion | flops 71303296 | bytes 12582944 | tf_op jit(solution)/shard_map/sb,brc->src/dot_general | solution.py:58
  274.9 11.2 %copy.42 = bf16[16,128,2048]{2,1,0:T(8,128)(2,1)} copy(bf16[16,128,2048]{2,0,1:T(8,128)(2,1)} %convolution_convert_fusion) | data formatting | bytes 16777216 | tf_op jit(solution)/shard_map/convert_element_type | solution.py:60
  286.2 0.0 all-to-all-done.1
  286.2 5.8 %all-to-all-start.4 = ((bf16[16,128,2048]{2,1,0:T(8,128)(2,1)}), bf16[16,128,2048]{2,1,0:T(8,128)(2,1)}, u32[]{:S(2)}, u32[]{:S(2)}) async-start(bf16[16,128,2048]{2,1,0:T(8,128)(2,1)} %copy.42), calls=%async_computation.5 | async-start | bytes 16777216 | tf_op jit(solution)/shard_map/all_to_all | solution.py:63
  292.0 0.4 subtract_reduce_fusion
  292.4 0.1 convert_element_type.85
  292.5 0.8 fusion.17
  293.3 112.2 %all-to-all-done.4 = bf16[16,128,2048]{2,1,0:T(8,128)(2,1)} async-done(((bf16[16,128,2048]{2,1,0:T(8,128)(2,1)}), bf16[16,128,2048]{2,1,0:T(8,128)(2,1)}, u32[]{:S(2)}, u32[]{:S(2)}) %all-to-all-start.4) | async-done | bytes 8388640 | tf_op jit(solution)/shard_map/all_to_all | solution.py:63
  405.4 12.5 %fusion.3 = bf16[8,128,2048]{2,0,1:T(8,128)(2,1)S(1)} fusion(bf16[16,128,2048]{2,1,0:T(8,128)(2,1)} %all-to-all-done.4, s32[16]{0:T(128)S(1)} %subtract_reduce_fusion), kind=kOutput, calls=%fused_computation.4 | convolution fusion | flops 69206144 | bytes 12582976 | tf_op jit(solution)/shard_map/gs,src->grc/dot_general | solution.py:70
  418.0 4.3 %copy.44 = bf16[8,128,2048]{2,1,0:T(8,128)(2,1)} copy(bf16[8,128,2048]{2,0,1:T(8,128)(2,1)S(1)} %fusion.3) | data formatting | bytes 8388608 | tf_op jit(solution)/shard_map/convert_element_type | solution.py:72
  (21 shorter events, 0.1 us)
Async XLA Ops:
  7.2 15.2 %copy-start = (bf16[1024,1,256]{2,0,1:T(8,128)(2,1)S(1)}, bf16[1024,1,256]{2,0,1:T(8,128)(2,1)}, u32[]{:S(2)}) copy-start(bf16[1024,1,256]{2,0,1:T(8,128)(2,1)} %param.12) | copy-start | bytes 1572868
  7.2 143.2 %reduce-scatter.2.cloned.1.call-start = ((), (), s32[]{:S(2)}) async-start(), calls=%async_computation.6 | async-start | bytes 626688 | tf_op jit(solution)/shard_map/reduce_scatter | solution.py:96
  142.5 7.6 %copy-start.5 = (s32[8]{0:T(128)S(1)}, s32[8]{0:T(128)}, u32[]{:S(2)}) copy-start(s32[8]{0:T(128)} %param.17) | copy-start | bytes 100
  142.5 7.9 %copy-start.4 = (s32[8]{0:T(128)S(1)}, s32[8]{0:T(128)}, u32[]{:S(2)}) copy-start(s32[8]{0:T(128)} %param.15) | copy-start | bytes 100
  142.5 60.5 %all-to-all-start.3 = ((bf16[8,2,131072]{2,1,0:T(2,128)(2,1)}), bf16[8,2,131072]{2,1,0:T(2,128)(2,1)}, u32[]{:S(2)}, u32[]{:S(2)}) async-start(bf16[8,2,131072]{2,1,0:T(2,128)(2,1)} %reshape.158), calls=%async_computation.4 | async-start | bytes 8388608 | tf_op jit(solution)/shard_map/all_to_all | solution.py:49
  150.0 108.2 %all-reduce.2.cloned.1.call-start = ((), (), s32[]{:S(2)}) async-start(), calls=%async_computation.7 | async-start | bytes 524288 | tf_op jit(solution)/shard_map/psum | solution.py:121
  150.4 26.6 %copy-start.2 = (bf16[2048,1024]{1,0:T(8,128)(2,1)S(1)}, bf16[2048,1024]{1,0:T(8,128)(2,1)}, u32[]{:S(2)}) copy-start(bf16[2048,1024]{1,0:T(8,128)(2,1)} %param.13) | copy-start | bytes 12582916
  203.0 30.3 %all-to-all-start.2 = ((s32[16,1,1]{2,1,0:T(1,128)}), s32[16,1,1]{2,1,0:T(1,128)S(1)}, u32[]{:S(2)}, u32[]{:S(2)}) async-start(s32[16,1,1]{2,1,0:T(1,128)} %copy.39), calls=%async_computation.3 | async-start | bytes 16384 | tf_op jit(solution)/shard_map/all_to_all | solution.py:64
  258.2 28.0 %all-to-all-start.1 = ((bf16[16,8,1024]{2,1,0:T(8,128)(2,1)}), bf16[16,8,1024]{2,1,0:T(8,128)(2,1)S(1)}, u32[]{:S(2)}, u32[]{:S(2)}) async-start(bf16[16,8,1024]{2,1,0:T(8,128)(2,1)} %all-reduce.2.cloned.1.call-done), calls=%async_computation.2 | async-start | bytes 524288 | tf_op jit(solution)/shard_map/all_to_all | solution.py:122
  286.2 6.3 %copy-start.3 = (bf16[8,16384]{1,0:T(8,128)(2,1)S(1)}, bf16[8,16384]{1,0:T(8,128)(2,1)}, u32[]{:S(2)}) copy-start(bf16[8,16384]{1,0:T(8,128)(2,1)} %param.9) | copy-start | bytes 786436
  286.2 119.2 %all-to-all-start.4 = ((bf16[16,128,2048]{2,1,0:T(8,128)(2,1)}), bf16[16,128,2048]{2,1,0:T(8,128)(2,1)}, u32[]{:S(2)}, u32[]{:S(2)}) async-start(bf16[16,128,2048]{2,1,0:T(8,128)(2,1)} %copy.42), calls=%async_computation.5 | async-start | bytes 16777216 | tf_op jit(solution)/shard_map/all_to_all | solution.py:63
  405.4 16.9 %copy-start.1 = (bf16[1024,1,256]{2,0,1:T(8,128)(2,1)S(1)}, bf16[1024,1,256]{2,0,1:T(8,128)(2,1)}, u32[]{:S(2)}) copy-start(bf16[1024,1,256]{2,0,1:T(8,128)(2,1)} %param.12) | copy-start | bytes 1572868
Sparse Core Ops, SparseCore 0:
  26.6 54.4 reduce-scatter.1
  178.6 79.4 all-reduce.1
where the time goes:
time: 431 us; the launch traced here: 429 us
  waiting for transfers between devices  161 us (37%)
  other arithmetic  96.7 us (22%)
  local copies, waits for them, and re-layouts  64.7 us (15%)
  starting transfers between devices  32.8 us (8%)
  blocking collectives  32.1 us (7%)
  matrix products  28 us (6%)
  between operations  14.1 us (3%)
    all_to_all x1, waiting for transfers between devices, relayout(): lax.all_to_all(outgoing, 'dp', split_axis=0, concat_axis=0, tiled=True)  112 us
    unnamed x1, other arithmetic  90.7 us
    unnamed x18, local copies, waits for them, and re-layouts  39.9 us
    psum x1, waiting for transfers between devices, on_device(): summed = lax.psum(partial_out.astype(jnp.bfloat16), 'tensor')  24.9 us
    all_to_all x1, waiting for transfers between devices, relayout(): lax.all_to_all(next_source, 'tensor', split_axis=2, concat_axis=0, tiled=...  23.7 us
    all_gather x1, blocking collectives, on_device(): lax.all_gather(heads_out, 'dp', axis=0, tiled=True)  20 us
    dot_general x1, matrix products, relayout(): jnp.einsum('gs,src->grc', place_table, incoming, preferred_element_type=j...  12.5 us
    all_to_all x1, blocking collectives, on_device(): lax.all_to_all(normed, 'dp', split_axis=1, concat_axis=0, tiled=True)  12 us
  transfers between devices with their start and end apart: 6, of which 3 were waited for; matrix products, arithmetic and copies ran while one was open for 39% of the time, Pallas kernels for 0%

commit v1 on v0

v1 whole, which is shorter than its diff:
```python
import functools

import jax
import jax.numpy as jnp
from jax import lax
from jax.experimental import pallas as pl
from jax.experimental.pallas import tpu as pltpu
from jax.sharding import PartitionSpec as P

ANY = pl.BlockSpec(memory_space=pl.ANY)


def scatter_kernel(ids_ref, src_ref, dst_ref, sem):
    count = src_ref.shape[0]

    @pl.loop(0, count)
    def _(b):
        pltpu.make_async_copy(src_ref.at[b], dst_ref.at[ids_ref[b]], sem).start()

    pltpu.make_async_copy(src_ref, dst_ref, sem).wait()


def scatter_slabs(ids, slabs):
    return pl.pallas_call(
        scatter_kernel,
        out_shape=jax.ShapeDtypeStruct(slabs.shape, slabs.dtype),
        in_specs=[pl.BlockSpec(memory_space=pltpu.SMEM), ANY],
        out_specs=ANY,
        scratch_shapes=[pltpu.SemaphoreType.DMA],
        cost_estimate=pl.CostEstimate(
            flops=0, bytes_accessed=2 * slabs.size * 2, transcendentals=0
        ),
        name="scatter_slabs",
    )(ids, slabs)


def swap_kernel(src_ref, dst_ref, sem):
    for m in range(src_ref.shape[0]):
        pltpu.make_async_copy(src_ref.at[m], dst_ref.at[:, m], sem).start()
    pltpu.make_async_copy(src_ref, src_ref, sem).wait()


def swap_leading(src):
    m, g, r, c = src.shape
    return pl.pallas_call(
        swap_kernel,
        out_shape=jax.ShapeDtypeStruct((g, m, r, c), src.dtype),
        in_specs=[ANY],
        out_specs=ANY,
        scratch_shapes=[pltpu.SemaphoreType.DMA],
        cost_estimate=pl.CostEstimate(flops=0, bytes_accessed=2 * src.size * 2, transcendentals=0),
        name="swap_leading",
    )(src)


def tile_kernel(src_ref, dst_ref, sem):
    tiles, width = dst_ref.shape[1], dst_ref.shape[3]
    for t in range(tiles):
        pltpu.make_async_copy(
            src_ref.at[:, :, pl.ds(t * width, width)], dst_ref.at[:, t], sem
        ).start()
    pltpu.make_async_copy(dst_ref, dst_ref, sem).wait()


def cut_tiles(src, tiles):
    m, r, c = src.shape
    return pl.pallas_call(
        tile_kernel,
        out_shape=jax.ShapeDtypeStruct((m, tiles, r, c // tiles), src.dtype),
        in_specs=[ANY],
        out_specs=ANY,
        scratch_shapes=[pltpu.SemaphoreType.DMA],
        cost_estimate=pl.CostEstimate(flops=0, bytes_accessed=2 * src.size * 2, transcendentals=0),
        name="cut_tiles",
    )(src)


def attend(queries, new_keyval, kv_cache, cache_lengths):
    rows, groups, length, twice = kv_cache.shape
    head_dim = twice // 2
    score_scale = head_dim ** (-0.5)
    query_heads = queries.reshape(rows, groups, -1, head_dim)
    scores = (
        jnp.einsum(
            "rjhd,rjpd->rjhp",
            query_heads,
            kv_cache[..., :head_dim],
            preferred_element_type=jnp.float32,
        )
        * score_scale
    )
    visible = jnp.arange(length)[None, :] < cache_lengths[:, None]
    scores = jnp.where(visible[:, None, None, :], scores, -jnp.inf)
    self_score = (
        jnp.einsum(
            "rjhd,rjd->rjh",
            query_heads,
            new_keyval[..., :head_dim],
            preferred_element_type=jnp.float32,
        )
        * score_scale
    )
    highest = jnp.maximum(jnp.max(scores, axis=-1), self_score)
    expo = jnp.exp(scores - highest[..., None])
    self_expo = jnp.exp(self_score - highest)
    denominator = jnp.sum(expo, axis=-1) + self_expo
    weights = (expo / denominator[..., None]).astype(jnp.bfloat16)
    self_weight = (self_expo / denominator).astype(jnp.bfloat16)
    summed = jnp.einsum(
        "rjhp,rjpd->rjhd", weights, kv_cache[..., head_dim:], preferred_element_type=jnp.float32
    )
    summed = summed + self_weight.astype(jnp.float32)[..., None] * new_keyval[
        :, :, None, head_dim:
    ].astype(jnp.float32)
    return summed.astype(jnp.bfloat16).reshape(rows, -1)


def exchange(x, axes):
    return lax.all_to_all(x, axes, split_axis=0, concat_axis=0, tiled=True)


def on_device(
    hidden,
    norm_gain,
    query_weight,
    keyval_weight,
    output_weight,
    kv_cache,
    cache_lengths,
    next_source,
    block_ids,
):
    barrier = lax.optimization_barrier
    dp, tensor = lax.axis_size("dp"), lax.axis_size("tensor")
    rows, width = hidden.shape
    depth = width // dp
    group = block_ids.shape[0]
    query_cols = query_weight.shape[1]

    stream = hidden.astype(jnp.float32)
    meansq = jnp.mean(stream * stream, axis=-1, keepdims=True)
    normed = (stream * lax.rsqrt(meansq + 1e-05) * norm_gain.astype(jnp.float32)).astype(
        jnp.bfloat16
    )
    lanes = jnp.broadcast_to(block_ids.astype(jnp.bfloat16)[None, :, None], (dp, group, 128))
    outbound = jnp.concatenate(
        [normed.reshape(rows, dp, depth).transpose(1, 0, 2), lanes], axis=2
    )
    arrived = exchange(outbound, "dp")
    pieces = arrived[:, :, :depth].reshape(dp * rows, depth)
    ids = arrived[:, :, depth].reshape(dp * group).astype(jnp.int32)

    block_rows = next_source.shape[1]
    piece_rows = block_rows // dp
    slabs = cut_tiles(next_source.reshape(dp, piece_rows, -1), tensor)
    tile_cols = slabs.shape[3]
    slabs = slabs.reshape(dp * tensor, piece_rows, tile_cols)
    slabs, pieces, ids = barrier((slabs, pieces, ids))
    spread = exchange(slabs, ("dp", "tensor"))

    flat_kv = keyval_weight.reshape(keyval_weight.shape[0], -1)
    partial = jnp.concatenate(
        [
            jnp.dot(pieces, query_weight, preferred_element_type=jnp.float32).astype(jnp.bfloat16),
            jnp.dot(pieces, flat_kv, preferred_element_type=jnp.float32).astype(jnp.bfloat16),
        ],
        axis=1,
    )
    partial, spread = barrier((partial, spread))
    terms = exchange(partial.reshape(dp, rows, -1), "dp")
    projected = jnp.sum(terms.astype(jnp.float32), axis=0).astype(jnp.bfloat16)

    sorted_slabs = scatter_slabs(ids, spread)
    sorted_slabs, projected = barrier((sorted_slabs, projected))
    incoming = exchange(sorted_slabs, "dp")

    queries = projected[:, :query_cols]
    new_keyval = projected[:, query_cols:].reshape(
        rows, keyval_weight.shape[1], keyval_weight.shape[2]
    )
    heads_out = attend(queries, new_keyval, kv_cache, cache_lengths)
    heads_out, incoming = barrier((heads_out, incoming))

    placed = swap_leading(incoming.reshape(dp, group, piece_rows, tile_cols))
    next_weight = placed.reshape(group * block_rows, tile_cols)

    all_heads = exchange(jnp.broadcast_to(heads_out[None], (dp,) + heads_out.shape), "dp")
    partial_out = jnp.dot(
        all_heads.reshape(dp * rows, -1), output_weight, preferred_element_type=jnp.float32
    ).astype(jnp.bfloat16)
    chunk = partial_out.shape[1] // tensor
    outbound = partial_out.reshape(dp, rows, tensor, chunk).transpose(0, 2, 1, 3)
    terms = exchange(outbound.reshape(dp * tensor, rows, chunk), ("dp", "tensor"))
    summed = jnp.sum(
        terms.reshape(dp, tensor, rows, chunk).astype(jnp.float32), axis=1
    ).astype(jnp.bfloat16)
    chunks = exchange(jnp.broadcast_to(summed[None], (tensor,) + summed.shape), "tensor")
    attention = (
        chunks.reshape(tensor, dp, rows, chunk).transpose(2, 1, 0, 3).reshape(rows, width)
    )
    mixed = (stream + attention.astype(jnp.float32)).astype(jnp.bfloat16)
    return (mixed, next_weight)


def solution(mesh):
    return jax.shard_map(
        on_device,
        mesh=mesh,
        in_specs=(
            P("dp", None),
            P(),
            P("dp", "tensor"),
            P("dp", "tensor", None),
            P("tensor", "dp"),
            P("dp", "tensor", None, None),
            P("dp"),
            P(("dp", "tensor"), None, None),
            P("dp"),
        ),
        out_specs=(P("dp", None), P("dp", "tensor")),
        check_vma=False,
    )
```

time: 431 us -> 567 us (1.32)
  Pallas kernels: 0 us -> 385 us
  other arithmetic: 96.7 us -> 7.21 us
  local copies, waits for them, and re-layouts: 64.7 us -> 1.83 us
  waiting for transfers between devices: 161 us -> 99.3 us
  matrix products: 28 us -> 10.6 us
  between operations: 14.1 us -> 0.84 us
    pallas_call x0 -> x3, Pallas kernels: none -> 385 us  [the longest x1 129 us: scatter_slabs(): pl.pallas_call(scatter_kernel, out_shape=jax.ShapeDtypeStruct(slabs.shape...]
    unnamed x1 -> x0, other arithmetic: 90.7 us -> none
    unnamed x18 -> x8, local copies, waits for them, and re-layouts: 39.9 us -> 0.04 us
    all_to_all x4 -> x5, waiting for transfers between devices: 136 us -> 99.3 us  [exchange(): return lax.all_to_all(x, axes, split_axis=0, concat_axis=0, tiled=True)]
    psum x1 -> x0, waiting for transfers between devices: 24.9 us -> none  [on_device(): summed = lax.psum(partial_out.astype(jnp.bfloat16), 'tensor')]
    all_gather x1 -> x0, blocking collectives: 20 us -> none  [on_device(): lax.all_gather(heads_out, 'dp', axis=0, tiled=True)]
    dot_general x3 -> x1, matrix products: 20.3 us -> 2.95 us  [on_device(): jnp.dot(all_heads.reshape(dp * rows, -1), output_weight, preferred_elemen...]
    all_to_all x1 -> x2, blocking collectives: 12 us -> 28.4 us  [exchange(): return lax.all_to_all(x, axes, split_axis=0, concat_axis=0, tiled=True)]
  transfers between devices with their start and end apart: 6 -> 5, of which waited for: 3 -> 2; matrix products, arithmetic and copies ran while one was open for 39% -> 2% of each run, Pallas kernels for 0% -> 68%
where the time goes in v1:
time: 567 us; the launch traced here: 564 us
  Pallas kernels  385 us (68%)
  waiting for transfers between devices  99.3 us (18%)
  starting transfers between devices  30.5 us (5%)
  blocking collectives  28.4 us (5%)
  matrix products  10.6 us (2%)
  other arithmetic  7.21 us (1%)
    pallas_call x1, Pallas kernels, scatter_slabs(): pl.pallas_call(scatter_kernel, out_shape=jax.ShapeDtypeStruct(slabs.shape...  129 us
    pallas_call x1, Pallas kernels, swap_leading(): pl.pallas_call(swap_kernel, out_shape=jax.ShapeDtypeStruct((g, m, r, c),...  128 us
    pallas_call x1, Pallas kernels, cut_tiles(): pl.pallas_call(tile_kernel, out_shape=jax.ShapeDtypeStruct((m, tiles, r,...  128 us
    all_to_all x5, waiting for transfers between devices, exchange(): return lax.all_to_all(x, axes, split_axis=0, concat_axis=0, tiled=True)  99.3 us
    all_to_all x5, starting transfers between devices, exchange(): return lax.all_to_all(x, axes, split_axis=0, concat_axis=0, tiled=True)  30.5 us
    all_to_all x2, blocking collectives, exchange(): return lax.all_to_all(x, axes, split_axis=0, concat_axis=0, tiled=True)  28.4 us
  transfers between devices with their start and end apart: 5, of which 2 were waited for; matrix products, arithmetic and copies ran while one was open for 2% of the time, Pallas kernels for 68%

profile of v1, /device:TPU:3, one launch (start us, length us, event | category | flops | bytes accessed | tf_op | source)
XLA Modules:
  0.0 563.9 jit_solution(9100576357450208734)
XLA Ops:
  0.6 0.0 copy-start
  0.6 0.7 convert_element_type.73
  1.4 1.2 fusion.7
  2.6 0.8 convert_element_type.71
  3.3 1.1 fusion.9
  4.4 0.1 broadcast_in_dim.19
  4.5 0.7 pad_maximum_fusion.1
  5.2 6.2 %all-to-all-start = ((bf16[16,8,1152]{2,1,0:T(8,128)(2,1)}), bf16[16,8,1152]{2,1,0:T(8,128)(2,1)S(1)}, u32[]{:S(2)}, u32[]{:S(2)}) async-start(bf16[16,8,1152]{2,1,0:T(8,128)(2,1)} %pad_maximum_fusion.1), calls=%async_computation | async-start | bytes 589824 | tf_op jit(solution)/shard_map/all_to_all | solution.py:119
  11.4 128.2 %cut_tiles.1 = bf16[16,8,8,2048]{3,2,1,0:T(8,128)(2,1)} custom-call(bf16[16,8,16384]{2,1,0:T(8,128)(2,1)} %bitcast.82), custom_call_target="tpu_custom_call" | custom-call | bytes 8388608 | tf_op jit(solution)/shard_map/cut_tiles/pallas_call | solution.py:67
  139.6 0.0 all-to-all-done
  139.6 0.3 convert_reduce_fusion
  139.9 0.6 reshape.168.ids_ref
  140.6 10.7 %all-to-all-start.1 = ((bf16[128,8,2048]{2,1,0:T(8,128)(2,1)}), bf16[128,8,2048]{2,1,0:T(8,128)(2,1)}, u32[]{:S(2)}, u32[]{:S(2)}) async-start(bf16[128,8,2048]{2,1,0:T(8,128)(2,1)} %bitcast.81), calls=%async_computation.1 | async-start | bytes 8388608 | tf_op jit(solution)/shard_map/all_to_all | solution.py:119
  151.2 0.0 copy-done
  151.3 0.2 convolution_convert_fusion.2
  151.5 2.9 convolution_convert_fusion
  154.4 0.9 pad_maximum_fusion
  155.3 47.5 %all-to-all-done.1.src_ref = bf16[128,8,2048]{2,1,0:T(8,128)(2,1)} async-done(((bf16[128,8,2048]{2,1,0:T(8,128)(2,1)}), bf16[128,8,2048]{2,1,0:T(8,128)(2,1)}, u32[]{:S(2)}, u32[]{:S(2)}) %all-to-all-start.1) | async-done | bytes 4194336 | tf_op jit(solution)/shard_map/all_to_all | solution.py:119
  202.8 4.5 all-to-all-start.2
  207.3 128.8 %scatter_slabs.1 = bf16[128,8,2048]{2,1,0:T(8,128)(2,1)} custom-call(s32[128]{0:T(128)} %reshape.168.ids_ref, bf16[128,8,2048]{2,1,0:T(8,128)(2,1)} %all-to-all-done.1.src_ref), custom_call_target="tpu_custom_call" | custom-call | bytes 8388608 | tf_op jit(solution)/shard_map/scatter_slabs/pallas_call | solution.py:24
  336.1 0.0 all-to-all-done.2
  336.2 0.1 reduce_sum.43
  336.2 0.0 copy-start.2
  336.3 5.7 %all-to-all-start.3 = ((bf16[128,8,2048]{2,1,0:T(8,128)(2,1)}), bf16[128,8,2048]{2,1,0:T(8,128)(2,1)}, u32[]{:S(2)}, u32[]{:S(2)}) async-start(bf16[128,8,2048]{2,1,0:T(8,128)(2,1)} %scatter_slabs.1), calls=%async_computation.3 | async-start | bytes 8388608 | tf_op jit(solution)/shard_map/all_to_all | solution.py:119
  342.0 0.0 copy-done.2
  342.0 0.1 iota_compare_fusion
  342.1 0.1 fusion.16
  342.2 2.3 fusion.25
  344.6 0.2 fusion.13
  344.8 2.1 fusion.6
  346.9 51.8 %all-to-all-done.3 = bf16[128,8,2048]{2,1,0:T(8,128)(2,1)} async-done(((bf16[128,8,2048]{2,1,0:T(8,128)(2,1)}), bf16[128,8,2048]{2,1,0:T(8,128)(2,1)}, u32[]{:S(2)}, u32[]{:S(2)}) %all-to-all-start.3) | async-done | bytes 4194336 | tf_op jit(solution)/shard_map/all_to_all | solution.py:119
  398.8 12.3 %all_to_all.35 = bf16[16,8,2048]{2,1,0:T(8,128)(2,1)S(1)} all-to-all(bf16[16,8,2048]{2,1,0:T(8,128)(2,1)S(1)} %broadcast_in_dim.21), channel_id=1, replica_groups=mesh['dp'=16,'tensor'=8] {'dp'}, dimensions={0} | all-to-all | bytes 1048576 | tf_op jit(solution)/shard_map/all_to_all | solution.py:119
  411.1 2.9 convolution_convert_fusion.1
  414.0 16.1 %all_to_all.36 = bf16[128,8,128]{2,1,0:T(8,128)(2,1)S(1)} all-to-all(bf16[128,8,128]{2,1,0:T(8,128)(2,1)S(1)} %bitcast.85), channel_id=1, replica_groups=mesh['dp'=16,'tensor'=8] {'dp','tensor'}, dimensions={0} | all-to-all | bytes 524288 | tf_op jit(solution)/shard_map/all_to_all | solution.py:119
  430.2 0.7 broadcast_in_dim.22
  430.9 3.4 all-to-all-start.6
  434.4 0.0 copy-start.1
  434.4 128.2 %swap_leading.1 = bf16[8,16,8,2048]{3,2,1,0:T(8,128)(2,1)} custom-call(bf16[16,8,8,2048]{3,2,1,0:T(8,128)(2,1)} %bitcast.23.src_ref), custom_call_target="tpu_custom_call" | custom-call | bytes 8388608 | tf_op jit(solution)/shard_map/swap_leading/pallas_call | solution.py:45
  562.6 0.0 all-to-all-done.6
  562.6 0.3 copy.41
  562.9 0.0 copy-done.1
  562.9 1.0 fusion.10
  (11 shorter events, 0.2 us)
Async XLA Ops:
  0.6 150.6 %copy-start = (bf16[1024,1,256]{2,0,1:T(8,128)(2,1)S(1)}, bf16[1024,1,256]{2,0,1:T(8,128)(2,1)}, u32[]{:S(2)}) copy-start(bf16[1024,1,256]{2,0,1:T(8,128)(2,1)} %param.12) | copy-start | bytes 1572868
  5.2 134.3 %all-to-all-start = ((bf16[16,8,1152]{2,1,0:T(8,128)(2,1)}), bf16[16,8,1152]{2,1,0:T(8,128)(2,1)S(1)}, u32[]{:S(2)}, u32[]{:S(2)}) async-start(bf16[16,8,1152]{2,1,0:T(8,128)(2,1)} %pad_maximum_fusion.1), calls=%async_computation | async-start | bytes 589824 | tf_op jit(solution)/shard_map/all_to_all | solution.py:119
  140.6 62.2 %all-to-all-start.1 = ((bf16[128,8,2048]{2,1,0:T(8,128)(2,1)}), bf16[128,8,2048]{2,1,0:T(8,128)(2,1)}, u32[]{:S(2)}, u32[]{:S(2)}) async-start(bf16[128,8,2048]{2,1,0:T(8,128)(2,1)} %bitcast.81), calls=%async_computation.1 | async-start | bytes 8388608 | tf_op jit(solution)/shard_map/all_to_all | solution.py:119
  202.8 133.4 %all-to-all-start.2 = ((bf16[16,8,2304]{2,1,0:T(8,128)(2,1)}), bf16[16,8,2304]{2,1,0:T(8,128)(2,1)S(1)}, u32[]{:S(2)}, u32[]{:S(2)}) async-start(bf16[16,8,2304]{2,1,0:T(8,128)(2,1)} %bitcast.6), calls=%async_computation.2 | async-start | bytes 1179648 | tf_op jit(solution)/shard_map/all_to_all | solution.py:119
  336.2 5.7 %copy-start.2 = (s32[8]{0:T(128)S(1)}, s32[8]{0:T(128)}, u32[]{:S(2)}) copy-start(s32[8]{0:T(128)} %param.15) | copy-start | bytes 100
  336.3 62.5 %all-to-all-start.3 = ((bf16[128,8,2048]{2,1,0:T(8,128)(2,1)}), bf16[128,8,2048]{2,1,0:T(8,128)(2,1)}, u32[]{:S(2)}, u32[]{:S(2)}) async-start(bf16[128,8,2048]{2,1,0:T(8,128)(2,1)} %scatter_slabs.1), calls=%async_computation.3 | async-start | bytes 8388608 | tf_op jit(solution)/shard_map/all_to_all | solution.py:119
  430.9 131.6 %all-to-all-start.6 = ((bf16[8,16,8,128]{3,2,1,0:T(8,128)(2,1)}), bf16[8,16,8,128]{3,2,1,0:T(8,128)(2,1)S(1)}, u32[]{:S(2)}, u32[]{:S(2)}) async-start(bf16[8,16,8,128]{3,2,1,0:T(8,128)(2,1)} %broadcast_in_dim.22), calls=%async_computation.6 | async-start | bytes 524288 | tf_op jit(solution)/shard_map/all_to_all | solution.py:119
  434.4 128.6 %copy-start.1 = (bf16[8,16384]{1,0:T(8,128)(2,1)S(1)}, bf16[8,16384]{1,0:T(8,128)(2,1)}, u32[]{:S(2)}) copy-start(bf16[8,16384]{1,0:T(8,128)(2,1)} %param.9) | copy-start | bytes 786436

commit v2 on v1

v2 whole, which is shorter than its diff:
```python
import jax
import jax.numpy as jnp
from jax import lax
from jax.experimental import pallas as pl
from jax.experimental.pallas import tpu as pltpu
from jax.sharding import PartitionSpec as P

ANY = pl.BlockSpec(memory_space=pl.ANY)
VMEM = pl.BlockSpec(memory_space=pltpu.VMEM)


def pick_kernel(table_ref, src_ref, *out_refs):
    group = out_refs[0].shape[0]
    for j, out_ref in enumerate(out_refs):

        @pl.loop(0, group)
        def _(g):
            out_ref[g] = src_ref[table_ref[j * group + g]]


def pick_slabs(table, slabs, parts):
    group = table.shape[0] // parts
    part = jax.ShapeDtypeStruct((group,) + slabs.shape[1:], slabs.dtype)
    return pl.pallas_call(
        pick_kernel,
        out_shape=[part] * parts,
        in_specs=[pl.BlockSpec(memory_space=pltpu.SMEM), VMEM],
        out_specs=[VMEM] * parts,
        compiler_params=pltpu.CompilerParams(vmem_limit_bytes=32 << 20),
        cost_estimate=pl.CostEstimate(
            flops=0, bytes_accessed=2 * slabs.size * 2, transcendentals=0
        ),
        name="pick_slabs",
    )(table, slabs)


def place_kernel(owner_ref, *refs):
    *refs, dst_ref, sem = refs
    part_refs = [ref for ref in refs if ref.shape != dst_ref.shape]
    copies = [
        pltpu.make_async_copy(part_ref, dst_ref.at[:, owner_ref[j]], sem.at[j])
        for j, part_ref in enumerate(part_refs)
    ]
    for copy in copies:
        copy.start()
    for copy in copies:
        copy.wait()


def place_parts(owners, parts, count, into=None):
    group, r, c = parts[0].shape
    held = [] if into is None else [into]
    return pl.pallas_call(
        place_kernel,
        out_shape=jax.ShapeDtypeStruct((group, count, r, c), parts[0].dtype),
        in_specs=[pl.BlockSpec(memory_space=pltpu.SMEM)] + [VMEM] * len(parts) + [ANY] * len(held),
        out_specs=ANY,
        input_output_aliases={1 + len(parts): 0} if held else {},
        scratch_shapes=[pltpu.SemaphoreType.DMA((len(parts),))],
        compiler_params=pltpu.CompilerParams(vmem_limit_bytes=16 << 20),
        cost_estimate=pl.CostEstimate(
            flops=0, bytes_accessed=4 * len(parts) * parts[0].size, transcendentals=0
        ),
        name="place_parts",
    )(owners, *parts, *held)


ROUNDS = (
    ((0, 1, 0), (1, 3, 1), (1, 2, 0), (0, 0, 1)),
    ((0, 1, 1), (1, 3, 0), (0, 2, 1), (1, 0, 0)),
    ((1, 1, 0), (0, 3, 1), (0, 2, 0), (1, 0, 1)),
    ((1, 1, 1), (0, 3, 0), (1, 2, 1)),
)
STEPS = ((0, 0, 0),) + tuple(step for steps in ROUNDS for step in steps)


def shifted(index, step, sign):
    y_lo, x, core = index // 8, index // 2 % 4, index % 2
    return ((y_lo + step[0]) % 2 * 4 + (x + sign * step[1]) % 4) * 2 + (core + step[2]) % 2


def send(part, step):
    return lax.ppermute(part, "dp", [(s, shifted(s, step, 1)) for s in range(16)])


def attend(queries, new_keyval, kv_cache, cache_lengths):
    rows, groups, length, twice = kv_cache.shape
    head_dim = twice // 2
    score_scale = head_dim ** (-0.5)
    query_heads = queries.reshape(rows, groups, -1, head_dim)
    scores = (
        jnp.einsum(
            "rjhd,rjpd->rjhp",
            query_heads,
            kv_cache[..., :head_dim],
            preferred_element_type=jnp.float32,
        )
        * score_scale
    )
    visible = jnp.arange(length)[None, :] < cache_lengths[:, None]
    scores = jnp.where(visible[:, None, None, :], scores, -jnp.inf)
    self_score = (
        jnp.einsum(
            "rjhd,rjd->rjh",
            query_heads,
            new_keyval[..., :head_dim],
            preferred_element_type=jnp.float32,
        )
        * score_scale
    )
    highest = jnp.maximum(jnp.max(scores, axis=-1), self_score)
    expo = jnp.exp(scores - highest[..., None])
    self_expo = jnp.exp(self_score - highest)
    denominator = jnp.sum(expo, axis=-1) + self_expo
    weights = (expo / denominator[..., None]).astype(jnp.bfloat16)
    self_weight = (self_expo / denominator).astype(jnp.bfloat16)
    summed = jnp.einsum(
        "rjhp,rjpd->rjhd", weights, kv_cache[..., head_dim:], preferred_element_type=jnp.float32
    )
    summed = summed + self_weight.astype(jnp.float32)[..., None] * new_keyval[
        :, :, None, head_dim:
    ].astype(jnp.float32)
    return summed.astype(jnp.bfloat16).reshape(rows, -1)


def exchange(x, axes):
    return lax.all_to_all(x, axes, split_axis=0, concat_axis=0, tiled=True)


def on_device(
    hidden,
    norm_gain,
    query_weight,
    keyval_weight,
    output_weight,
    kv_cache,
    cache_lengths,
    next_source,
    block_ids,
):
    barrier = lax.optimization_barrier
    dp, tensor = lax.axis_size("dp"), lax.axis_size("tensor")
    rows, width = hidden.shape
    depth = width // dp
    group = block_ids.shape[0]
    query_cols = query_weight.shape[1]

    mine = lax.axis_index("dp")
    lanes = jnp.broadcast_to(block_ids.astype(jnp.bfloat16)[None, :, None], (dp, group, 128))
    outbound = jnp.concatenate(
        [hidden.reshape(rows, dp, depth).transpose(1, 0, 2), lanes], axis=2
    )
    arrived = exchange(outbound, "dp")

    block_rows = next_source.shape[1]
    piece_rows = block_rows // dp
    tile_cols = next_source.shape[2] // tensor
    slabs = next_source.reshape(dp, piece_rows, tensor, tile_cols).transpose(0, 2, 1, 3)
    slabs, arrived = barrier((slabs.reshape(dp * tensor, piece_rows, tile_cols), arrived))
    spread = exchange(slabs, ("dp", "tensor"))

    stream = hidden.astype(jnp.float32)
    meansq = jnp.mean(stream * stream, axis=-1, keepdims=True)
    row_scale = lax.rsqrt(meansq + 1e-05)

    gain = lax.dynamic_slice(norm_gain, (mine * depth,), (depth,))
    pieces = (
        arrived[:, :, :depth].reshape(dp * rows, depth).astype(jnp.float32)
        * gain.astype(jnp.float32)
    ).astype(jnp.bfloat16)
    flat_kv = keyval_weight.reshape(keyval_weight.shape[0], -1)
    partial = jnp.concatenate(
        [
            jnp.dot(pieces, query_weight, preferred_element_type=jnp.float32).astype(jnp.bfloat16),
            jnp.dot(pieces, flat_kv, preferred_element_type=jnp.float32).astype(jnp.bfloat16),
        ],
        axis=1,
    )

    ids = arrived[:, :, depth].reshape(dp * group).astype(jnp.int32)
    targets = jnp.stack([shifted(mine, step, 1) for step in STEPS])
    wanted = (targets[:, None] * group + jnp.arange(group, dtype=jnp.int32)[None, :]).reshape(-1)
    table = jnp.sum(
        jnp.where(
            ids[None, :] == wanted[:, None],
            jnp.arange(dp * group, dtype=jnp.int32)[None, :],
            0,
        ),
        axis=1,
    )
    owners = jnp.stack([shifted(mine, step, -1) for step in STEPS])
    partial, row_scale, table, spread = barrier((partial, row_scale, table, spread))
    terms = exchange(partial.reshape(dp, rows, -1), "dp")
    bounds = [0, 1 + len(ROUNDS[0])]
    for steps in ROUNDS[1:]:
        bounds.append(bounds[-1] + len(steps))
    picked = [
        pick_slabs(table[first * group : last * group], spread, last - first)
        for first, last in zip(bounds[:-1], bounds[1:])
    ]

    def start_round(number, anchor):
        anchor, *ready = barrier((anchor, *picked[number]))
        return anchor, [send(part, step) for part, step in zip(ready, ROUNDS[number])]

    kept, *ready = picked[0]
    landed = [[kept] + [send(part, step) for part, step in zip(ready, ROUNDS[0])]]
    projected = (jnp.sum(terms.astype(jnp.float32), axis=0) * row_scale).astype(jnp.bfloat16)
    queries = projected[:, :query_cols]
    new_keyval = projected[:, query_cols:].reshape(
        rows, keyval_weight.shape[1], keyval_weight.shape[2]
    )
    heads_out = attend(queries, new_keyval, kv_cache, cache_lengths)

    heads_out, results = start_round(1, heads_out)
    landed.append(results)
    all_heads = exchange(jnp.broadcast_to(heads_out[None], (dp,) + heads_out.shape), "dp")
    partial_out = jnp.dot(
        all_heads.reshape(dp * rows, -1), output_weight, preferred_element_type=jnp.float32
    ).astype(jnp.bfloat16)
    chunk = partial_out.shape[1] // tensor
    outbound = partial_out.reshape(dp, rows, tensor, chunk).transpose(0, 2, 1, 3)
    outbound = outbound.reshape(dp * tensor, rows, chunk)

    outbound, results = start_round(2, outbound)
    landed.append(results)
    terms = exchange(outbound, ("dp", "tensor"))
    summed = jnp.sum(
        terms.reshape(dp, tensor, rows, chunk).astype(jnp.float32), axis=1
    ).astype(jnp.bfloat16)

    first_rows = [owners[first:last] for first, last in zip(bounds[:-1], bounds[1:])]
    placed = place_parts(first_rows[0], landed[0], dp)
    placed = place_parts(first_rows[1], landed[1], dp, placed)
    summed, placed = barrier((summed, placed))
    summed, results = start_round(3, summed)
    landed.append(results)
    chunks = exchange(jnp.broadcast_to(summed[None], (tensor,) + summed.shape), "tensor")
    attention = (
        chunks.reshape(tensor, dp, rows, chunk).transpose(2, 1, 0, 3).reshape(rows, width)
    )
    mixed = (stream + attention.astype(jnp.float32)).astype(jnp.bfloat16)

    placed = place_parts(first_rows[2], landed[2], dp, placed)
    placed = place_parts(first_rows[3], landed[3], dp, placed)
    next_weight = placed.reshape(group * block_rows, tile_cols)
    return (mixed, next_weight)


def solution(mesh):
    return jax.shard_map(
        on_device,
        mesh=mesh,
        in_specs=(
            P("dp", None),
            P(),
            P("dp", "tensor"),
            P("dp", "tensor", None),
            P("tensor", "dp"),
            P("dp", "tensor", None, None),
            P("dp"),
            P(("dp", "tensor"), None, None),
            P("dp"),
        ),
        out_specs=(P("dp", None), P("dp", "tensor")),
        check_vma=False,
    )
```

time: 567 us -> 179 us (0.32)
  the two profiles are of different devices: /device:TPU:3 before, /device:TPU:4 now
where the time goes in v2:
time: 179 us; the launch traced here: 178 us
  waiting for transfers between devices  68.2 us (38%)
  starting transfers between devices  58.5 us (33%)
  Pallas kernels  18.4 us (10%)
  matrix products  11.4 us (6%)
  blocking collectives  10.8 us (6%)
  other arithmetic  6.82 us (4%)
  local copies, waits for them, and re-layouts  2.53 us (1%)
    all_to_all x5, waiting for transfers between devices, exchange(): return lax.all_to_all(x, axes, split_axis=0, concat_axis=0, tiled=True)  62.6 us
    all_to_all x5, starting transfers between devices, exchange(): return lax.all_to_all(x, axes, split_axis=0, concat_axis=0, tiled=True)  38.6 us
    ppermute x15, starting transfers between devices, send(): lax.ppermute(part, 'dp', [(s, shifted(s, step, 1)) for s in range(16)])  19.9 us
    pallas_call x4, Pallas kernels, pick_slabs(): pl.pallas_call(pick_kernel, out_shape=[part] * parts, in_specs=[pl.BlockS...  12.2 us
    all_to_all x1, blocking collectives, exchange(): return lax.all_to_all(x, axes, split_axis=0, concat_axis=0, tiled=True)  10.8 us
    pallas_call x4, Pallas kernels, place_parts(): pl.pallas_call(place_kernel, out_shape=jax.ShapeDtypeStruct((group, count...  6.17 us
    ppermute x15, waiting for transfers between devices, send(): lax.ppermute(part, 'dp', [(s, shifted(s, step, 1)) for s in range(16)])  5.64 us
    dot_general x1, matrix products, on_device(): jnp.dot(all_heads.reshape(dp * rows, -1), output_weight, preferred_elemen...  3.78 us
  transfers between devices with their start and end apart: 20, of which 5 were waited for; matrix products, arithmetic and copies ran while one was open for 7% of the time, Pallas kernels for 10%

profile of v2, /device:TPU:4, one launch (start us, length us, event | category | flops | bytes accessed | tf_op | source)
XLA Modules:
  0.0 177.9 jit_solution(17108005565151942032)
XLA Ops:
  0.6 0.7 convert_element_type.93
  1.4 1.0 pad_maximum_fusion.1
  2.4 10.8 %all_to_all.30 = bf16[16,8,1152]{2,1,0:T(8,128)(2,1)S(1)} all-to-all(bf16[16,8,1152]{2,1,0:T(8,128)(2,1)S(1)} %pad_maximum_fusion.1), channel_id=1, replica_groups=mesh['dp'=16,'tensor'=8] {'dp'}, dimensions={0} | all-to-all | bytes 589824 | tf_op jit(solution)/shard_map/all_to_all | solution.py:127
  13.2 11.1 %all-to-all-start.1 = ((bf16[128,8,2048]{2,1,0:T(8,128)(2,1)}), bf16[128,8,2048]{2,1,0:T(8,128)(2,1)}, u32[]{:S(2)}, u32[]{:S(2)}) async-start(bf16[128,8,2048]{2,1,0:T(8,128)(2,1)} %bitcast.123), calls=%async_computation.1 | async-start | bytes 8388608 | tf_op jit(solution)/shard_map/all_to_all | solution.py:127
  24.8 0.7 dynamic-slice_convert_fusion
  25.8 0.3 convert_reduce_fusion.1
  26.7 2.9 %convolution_convert_fusion = bf16[128,2048]{1,0:T(8,128)(2,1)S(1)} fusion(bf16[1024,2048]{1,0:T(8,128)(2,1)} %param.11, f32[1024]{0:T(1024)S(1)} %dynamic-slice_convert_fusion, bf16[16,8,1152]{2,1,0:T(8,128)(2,1)S(1)} %all_to_all.30), kind=kOutput, calls=%fused_computation | convolution fusion | flops 537526272 | bytes 4984832 | tf_op jit(solution)/shard_map/dot_general | solution.py:174
  29.6 0.9 pad_maximum_fusion
  30.4 44.5 %all-to-all-done.1.src_ref = bf16[128,8,2048]{2,1,0:T(8,128)(2,1)} async-done(((bf16[128,8,2048]{2,1,0:T(8,128)(2,1)}), bf16[128,8,2048]{2,1,0:T(8,128)(2,1)}, u32[]{:S(2)}, u32[]{:S(2)}) %all-to-all-start.1) | async-done | bytes 4194336 | tf_op jit(solution)/shard_map/all_to_all | solution.py:127
  74.9 5.5 %all-to-all-start.2 = ((bf16[16,8,2304]{2,1,0:T(8,128)(2,1)}), bf16[16,8,2304]{2,1,0:T(8,128)(2,1)S(1)}, u32[]{:S(2)}, u32[]{:S(2)}) async-start(bf16[16,8,2304]{2,1,0:T(8,128)(2,1)} %bitcast.25), calls=%async_computation.2 | async-start | bytes 1179648 | tf_op jit(solution)/shard_map/all_to_all | solution.py:127
  80.6 3.4 %pick_slabs.4 = (bf16[8,8,2048]{2,1,0:T(8,128)(2,1)}, bf16[8,8,2048]{2,1,0:T(8,128)(2,1)}, bf16[8,8,2048]{2,1,0:T(8,128)(2,1)}, bf16[8,8,2048]{2,1,0:T(8,128)(2,1)}) custom-call(s32[32]{0:T(128)S(1)} %get-tuple-element.83.table_ref, bf16[128,8,2048]{2,1,0:T(8,128)(2,1)} %all-to-all-done.1.src_ref), custom_call_target="tpu_custom_call" | custom-call | bytes 8388608 | tf_op jit(solution)/shard_map/pick_slabs/pallas_call | solution.py:24
  84.0 4.6 %all-to-all-done.2 = bf16[16,8,2304]{2,1,0:T(8,128)(2,1)S(1)} async-done(((bf16[16,8,2304]{2,1,0:T(8,128)(2,1)}), bf16[16,8,2304]{2,1,0:T(8,128)(2,1)S(1)}, u32[]{:S(2)}, u32[]{:S(2)}) %all-to-all-start.2) | async-done | bytes 589856 | tf_op jit(solution)/shard_map/all_to_all | solution.py:127
  88.9 2.3 %fusion.34 = (f32[8,16]{1,0:T(8,128)S(1)}, f32[8,16,1024]{2,1,0:T(8,128)S(1)}) fusion(bf16[8,1,1024,256]{3,2,0,1:T(8,128)(2,1)} %bitcast.127, bf16[1,8,16,128]{3,1,2,0:T(8,128)(2,1)S(1)} %slice_bitcast_fusion.14, pred[8,1024]{1,0:T(8,128)(4,1)S(1)} %iota_compare_fusion), kind=kOutput, calls=%fused_computation.68 | convolution fusion | flops 33947520 | bytes 2662912 | tf_op jit(solution)/shard_map/rjhd,rjpd->rjhp/dot_general | solution.py:92
  91.5 2.1 %fusion.6 = bf16[1,8,16,128]{3,2,1,0:T(8,128)(2,1)S(1)} fusion(bf16[8,1,1024,256]{3,2,0,1:T(8,128)(2,1)} %bitcast.128, f32[8,16,1024]{2,1,0:T(8,128)S(1)} %get-tuple-element.85, f32[8,16]{1,0:T(8,128)S(1)} %get-tuple-element.79, f32[8,16]{1,0:T(8,128)S(1)} %multiply_maximum_fusion, f32[8,128]{1,0:T(8,128)S(1)} %get-tuple-element.80, ...), kind=kOutput, calls=%fused_computation.12 | convolution fusion | flops 33996800 | bytes 2659840 | tf_op jit(solution)/shard_map/rjhp,rjpd->rjhd/dot_general | solution.py:117
  93.6 0.8 broadcast_in_dim.35
  94.5 7.4 %all-to-all-start.3 = ((bf16[16,8,2048]{2,1,0:T(8,128)(2,1)}), bf16[16,8,2048]{2,1,0:T(8,128)(2,1)}, u32[]{:S(2)}, u32[]{:S(2)}) async-start(bf16[16,8,2048]{2,1,0:T(8,128)(2,1)} %broadcast_in_dim.35), calls=%async_computation.3 | async-start | bytes 1048576 | tf_op jit(solution)/shard_map/all_to_all | solution.py:127
  101.9 3.2 %pick_slabs.6 = (bf16[8,8,2048]{2,1,0:T(8,128)(2,1)S(1)}, bf16[8,8,2048]{2,1,0:T(8,128)(2,1)S(1)}, bf16[8,8,2048]{2,1,0:T(8,128)(2,1)S(1)}, bf16[8,8,2048]{2,1,0:T(8,128)(2,1)S(1)}, bf16[8,8,2048]{2,1,0:T(8,128)(2,1)}) custom-call(s32[40]{0:T(128)S(1)} %bitcast.121, bf16[128,8,2048]{2,1,0:T(8,128)(2,1)} %all-to-all-done.1.src_ref), custom_call_target="tpu_custom_call" | custom-call | bytes 8388608 | tf_op jit(solution)/shard_map/pick_slabs/pallas_call | solution.py:24
  105.1 1.2 collective-permute-start.4
  106.3 1.3 collective-permute-start.5
  107.6 1.5 collective-permute-start.6
  109.1 3.2 %pick_slabs.5 = (bf16[8,8,2048]{2,1,0:T(8,128)(2,1)}, bf16[8,8,2048]{2,1,0:T(8,128)(2,1)}, bf16[8,8,2048]{2,1,0:T(8,128)(2,1)S(1)}, bf16[8,8,2048]{2,1,0:T(8,128)(2,1)S(1)}) custom-call(s32[32]{0:T(128)S(1)} %get-tuple-element.82.table_ref, bf16[128,8,2048]{2,1,0:T(8,128)(2,1)} %all-to-all-done.1.src_ref), custom_call_target="tpu_custom_call" | custom-call | bytes 8388608 | tf_op jit(solution)/shard_map/pick_slabs/pallas_call | solution.py:24
  112.3 0.3 collective-permute-start.7
  112.6 0.9 collective-permute-start
  113.5 1.5 collective-permute-done.4.refs_1_
  115.0 1.9 %collective-permute-start.1 = (bf16[8,8,2048]{2,1,0:T(8,128)(2,1)}, bf16[8,8,2048]{2,1,0:T(8,128)(2,1)S(1)}, u32[]{:S(2)}, u32[]{:S(2)}) collective-permute-start(bf16[8,8,2048]{2,1,0:T(8,128)(2,1)} %get-tuple-element.57), channel_id=1, source_target_pairs={{0,112},{8,120},{16,64},{24,72},{32,80},{40,88},{48,96},{56,104},{... | collective-permute-start | bytes 786440 | tf_op jit(solution)/shard_map/ppermute | solution.py:83
  116.9 1.5 collective-permute-start.2
  118.4 4.1 %collective-permute-done.6.refs_3_ = bf16[8,8,2048]{2,1,0:T(8,128)(2,1)S(1)} collective-permute-done((bf16[8,8,2048]{2,1,0:T(8,128)(2,1)S(1)}, bf16[8,8,2048]{2,1,0:T(8,128)(2,1)S(1)}, u32[]{:S(2)}, u32[]{:S(2)}) %collective-permute-start.6) | collective-permute-done | bytes 262176 | tf_op jit(solution)/shard_map/ppermute | solution.py:83
  122.5 0.6 collective-permute-start.3
  123.1 3.8 %convolution_convert_fusion.1 = bf16[128,1024]{1,0:T(8,128)(2,1)} fusion(bf16[2048,1024]{1,0:T(8,128)(2,1)} %param.13, bf16[16,8,2048]{2,1,0:T(8,128)(2,1)} %all-to-all-done.3), kind=kOutput, calls=%fused_computation.7 | convolution fusion | flops 537001984 | bytes 4980736 | tf_op jit(solution)/shard_map/dot_general | solution.py:218
  126.9 7.9 %all-to-all-start.4 = ((bf16[128,8,128]{2,1,0:T(8,128)(2,1)}), bf16[128,8,128]{2,1,0:T(8,128)(2,1)}, u32[]{:S(2)}, u32[]{:S(2)}) async-start(bf16[128,8,128]{2,1,0:T(8,128)(2,1)} %bitcast.126), calls=%async_computation.4 | async-start | bytes 524288 | tf_op jit(solution)/shard_map/all_to_all | solution.py:127
  135.1 2.4 %pick_slabs.7 = (bf16[8,8,2048]{2,1,0:T(8,128)(2,1)S(1)}, bf16[8,8,2048]{2,1,0:T(8,128)(2,1)S(1)}, bf16[8,8,2048]{2,1,0:T(8,128)(2,1)S(1)}) custom-call(s32[24]{0:T(128)S(1)} %slice.55.table_ref, bf16[128,8,2048]{2,1,0:T(8,128)(2,1)} %all-to-all-done.1.src_ref), custom_call_target="tpu_custom_call" | custom-call | bytes 8388608 | tf_op jit(solution)/shard_map/pick_slabs/pallas_call | solution.py:24
  137.5 1.6 place_parts.4.refs_4_
  139.2 1.5 place_parts.5.refs_4_
  140.8 2.2 %collective-permute-start.11 = (bf16[8,8,2048]{2,1,0:T(8,128)(2,1)}, bf16[8,8,2048]{2,1,0:T(8,128)(2,1)S(1)}, u32[]{:S(2)}, u32[]{:S(2)}) collective-permute-start(bf16[8,8,2048]{2,1,0:T(8,128)(2,1)} %get-tuple-element.73), channel_id=1, source_target_pairs={{0,80},{8,88},{16,96},{24,104},{32,112},{40,120},{48,64},{56,72},{... | collective-permute-start | bytes 786440 | tf_op jit(solution)/shard_map/ppermute | solution.py:83
  143.0 0.3 collective-permute-start.12
  143.3 1.8 %collective-permute-start.13 = (bf16[8,8,2048]{2,1,0:T(8,128)(2,1)S(1)}, bf16[8,8,2048]{2,1,0:T(8,128)(2,1)S(1)}, u32[]{:S(2)}, u32[]{:S(2)}) collective-permute-start(bf16[8,8,2048]{2,1,0:T(8,128)(2,1)S(1)} %get-tuple-element.75), channel_id=1, source_target_pairs={{0,32},{8,40},{16,48},{24,56},{32,0},{40,8},{48,16},{56,24},{64,96... | collective-permute-start | bytes 786440 | tf_op jit(solution)/shard_map/ppermute | solution.py:83
  145.1 1.1 collective-permute-start.14
  146.2 1.0 bitcast_reduce_fusion
  147.2 0.7 broadcast_in_dim.36
  147.9 6.6 %all-to-all-start.5 = ((bf16[8,16,8,128]{3,2,1,0:T(8,128)(2,1)}), bf16[8,16,8,128]{3,2,1,0:T(8,128)(2,1)S(1)}, u32[]{:S(2)}, u32[]{:S(2)}) async-start(bf16[8,16,8,128]{3,2,1,0:T(8,128)(2,1)} %broadcast_in_dim.36), calls=%async_computation.5 | async-start | bytes 524288 | tf_op jit(solution)/shard_map/all_to_all | solution.py:127
  154.6 0.5 collective-permute-start.8
  155.1 1.1 collective-permute-start.9
  156.3 3.8 %collective-permute-start.10 = (bf16[8,8,2048]{2,1,0:T(8,128)(2,1)}, bf16[8,8,2048]{2,1,0:T(8,128)(2,1)S(1)}, u32[]{:S(2)}, u32[]{:S(2)}) collective-permute-start(bf16[8,8,2048]{2,1,0:T(8,128)(2,1)} %copy-done.1), channel_id=1, source_target_pairs={{0,104},{8,96},{16,120},{24,112},{32,72},{40,64},{48,88},{56,80},{... | collective-permute-start | bytes 786440 | tf_op jit(solution)/shard_map/ppermute | solution.py:83
  160.0 1.5 place_parts.6.refs_3_
  161.6 13.5 %all-to-all-done.5 = bf16[8,16,8,128]{3,2,1,0:T(8,128)(2,1)S(1)} async-done(((bf16[8,16,8,128]{3,2,1,0:T(8,128)(2,1)}), bf16[8,16,8,128]{3,2,1,0:T(8,128)(2,1)S(1)}, u32[]{:S(2)}, u32[]{:S(2)}) %all-to-all-start.5) | async-done | bytes 262176 | tf_op jit(solution)/shard_map/all_to_all | solution.py:127
  175.2 0.3 copy.47
  175.5 1.0 fusion.8
  176.5 1.4 place_parts.7
  (57 shorter events, 2.3 us)
Async XLA Ops:
  0.6 25.8 %copy-start = (bf16[1024,1,256]{2,0,1:T(8,128)(2,1)S(1)}, bf16[1024,1,256]{2,0,1:T(8,128)(2,1)}, u32[]{:S(2)}) copy-start(bf16[1024,1,256]{2,0,1:T(8,128)(2,1)} %param.12) | copy-start | bytes 1572868
  13.2 12.3 %copy-start.4 = (bf16[8,16384]{1,0:T(8,128)(2,1)S(1)}, bf16[8,16384]{1,0:T(8,128)(2,1)}, u32[]{:S(2)}) copy-start(bf16[8,16384]{1,0:T(8,128)(2,1)} %param.9) | copy-start | bytes 786436
  13.2 61.7 %all-to-all-start.1 = ((bf16[128,8,2048]{2,1,0:T(8,128)(2,1)}), bf16[128,8,2048]{2,1,0:T(8,128)(2,1)}, u32[]{:S(2)}, u32[]{:S(2)}) async-start(bf16[128,8,2048]{2,1,0:T(8,128)(2,1)} %bitcast.123), calls=%async_computation.1 | async-start | bytes 8388608 | tf_op jit(solution)/shard_map/all_to_all | solution.py:127
  25.8 54.7 %copy-start.6 = (s32[8]{0:T(128)S(1)}, s32[8]{0:T(128)}, u32[]{:S(2)}) copy-start(s32[8]{0:T(128)} %param.15) | copy-start | bytes 100
  74.9 13.8 %all-to-all-start.2 = ((bf16[16,8,2304]{2,1,0:T(8,128)(2,1)}), bf16[16,8,2304]{2,1,0:T(8,128)(2,1)S(1)}, u32[]{:S(2)}, u32[]{:S(2)}) async-start(bf16[16,8,2304]{2,1,0:T(8,128)(2,1)} %bitcast.25), calls=%async_computation.2 | async-start | bytes 1179648 | tf_op jit(solution)/shard_map/all_to_all | solution.py:127
  94.5 28.6 %all-to-all-start.3 = ((bf16[16,8,2048]{2,1,0:T(8,128)(2,1)}), bf16[16,8,2048]{2,1,0:T(8,128)(2,1)}, u32[]{:S(2)}, u32[]{:S(2)}) async-start(bf16[16,8,2048]{2,1,0:T(8,128)(2,1)} %broadcast_in_dim.35), calls=%async_computation.3 | async-start | bytes 1048576 | tf_op jit(solution)/shard_map/all_to_all | solution.py:127
  105.1 9.9 %collective-permute-start.4 = (bf16[8,8,2048]{2,1,0:T(8,128)(2,1)S(1)}, bf16[8,8,2048]{2,1,0:T(8,128)(2,1)S(1)}, u32[]{:S(2)}, u32[]{:S(2)}) collective-permute-start(bf16[8,8,2048]{2,1,0:T(8,128)(2,1)S(1)} %get-tuple-element.61), channel_id=1, source_target_pairs={{0,16},{8,24},{16,32},{24,40},{32,48},{40,56},{48,0},{56,8},{64,80... | collective-permute-start | bytes 786440 | tf_op jit(solution)/shard_map/ppermute | solution.py:83
  106.3 10.6 %collective-permute-start.5 = (bf16[8,8,2048]{2,1,0:T(8,128)(2,1)S(1)}, bf16[8,8,2048]{2,1,0:T(8,128)(2,1)S(1)}, u32[]{:S(2)}, u32[]{:S(2)}) collective-permute-start(bf16[8,8,2048]{2,1,0:T(8,128)(2,1)S(1)} %get-tuple-element.62), channel_id=1, source_target_pairs={{0,120},{8,112},{16,72},{24,64},{32,88},{40,80},{48,104},{56,96},{... | collective-permute-start | bytes 786440 | tf_op jit(solution)/shard_map/ppermute | solution.py:83
  107.6 14.9 %collective-permute-start.6 = (bf16[8,8,2048]{2,1,0:T(8,128)(2,1)S(1)}, bf16[8,8,2048]{2,1,0:T(8,128)(2,1)S(1)}, u32[]{:S(2)}, u32[]{:S(2)}) collective-permute-start(bf16[8,8,2048]{2,1,0:T(8,128)(2,1)S(1)} %get-tuple-element.63), channel_id=1, source_target_pairs={{0,96},{8,104},{16,112},{24,120},{32,64},{40,72},{48,80},{56,88},{... | collective-permute-start | bytes 786440 | tf_op jit(solution)/shard_map/ppermute | solution.py:83
  112.3 25.2 %collective-permute-start.7 = (bf16[8,8,2048]{2,1,0:T(8,128)(2,1)}, bf16[8,8,2048]{2,1,0:T(8,128)(2,1)S(1)}, u32[]{:S(2)}, u32[]{:S(2)}) collective-permute-start(bf16[8,8,2048]{2,1,0:T(8,128)(2,1)} %get-tuple-element.64), channel_id=1, source_target_pairs={{0,8},{8,0},{16,24},{24,16},{32,40},{40,32},{48,56},{56,48},{64,72... | collective-permute-start | bytes 786440 | tf_op jit(solution)/shard_map/ppermute | solution.py:83
  112.6 26.6 %collective-permute-start = (bf16[8,8,2048]{2,1,0:T(8,128)(2,1)}, bf16[8,8,2048]{2,1,0:T(8,128)(2,1)S(1)}, u32[]{:S(2)}, u32[]{:S(2)}) collective-permute-start(bf16[8,8,2048]{2,1,0:T(8,128)(2,1)} %get-tuple-element.56), channel_id=1, source_target_pairs={{0,24},{8,16},{16,40},{24,32},{32,56},{40,48},{48,8},{56,0},{64,88... | collective-permute-start | bytes 786440 | tf_op jit(solution)/shard_map/ppermute | solution.py:83
  115.0 24.2 %collective-permute-start.1 = (bf16[8,8,2048]{2,1,0:T(8,128)(2,1)}, bf16[8,8,2048]{2,1,0:T(8,128)(2,1)S(1)}, u32[]{:S(2)}, u32[]{:S(2)}) collective-permute-start(bf16[8,8,2048]{2,1,0:T(8,128)(2,1)} %get-tuple-element.57), channel_id=1, source_target_pairs={{0,112},{8,120},{16,64},{24,72},{32,80},{40,88},{48,96},{56,104},{... | collective-permute-start | bytes 786440 | tf_op jit(solution)/shard_map/ppermute | solution.py:83
  116.9 22.3 %collective-permute-start.2 = (bf16[8,8,2048]{2,1,0:T(8,128)(2,1)}, bf16[8,8,2048]{2,1,0:T(8,128)(2,1)S(1)}, u32[]{:S(2)}, u32[]{:S(2)}) collective-permute-start(bf16[8,8,2048]{2,1,0:T(8,128)(2,1)} %get-tuple-element.58), channel_id=1, source_target_pairs={{0,40},{8,32},{16,56},{24,48},{32,8},{40,0},{48,24},{56,16},{64,10... | collective-permute-start | bytes 786440 | tf_op jit(solution)/shard_map/ppermute | solution.py:83
  122.5 16.7 %collective-permute-start.3 = (bf16[8,8,2048]{2,1,0:T(8,128)(2,1)}, bf16[8,8,2048]{2,1,0:T(8,128)(2,1)S(1)}, u32[]{:S(2)}, u32[]{:S(2)}) collective-permute-start(bf16[8,8,2048]{2,1,0:T(8,128)(2,1)} %get-tuple-element.59), channel_id=1, source_target_pairs={{0,64},{8,72},{16,80},{24,88},{32,96},{40,104},{48,112},{56,120},{... | collective-permute-start | bytes 786440 | tf_op jit(solution)/shard_map/ppermute | solution.py:83
  126.9 19.3 %all-to-all-start.4 = ((bf16[128,8,128]{2,1,0:T(8,128)(2,1)}), bf16[128,8,128]{2,1,0:T(8,128)(2,1)}, u32[]{:S(2)}, u32[]{:S(2)}) async-start(bf16[128,8,128]{2,1,0:T(8,128)(2,1)} %bitcast.126), calls=%async_computation.4 | async-start | bytes 524288 | tf_op jit(solution)/shard_map/all_to_all | solution.py:127
  137.5 3.3 %copy-start.1 = (bf16[8,8,2048]{2,1,0:T(8,128)(2,1)}, bf16[8,8,2048]{2,1,0:T(8,128)(2,1)S(1)}, u32[]{:S(2)}) copy-start(bf16[8,8,2048]{2,1,0:T(8,128)(2,1)S(1)} %get-tuple-element.72) | copy-start | bytes 786436
  137.5 3.3 %copy-start.2 = (bf16[8,8,2048]{2,1,0:T(8,128)(2,1)}, bf16[8,8,2048]{2,1,0:T(8,128)(2,1)S(1)}, u32[]{:S(2)}) copy-start(bf16[8,8,2048]{2,1,0:T(8,128)(2,1)S(1)} %get-tuple-element.71) | copy-start | bytes 786436
  137.5 3.3 %copy-start.3 = (bf16[8,8,2048]{2,1,0:T(8,128)(2,1)}, bf16[8,8,2048]{2,1,0:T(8,128)(2,1)S(1)}, u32[]{:S(2)}) copy-start(bf16[8,8,2048]{2,1,0:T(8,128)(2,1)S(1)} %get-tuple-element.70) | copy-start | bytes 786436
  140.8 14.3 %collective-permute-start.11 = (bf16[8,8,2048]{2,1,0:T(8,128)(2,1)}, bf16[8,8,2048]{2,1,0:T(8,128)(2,1)S(1)}, u32[]{:S(2)}, u32[]{:S(2)}) collective-permute-start(bf16[8,8,2048]{2,1,0:T(8,128)(2,1)} %get-tuple-element.73), channel_id=1, source_target_pairs={{0,80},{8,88},{16,96},{24,104},{32,112},{40,120},{48,64},{56,72},{... | collective-permute-start | bytes 786440 | tf_op jit(solution)/shard_map/ppermute | solution.py:83
  143.0 13.3 %collective-permute-start.12 = (bf16[8,8,2048]{2,1,0:T(8,128)(2,1)}, bf16[8,8,2048]{2,1,0:T(8,128)(2,1)S(1)}, u32[]{:S(2)}, u32[]{:S(2)}) collective-permute-start(bf16[8,8,2048]{2,1,0:T(8,128)(2,1)} %get-tuple-element.74), channel_id=1, source_target_pairs={{0,56},{8,48},{16,8},{24,0},{32,24},{40,16},{48,40},{56,32},{64,12... | collective-permute-start | bytes 786440 | tf_op jit(solution)/shard_map/ppermute | solution.py:83
  143.3 16.8 %collective-permute-start.13 = (bf16[8,8,2048]{2,1,0:T(8,128)(2,1)S(1)}, bf16[8,8,2048]{2,1,0:T(8,128)(2,1)S(1)}, u32[]{:S(2)}, u32[]{:S(2)}) collective-permute-start(bf16[8,8,2048]{2,1,0:T(8,128)(2,1)S(1)} %get-tuple-element.75), channel_id=1, source_target_pairs={{0,32},{8,40},{16,48},{24,56},{32,0},{40,8},{48,16},{56,24},{64,96... | collective-permute-start | bytes 786440 | tf_op jit(solution)/shard_map/ppermute | solution.py:83
  145.1 15.0 %collective-permute-start.14 = (bf16[8,8,2048]{2,1,0:T(8,128)(2,1)S(1)}, bf16[8,8,2048]{2,1,0:T(8,128)(2,1)S(1)}, u32[]{:S(2)}, u32[]{:S(2)}) collective-permute-start(bf16[8,8,2048]{2,1,0:T(8,128)(2,1)S(1)} %get-tuple-element.76), channel_id=1, source_target_pairs={{0,72},{8,64},{16,88},{24,80},{32,104},{40,96},{48,120},{56,112},{... | collective-permute-start | bytes 786440 | tf_op jit(solution)/shard_map/ppermute | solution.py:83
  147.9 27.2 %all-to-all-start.5 = ((bf16[8,16,8,128]{3,2,1,0:T(8,128)(2,1)}), bf16[8,16,8,128]{3,2,1,0:T(8,128)(2,1)S(1)}, u32[]{:S(2)}, u32[]{:S(2)}) async-start(bf16[8,16,8,128]{3,2,1,0:T(8,128)(2,1)} %broadcast_in_dim.36), calls=%async_computation.5 | async-start | bytes 524288 | tf_op jit(solution)/shard_map/all_to_all | solution.py:127
  154.6 20.8 %copy-start.5 = (bf16[8,16384]{1,0:T(8,128)(2,1)S(1)}, bf16[8,16384]{1,0:T(8,128)(2,1)}, u32[]{:S(2)}) copy-start(bf16[8,16384]{1,0:T(8,128)(2,1)} %param.9) | copy-start | bytes 786436
  154.6 21.8 %collective-permute-start.8 = (bf16[8,8,2048]{2,1,0:T(8,128)(2,1)}, bf16[8,8,2048]{2,1,0:T(8,128)(2,1)S(1)}, u32[]{:S(2)}, u32[]{:S(2)}) collective-permute-start(bf16[8,8,2048]{2,1,0:T(8,128)(2,1)} %copy-done.3), channel_id=1, source_target_pairs={{0,88},{8,80},{16,104},{24,96},{32,120},{40,112},{48,72},{56,64},{... | collective-permute-start | bytes 786440 | tf_op jit(solution)/shard_map/ppermute | solution.py:83
  155.1 21.4 %collective-permute-start.9 = (bf16[8,8,2048]{2,1,0:T(8,128)(2,1)}, bf16[8,8,2048]{2,1,0:T(8,128)(2,1)S(1)}, u32[]{:S(2)}, u32[]{:S(2)}) collective-permute-start(bf16[8,8,2048]{2,1,0:T(8,128)(2,1)} %copy-done.2), channel_id=1, source_target_pairs={{0,48},{8,56},{16,0},{24,8},{32,16},{40,24},{48,32},{56,40},{64,11... | collective-permute-start | bytes 786440 | tf_op jit(solution)/shard_map/ppermute | solution.py:83
  156.3 20.2 %collective-permute-start.10 = (bf16[8,8,2048]{2,1,0:T(8,128)(2,1)}, bf16[8,8,2048]{2,1,0:T(8,128)(2,1)S(1)}, u32[]{:S(2)}, u32[]{:S(2)}) collective-permute-start(bf16[8,8,2048]{2,1,0:T(8,128)(2,1)} %copy-done.1), channel_id=1, source_target_pairs={{0,104},{8,96},{16,120},{24,112},{32,72},{40,64},{48,88},{56,80},{... | collective-permute-start | bytes 786440 | tf_op jit(solution)/shard_map/ppermute | solution.py:83

commit v3 on v2

v3 whole, which is shorter than its diff:
```python
import jax
import jax.numpy as jnp
from jax import lax
from jax.experimental import pallas as pl
from jax.experimental.pallas import tpu as pltpu
from jax.sharding import PartitionSpec as P

ANY = pl.BlockSpec(memory_space=pl.ANY)
HBM = pl.BlockSpec(memory_space=pltpu.HBM)
VMEM = pl.BlockSpec(memory_space=pltpu.VMEM)
SMEM = pl.BlockSpec(memory_space=pltpu.SMEM)
LANES = 128


def cost(flops, bytes_accessed):
    return pl.CostEstimate(flops=flops, bytes_accessed=bytes_accessed, transcendentals=0)


def prep_kernel(ids_ref, hidden_ref, out_ref):
    parts, rows, wide = out_ref.shape
    depth = wide - LANES
    row = lax.broadcasted_iota(jnp.int32, (rows, LANES), 0)
    numbers = jnp.zeros((rows, LANES), jnp.int32)
    for i in range(rows):
        numbers = jnp.where(row == i, ids_ref[i], numbers)
    numbers = numbers.astype(jnp.float32).astype(out_ref.dtype)
    for m in range(parts):
        out_ref[m, :, :depth] = hidden_ref[:, m * depth : (m + 1) * depth]
        out_ref[m, :, depth:] = numbers


def prepare(ids, hidden, parts):
    rows, width = hidden.shape
    return pl.pallas_call(
        prep_kernel,
        out_shape=jax.ShapeDtypeStruct((parts, rows, width // parts + LANES), hidden.dtype),
        in_specs=[SMEM, VMEM],
        out_specs=VMEM,
        cost_estimate=cost(0, 4 * hidden.size),
        name="prepare",
    )(ids, hidden)


def attend_kernel(
    lengths_ref, terms_ref, scale_ref, cache_ref, out_ref,
    query_ref, held_ref, score_ref, weight_ref, sums_ref, sems,
):
    copies, rows, query_cols = out_ref.shape
    length, head_dim = cache_ref.shape[1], cache_ref.shape[2] // 2
    heads = query_cols // head_dim
    reads = [
        pltpu.make_async_copy(cache_ref.at[r], held_ref.at[r], sems.at[r]) for r in range(rows)
    ]
    for read in reads:
        read.start()
    total = terms_ref[0].astype(jnp.float32)
    for s in range(1, terms_ref.shape[0]):
        total = total + terms_ref[s].astype(jnp.float32)
    total = (total * scale_ref[...]).astype(jnp.bfloat16).astype(jnp.float32)
    for h in range(heads):
        query_ref[:, h, :] = total[:, h * head_dim : (h + 1) * head_dim]
    new_key = total[:, query_cols : query_cols + head_dim]
    new_value = total[:, query_cols + head_dim :]
    position = lax.broadcasted_iota(jnp.int32, (heads, length), 1)
    score_scale = head_dim ** (-0.5)
    for r in range(rows):
        reads[r].wait()
        scores = lax.dot_general(
            query_ref[r].astype(jnp.bfloat16),
            held_ref[r, :, :head_dim],
            (((1,), (1,)), ((), ())),
            preferred_element_type=jnp.float32,
        )
        score_ref[r] = jnp.where(position < lengths_ref[r], scores * score_scale, -jnp.inf)
    self_score = jnp.sum(query_ref[...] * new_key[:, None, :], axis=2, keepdims=True) * score_scale
    scores = score_ref[...]
    highest = jnp.maximum(jnp.max(scores, axis=2, keepdims=True), self_score)
    expo = jnp.exp(scores - highest)
    self_expo = jnp.exp(self_score - highest)
    denominator = jnp.sum(expo, axis=2, keepdims=True) + self_expo
    weight_ref[...] = (expo / denominator).astype(jnp.bfloat16)
    self_weight = (self_expo / denominator).astype(jnp.bfloat16).astype(jnp.float32)
    sums_ref[...] = self_weight * new_value[:, None, :]
    for r in range(rows):
        sums_ref[r] += jnp.dot(
            weight_ref[r], held_ref[r, :, head_dim:], preferred_element_type=jnp.float32
        )
    for h in range(heads):
        head = sums_ref[:, h, :].astype(out_ref.dtype)
        for copy in range(copies):
            out_ref[copy, :, h * head_dim : (h + 1) * head_dim] = head


def attend(lengths, terms, row_scale, cache):
    copies, rows, cols = terms.shape
    _, length, twice = cache.shape
    head_dim = twice // 2
    query_cols = cols - twice
    heads = query_cols // head_dim
    return pl.pallas_call(
        attend_kernel,
        out_shape=jax.ShapeDtypeStruct((copies, rows, query_cols), jnp.bfloat16),
        in_specs=[SMEM, VMEM, VMEM, HBM],
        out_specs=VMEM,
        scratch_shapes=[
            pltpu.VMEM((rows, heads, head_dim), jnp.float32),
            pltpu.VMEM(cache.shape, cache.dtype),
            pltpu.VMEM((rows, heads, length), jnp.float32),
            pltpu.VMEM((rows, heads, length), jnp.bfloat16),
            pltpu.VMEM((rows, heads, head_dim), jnp.float32),
            pltpu.SemaphoreType.DMA((rows,)),
        ],
        compiler_params=pltpu.CompilerParams(vmem_limit_bytes=60 << 20),
        cost_estimate=cost(4 * cache.size * heads, 2 * cache.size),
        name="attend",
    )(lengths, terms, row_scale, cache)


def output_kernel(heads_ref, weight_ref, out_ref, held_ref, total_ref, sems):
    parts, chunks, rows, chunk = out_ref.shape
    count, depth, cols = held_ref.shape
    reads = [
        pltpu.make_async_copy(
            weight_ref.at[pl.ds(k * depth, depth)], held_ref.at[k], sems.at[k]
        )
        for k in range(count)
    ]
    for read in reads:
        read.start()
    step = 2 * chunk
    for k, read in enumerate(reads):
        read.wait()
        heads = heads_ref[:, k * depth : (k + 1) * depth]
        for j in range(0, cols, step):
            product = jnp.dot(
                heads, held_ref[k, :, j : j + step], preferred_element_type=jnp.float32
            )
            if k:
                product = total_ref[:, j : j + step] + product
            if k < count - 1:
                total_ref[:, j : j + step] = product
                continue
            for i in range(2):
                tile = product[:, i * chunk : (i + 1) * chunk].reshape(parts, rows, chunk)
                out_ref[:, j // chunk + i] = tile.astype(out_ref.dtype)


def project_out(heads, weight, parts, chunks):
    rows, cols = heads.shape[0], weight.shape[1]
    steps = 4
    return pl.pallas_call(
        output_kernel,
        out_shape=jax.ShapeDtypeStruct(
            (parts, chunks, rows // parts, cols // chunks), jnp.bfloat16
        ),
        in_specs=[VMEM, HBM],
        out_specs=VMEM,
        scratch_shapes=[
            pltpu.VMEM((steps, weight.shape[0] // steps, cols), weight.dtype),
            pltpu.VMEM((rows, cols), jnp.float32),
            pltpu.SemaphoreType.DMA((steps,)),
        ],
        compiler_params=pltpu.CompilerParams(vmem_limit_bytes=60 << 20),
        cost_estimate=cost(2 * rows * weight.size, 2 * weight.size),
        name="project_out",
    )(heads, weight)


def pick_kernel(table_ref, src_ref, *refs):
    *out_refs, sem = refs
    count, _, width = out_refs[0].shape
    for j, out_ref in enumerate(out_refs):
        for i in range(count):
            pltpu.make_async_copy(
                src_ref.at[table_ref[j * count + i], :, pl.ds(0, width)], out_ref.at[i], sem.at[j]
            ).start()
    for j, out_ref in enumerate(out_refs):
        pltpu.make_async_copy(out_ref, out_ref, sem.at[j]).wait()


def pick_slabs(table, slabs, parts):
    count = table.shape[0] // parts
    shape = (count, slabs.shape[1], slabs.shape[2])
    return pl.pallas_call(
        pick_kernel,
        out_shape=[jax.ShapeDtypeStruct(shape, slabs.dtype)] * parts,
        in_specs=[SMEM, HBM],
        out_specs=[VMEM] * parts,
        scratch_shapes=[pltpu.SemaphoreType.DMA((parts,))],
        compiler_params=pltpu.CompilerParams(vmem_limit_bytes=16 << 20),
        cost_estimate=cost(0, 4 * parts * count * slabs[0].size),
        name="pick_slabs",
    )(table, slabs)


def place_kernel(owner_ref, *refs):
    *refs, dst_ref, sem = refs
    part_refs = [ref for ref in refs if ref.shape != dst_ref.shape]
    copies = [
        pltpu.make_async_copy(part_ref, dst_ref.at[:, owner_ref[j]], sem.at[j])
        for j, part_ref in enumerate(part_refs)
    ]
    for copy in copies:
        copy.start()
    for copy in copies:
        copy.wait()


def place_parts(owners, parts, count, into=None):
    group, r, c = parts[0].shape
    held = [] if into is None else [into]
    return pl.pallas_call(
        place_kernel,
        out_shape=jax.ShapeDtypeStruct((group, count, r, c), parts[0].dtype),
        in_specs=[SMEM] + [VMEM] * len(parts) + [ANY] * len(held),
        out_specs=ANY,
        input_output_aliases={1 + len(parts): 0} if held else {},
        scratch_shapes=[pltpu.SemaphoreType.DMA((len(parts),))],
        compiler_params=pltpu.CompilerParams(vmem_limit_bytes=16 << 20),
        cost_estimate=pl.CostEstimate(
            flops=0, bytes_accessed=4 * len(parts) * parts[0].size, transcendentals=0
        ),
        name="place_parts",
    )(owners, *parts, *held)


ROUNDS = (
    ((0, 1, 0), (1, 3, 1)),
    ((0, 2, 0), (1, 0, 0), (1, 1, 0), (0, 3, 0), (0, 2, 1)),
    ((1, 0, 1), (0, 1, 1), (1, 3, 0), (1, 1, 1)),
    ((0, 3, 1), (1, 2, 0), (0, 0, 1), (1, 2, 1)),
)
STEPS = ((0, 0, 0),) + tuple(step for steps in ROUNDS for step in steps)
FENCES = {'heads': 3}
EARLY = 8


def shifted(index, step, sign):
    y_lo, x, core = index // 8, index // 2 % 4, index % 2
    return ((y_lo + step[0]) % 2 * 4 + (x + sign * step[1]) % 4) * 2 + (core + step[2]) % 2


def send(part, step):
    return lax.ppermute(part, "dp", [(s, shifted(s, step, 1)) for s in range(16)])


def sum_kernel(terms_ref, out_ref):
    for m in range(terms_ref.shape[0]):
        total = terms_ref[m, 0].astype(jnp.float32)
        for t in range(1, terms_ref.shape[1]):
            total = total + terms_ref[m, t].astype(jnp.float32)
        total = total.astype(out_ref.dtype)
        for copy in range(out_ref.shape[0]):
            out_ref[copy, m] = total


def sum_over_tensor(terms):
    dp, tensor, rows, chunk = terms.shape
    return pl.pallas_call(
        sum_kernel,
        out_shape=jax.ShapeDtypeStruct((tensor, dp, rows, chunk), terms.dtype),
        in_specs=[VMEM],
        out_specs=VMEM,
        cost_estimate=cost(terms.size, 4 * terms.size),
        name="sum_over_tensor",
    )(terms)


def mix_kernel(hidden_ref, chunks_ref, out_ref):
    tensor, dp, _, chunk = chunks_ref.shape
    for m in range(dp):
        for t in range(tensor):
            columns = slice((m * tensor + t) * chunk, (m * tensor + t + 1) * chunk)
            out_ref[:, columns] = (
                hidden_ref[:, columns].astype(jnp.float32)
                + chunks_ref[t, m].astype(jnp.float32)
            ).astype(out_ref.dtype)


def mix(hidden, chunks):
    return pl.pallas_call(
        mix_kernel,
        out_shape=jax.ShapeDtypeStruct(hidden.shape, hidden.dtype),
        in_specs=[VMEM, VMEM],
        out_specs=VMEM,
        cost_estimate=cost(hidden.size, 6 * hidden.size),
        name="mix",
    )(hidden, chunks)


def exchange(x, axes):
    return lax.all_to_all(x, axes, split_axis=0, concat_axis=0, tiled=True)


def on_device(
    hidden,
    norm_gain,
    query_weight,
    keyval_weight,
    output_weight,
    kv_cache,
    cache_lengths,
    next_source,
    block_ids,
):
    barrier = lax.optimization_barrier
    dp, tensor = lax.axis_size("dp"), lax.axis_size("tensor")
    rows, width = hidden.shape
    depth = width // dp
    group = block_ids.shape[0]
    mine = lax.axis_index("dp")

    arrived = exchange(prepare(block_ids, hidden, dp), "dp")

    block_rows = next_source.shape[1]
    piece_rows = block_rows // dp
    tile_cols = next_source.shape[2] // tensor
    slabs = next_source.reshape(dp, piece_rows, tensor, tile_cols).transpose(0, 2, 1, 3)
    slabs, arrived = barrier((slabs.reshape(dp * tensor, piece_rows, tile_cols), arrived))
    spread = exchange(slabs, ("dp", "tensor"))

    stream = hidden.astype(jnp.float32)
    meansq = jnp.mean(stream * stream, axis=-1, keepdims=True)
    row_scale = lax.rsqrt(meansq + 1e-05)
    gain = lax.dynamic_slice(norm_gain, (mine * depth,), (depth,))
    pieces = (
        arrived[:, :, :depth].reshape(dp * rows, depth).astype(jnp.float32)
        * gain.astype(jnp.float32)
    ).astype(jnp.bfloat16)
    flat_kv = keyval_weight.reshape(keyval_weight.shape[0], -1)
    partial = jnp.concatenate(
        [
            jnp.dot(pieces, query_weight, preferred_element_type=jnp.float32).astype(jnp.bfloat16),
            jnp.dot(pieces, flat_kv, preferred_element_type=jnp.float32).astype(jnp.bfloat16),
        ],
        axis=1,
    )
    cache = kv_cache.reshape(rows, kv_cache.shape[2], kv_cache.shape[3])
    ids = arrived[:, :, depth].reshape(dp * group).astype(jnp.int32)
    targets = jnp.stack([shifted(mine, step, 1) for step in STEPS])
    wanted = (targets[:, None] * group + jnp.arange(group, dtype=jnp.int32)[None, :]).reshape(-1)
    table = jnp.sum(
        jnp.where(
            ids[None, :] == wanted[:, None],
            jnp.arange(dp * group, dtype=jnp.int32)[None, :],
            0,
        ),
        axis=1,
    )
    owners = jnp.stack([shifted(mine, step, -1) for step in STEPS])
    partial, row_scale, table, owners, spread = barrier(
        (partial, row_scale, table, owners, spread)
    )

    terms = exchange(partial.reshape(dp, rows, -1), "dp")

    bounds = [0, 1 + len(ROUNDS[0])]
    for steps in ROUNDS[1:]:
        bounds.append(bounds[-1] + len(steps))
    tables = [table[group * i : group * j] for i, j in zip(bounds[:-1], bounds[1:])]
    kept, *ready = pick_slabs(tables[0], spread, bounds[1])
    landed = [kept] + [send(part, step) for part, step in zip(ready, ROUNDS[0])]

    def start_round(number, anchor):
        count = len(ROUNDS[number])
        anchor, *ready = barrier((anchor, *pick_slabs(tables[number], spread, count)))
        landed.extend(send(part, step) for part, step in zip(ready, ROUNDS[number]))
        return anchor

    def fence(name, anchor):
        count = FENCES.get(name, 0)
        anchor, *done = barrier((anchor, *landed[:count]))
        landed[:count] = done
        return anchor

    heads_out = attend(cache_lengths, terms, row_scale, cache)
    heads_out = fence("heads", heads_out)
    heads_out = start_round(1, heads_out)
    all_heads = exchange(heads_out, "dp")
    outbound = project_out(all_heads.reshape(dp * rows, -1), output_weight, dp, tensor)
    chunk = outbound.shape[3]
    outbound = outbound.reshape(dp * tensor, rows, chunk)
    outbound = fence("outbound", outbound)
    outbound = start_round(2, outbound)
    terms = exchange(outbound, ("dp", "tensor"))
    summed = sum_over_tensor(terms.reshape(dp, tensor, rows, chunk))
    summed = fence("summed", summed)
    placed = place_parts(owners[:EARLY], landed[:EARLY], dp)
    summed, placed = barrier((summed, placed))
    summed = start_round(3, summed)
    chunks = exchange(summed, "tensor")
    mixed = mix(hidden, chunks)

    placed = place_parts(owners[EARLY:], landed[EARLY:], dp, placed)
    next_weight = placed.reshape(group * block_rows, tile_cols)
    return (mixed, next_weight)


def solution(mesh):
    return jax.shard_map(
        on_device,
        mesh=mesh,
        in_specs=(
            P("dp", None),
            P(),
            P("dp", "tensor"),
            P("dp", "tensor", None),
            P("tensor", "dp"),
            P("dp", "tensor", None, None),
            P("dp"),
            P(("dp", "tensor"), None, None),
            P("dp"),
        ),
        out_specs=(P("dp", None), P("dp", "tensor")),
        check_vma=False,
    )
```

time: 179 us -> 176 us (0.983)
  the two profiles are of different devices: /device:TPU:4 before, /device:TPU:3 now
where the time goes in v3:
time: 176 us; the launch traced here: 175 us
  starting transfers between devices  57.8 us (33%)
  waiting for transfers between devices  50.5 us (29%)
  blocking collectives  31.5 us (18%)
  Pallas kernels  27.2 us (15%)
  matrix products  3.14 us (2%)
  other arithmetic  2.41 us (1%)
    all_to_all x4, waiting for transfers between devices, exchange(): return lax.all_to_all(x, axes, split_axis=0, concat_axis=0, tiled=True)  49.5 us
    all_to_all x2, blocking collectives, exchange(): return lax.all_to_all(x, axes, split_axis=0, concat_axis=0, tiled=True)  31.5 us
    all_to_all x4, starting transfers between devices, exchange(): return lax.all_to_all(x, axes, split_axis=0, concat_axis=0, tiled=True)  31 us
    ppermute x15, starting transfers between devices, send(): lax.ppermute(part, 'dp', [(s, shifted(s, step, 1)) for s in range(16)])  26.8 us
    pallas_call x4, Pallas kernels, pick_slabs(): pl.pallas_call(pick_kernel, out_shape=[jax.ShapeDtypeStruct(shape, slabs....  8.76 us
    pallas_call x1, Pallas kernels, attend(): pl.pallas_call(attend_kernel, out_shape=jax.ShapeDtypeStruct((copies, row...  5.06 us
    pallas_call x1, Pallas kernels, project_out(): pl.pallas_call(output_kernel, out_shape=jax.ShapeDtypeStruct((parts, chun...  4.27 us
    pallas_call x2, Pallas kernels, place_parts(): pl.pallas_call(place_kernel, out_shape=jax.ShapeDtypeStruct((group, count...  3.9 us
  transfers between devices with their start and end apart: 19, of which 5 were waited for; matrix products, arithmetic and copies ran while one was open for 4% of the time, Pallas kernels for 13%

profile of v3, /device:TPU:3, one launch (start us, length us, event | category | flops | bytes accessed | tf_op | source)
XLA Modules:
  0.0 174.9 jit_solution(12436487256209964867)
XLA Ops:
  0.6 1.8 %prepare.1 = bf16[16,8,1152]{2,1,0:T(8,128)(2,1)} custom-call(s32[8]{0:T(128)} %ids_ref.1, bf16[8,16384]{1,0:T(8,128)(2,1)} %hidden_ref.3), custom_call_target="tpu_custom_call" | custom-call | bytes 524288 | tf_op jit(solution)/shard_map/prepare/pallas_call | solution.py:34
  2.4 12.5 %all_to_all.30 = bf16[16,8,1152]{2,1,0:T(8,128)(2,1)S(1)} all-to-all(bf16[16,8,1152]{2,1,0:T(8,128)(2,1)} %prepare.1), channel_id=1, replica_groups=mesh['dp'=16,'tensor'=8] {'dp'}, dimensions={0} | all-to-all | bytes 589824 | tf_op jit(solution)/shard_map/all_to_all | solution.py:292
  14.9 10.0 %all-to-all-start.1 = ((bf16[128,8,2048]{2,1,0:T(8,128)(2,1)}), bf16[128,8,2048]{2,1,0:T(8,128)(2,1)}, u32[]{:S(2)}, u32[]{:S(2)}) async-start(bf16[128,8,2048]{2,1,0:T(8,128)(2,1)} %bitcast.59), calls=%async_computation.1 | async-start | bytes 8388608 | tf_op jit(solution)/shard_map/all_to_all | solution.py:292
  25.2 0.1 stack.110
  25.3 0.1 add.488
  25.4 0.1 stack.123
  25.5 0.7 dynamic-slice_convert_fusion
  26.2 0.2 multiply_reduce_fusion
  26.5 0.4 convert_reduce_fusion
  26.9 0.1 reshape.222
  26.9 0.2 select_reduce_fusion
  27.1 0.2 convolution_convert_fusion.1
  27.4 2.9 %convolution_convert_fusion = bf16[128,2048]{1,0:T(8,128)(2,1)S(1)} fusion(bf16[1024,2048]{1,0:T(8,128)(2,1)} %param.11, f32[1024]{0:T(1024)S(1)} %dynamic-slice_convert_fusion, bf16[16,8,1152]{2,1,0:T(8,128)(2,1)S(1)} %all_to_all.30), kind=kOutput, calls=%fused_computation | convolution fusion | flops 537526272 | bytes 4984832 | tf_op jit(solution)/shard_map/dot_general | solution.py:333
  30.3 0.9 pad_maximum_fusion
  31.2 45.3 %all-to-all-done.1.src_ref = bf16[128,8,2048]{2,1,0:T(8,128)(2,1)} async-done(((bf16[128,8,2048]{2,1,0:T(8,128)(2,1)}), bf16[128,8,2048]{2,1,0:T(8,128)(2,1)}, u32[]{:S(2)}, u32[]{:S(2)}) %all-to-all-start.1) | async-done | bytes 4194336 | tf_op jit(solution)/shard_map/all_to_all | solution.py:292
  76.4 4.5 %all-to-all-start.2 = ((bf16[16,8,2304]{2,1,0:T(8,128)(2,1)}), bf16[16,8,2304]{2,1,0:T(8,128)(2,1)}, u32[]{:S(2)}, u32[]{:S(2)}) async-start(bf16[16,8,2304]{2,1,0:T(8,128)(2,1)} %bitcast.35), calls=%async_computation.2 | async-start | bytes 1179648 | tf_op jit(solution)/shard_map/all_to_all | solution.py:292
  81.0 1.6 pick_slabs.4
  82.6 1.3 collective-permute-start
  83.9 1.7 collective-permute-start.1
  85.7 0.7 copy.14.scale_ref
  86.3 2.7 %pick_slabs.5 = (bf16[8,8,2048]{2,1,0:T(8,128)(2,1)S(1)}, bf16[8,8,2048]{2,1,0:T(8,128)(2,1)S(1)}, bf16[8,8,2048]{2,1,0:T(8,128)(2,1)S(1)}, bf16[8,8,2048]{2,1,0:T(8,128)(2,1)}, bf16[8,8,2048]{2,1,0:T(8,128)(2,1)}) custom-call(s32[40]{0:T(128)S(1)} %slice.27.table_ref, bf16[128,8,2048]{2,1,0:T(8,128)(2,1)} %all-to-all-done.1.src_ref), custom_call_target="tpu_custom_call" | custom-call | bytes 2621440 | tf_op jit(solution)/shard_map/pick_slabs/pallas_call | solution.py:184
  89.0 1.4 all-to-all-done.2.terms_ref
  90.4 5.1 %attend.1 = bf16[16,8,2048]{2,1,0:T(8,128)(2,1)} custom-call(s32[8]{0:T(128)} %lengths_ref.1, bf16[16,8,2304]{2,1,0:T(8,128)(2,1)} %all-to-all-done.2.terms_ref, f32[8,1]{1,0:T(8,128)} %copy.14.scale_ref, bf16[8,1024,256]{2,1,0:T(8,128)(2,1)} %bitcast.58), custom_call_target="tpu_custom_call" | custom-call | flops 134217728 | bytes 4194304 | tf_op jit(solution)/shard_map/attend/pallas_call | solution.py:100
  95.4 0.7 collective-permute-done.1.refs_2_
  96.1 6.4 %all-to-all-start.3 = ((bf16[16,8,2048]{2,1,0:T(8,128)(2,1)}), bf16[16,8,2048]{2,1,0:T(8,128)(2,1)}, u32[]{:S(2)}, u32[]{:S(2)}) async-start(bf16[16,8,2048]{2,1,0:T(8,128)(2,1)} %attend.1), calls=%async_computation.3 | async-start | bytes 1048576 | tf_op jit(solution)/shard_map/all_to_all | solution.py:292
  102.5 1.8 %collective-permute-start.2 = (bf16[8,8,2048]{2,1,0:T(8,128)(2,1)S(1)}, bf16[8,8,2048]{2,1,0:T(8,128)(2,1)S(1)}, u32[]{:S(2)}, u32[]{:S(2)}) collective-permute-start(bf16[8,8,2048]{2,1,0:T(8,128)(2,1)S(1)} %get-tuple-element.72), channel_id=1, source_target_pairs={{0,32},{8,40},{16,48},{24,56},{32,0},{40,8},{48,16},{56,24},{64,96... | collective-permute-start | bytes 786440 | tf_op jit(solution)/shard_map/ppermute | solution.py:244
  104.3 1.2 collective-permute-start.3
  105.6 2.7 %pick_slabs.6 = (bf16[8,8,2048]{2,1,0:T(8,128)(2,1)}, bf16[8,8,2048]{2,1,0:T(8,128)(2,1)}, bf16[8,8,2048]{2,1,0:T(8,128)(2,1)}, bf16[8,8,2048]{2,1,0:T(8,128)(2,1)}) custom-call(s32[32]{0:T(128)S(1)} %get-tuple-element.95.table_ref, bf16[128,8,2048]{2,1,0:T(8,128)(2,1)} %all-to-all-done.1.src_ref), custom_call_target="tpu_custom_call" | custom-call | bytes 2097152 | tf_op jit(solution)/shard_map/pick_slabs/pallas_call | solution.py:184
  108.4 1.5 collective-permute-start.5
  109.8 2.7 %collective-permute-start.6 = (bf16[8,8,2048]{2,1,0:T(8,128)(2,1)}, bf16[8,8,2048]{2,1,0:T(8,128)(2,1)S(1)}, u32[]{:S(2)}, u32[]{:S(2)}) collective-permute-start(bf16[8,8,2048]{2,1,0:T(8,128)(2,1)} %get-tuple-element.76), channel_id=1, source_target_pairs={{0,40},{8,32},{16,56},{24,48},{32,8},{40,0},{48,24},{56,16},{64,10... | collective-permute-start | bytes 786440 | tf_op jit(solution)/shard_map/ppermute | solution.py:244
  112.5 4.3 %project_out.1 = bf16[16,8,8,128]{3,2,1,0:T(8,128)(2,1)} custom-call(bf16[128,2048]{1,0:T(8,128)(2,1)} %bitcast.37.heads_ref, bf16[2048,1024]{1,0:T(8,128)(2,1)} %weight_ref.1), custom_call_target="tpu_custom_call" | custom-call | flops 536870912 | bytes 4194304 | tf_op jit(solution)/shard_map/project_out/pallas_call | solution.py:151
  116.8 2.2 %collective-permute-start.7 = (bf16[8,8,2048]{2,1,0:T(8,128)(2,1)}, bf16[8,8,2048]{2,1,0:T(8,128)(2,1)S(1)}, u32[]{:S(2)}, u32[]{:S(2)}) collective-permute-start(bf16[8,8,2048]{2,1,0:T(8,128)(2,1)} %get-tuple-element.83), channel_id=1, source_target_pairs={{0,72},{8,64},{16,88},{24,80},{32,104},{40,96},{48,120},{56,112},{... | collective-permute-start | bytes 786440 | tf_op jit(solution)/shard_map/ppermute | solution.py:244
  119.0 2.3 %collective-permute-start.8 = (bf16[8,8,2048]{2,1,0:T(8,128)(2,1)}, bf16[8,8,2048]{2,1,0:T(8,128)(2,1)S(1)}, u32[]{:S(2)}, u32[]{:S(2)}) collective-permute-start(bf16[8,8,2048]{2,1,0:T(8,128)(2,1)} %get-tuple-element.84), channel_id=1, source_target_pairs={{0,24},{8,16},{16,40},{24,32},{32,56},{40,48},{48,8},{56,0},{64,88... | collective-permute-start | bytes 786440 | tf_op jit(solution)/shard_map/ppermute | solution.py:244
  121.3 0.2 collective-permute-done.4.refs_5_
  121.6 3.2 %collective-permute-start.9 = (bf16[8,8,2048]{2,1,0:T(8,128)(2,1)}, bf16[8,8,2048]{2,1,0:T(8,128)(2,1)S(1)}, u32[]{:S(2)}, u32[]{:S(2)}) collective-permute-start(bf16[8,8,2048]{2,1,0:T(8,128)(2,1)} %get-tuple-element.85), channel_id=1, source_target_pairs={{0,112},{8,120},{16,64},{24,72},{32,80},{40,88},{48,96},{56,104},{... | collective-permute-start | bytes 786440 | tf_op jit(solution)/shard_map/ppermute | solution.py:244
  124.7 10.1 %all-to-all-start.4 = ((bf16[128,8,128]{2,1,0:T(8,128)(2,1)}), bf16[128,8,128]{2,1,0:T(8,128)(2,1)}, u32[]{:S(2)}, u32[]{:S(2)}) async-start(bf16[128,8,128]{2,1,0:T(8,128)(2,1)} %bitcast.60), calls=%async_computation.4 | async-start | bytes 524288 | tf_op jit(solution)/shard_map/all_to_all | solution.py:292
  134.8 1.7 pick_slabs.7
  136.6 0.1 fusion.11
  136.7 2.0 %place_parts.2.refs_8_ = bf16[8,16,8,2048]{3,2,1,0:T(8,128)(2,1)} custom-call(s32[8]{0:T(128)S(1)} %get-tuple-element.93.owner_ref, bf16[8,8,2048]{2,1,0:T(8,128)(2,1)S(1)} %get-tuple-element.69.refs_0_, bf16[8,8,2048]{2,1,0:T(8,128)(2,1)S(1)} %collective-permute-done.refs_1_, bf16[8,8,2048]{2,1,0:T(8,128)(2,1)S(1)} %collective-permute-done.1.refs_2_, ...), custom_call_target="tpu_custom_call" | custom-call | bytes 4194304 | tf_op jit(solution)/shard_map/place_parts/pallas_call | solution.py:212
  138.7 2.4 %collective-permute-start.10 = (bf16[8,8,2048]{2,1,0:T(8,128)(2,1)}, bf16[8,8,2048]{2,1,0:T(8,128)(2,1)S(1)}, u32[]{:S(2)}, u32[]{:S(2)}) collective-permute-start(bf16[8,8,2048]{2,1,0:T(8,128)(2,1)} %get-tuple-element.86), channel_id=1, source_target_pairs={{0,88},{8,80},{16,104},{24,96},{32,120},{40,112},{48,72},{56,64},{... | collective-permute-start | bytes 786440 | tf_op jit(solution)/shard_map/ppermute | solution.py:244
  141.1 2.9 %all-to-all-done.4 = bf16[128,8,128]{2,1,0:T(8,128)(2,1)} async-done(((bf16[128,8,128]{2,1,0:T(8,128)(2,1)}), bf16[128,8,128]{2,1,0:T(8,128)(2,1)}, u32[]{:S(2)}, u32[]{:S(2)}) %all-to-all-start.4) | async-done | bytes 262176 | tf_op jit(solution)/shard_map/all_to_all | solution.py:292
  143.9 1.7 sum_over_tensor.1
  145.6 2.3 %collective-permute-start.11 = (bf16[8,8,2048]{2,1,0:T(8,128)(2,1)}, bf16[8,8,2048]{2,1,0:T(8,128)(2,1)S(1)}, u32[]{:S(2)}, u32[]{:S(2)}) collective-permute-start(bf16[8,8,2048]{2,1,0:T(8,128)(2,1)} %copy-done.4), channel_id=1, source_target_pairs={{0,56},{8,48},{16,8},{24,0},{32,24},{40,16},{48,40},{56,32},{64,12... | collective-permute-start | bytes 786440 | tf_op jit(solution)/shard_map/ppermute | solution.py:244
  147.9 0.5 collective-permute-start.12
  148.4 3.7 %collective-permute-start.14 = (bf16[8,8,2048]{2,1,0:T(8,128)(2,1)}, bf16[8,8,2048]{2,1,0:T(8,128)(2,1)S(1)}, u32[]{:S(2)}, u32[]{:S(2)}) collective-permute-start(bf16[8,8,2048]{2,1,0:T(8,128)(2,1)} %copy-done.1), channel_id=1, source_target_pairs={{0,104},{8,96},{16,120},{24,112},{32,72},{40,64},{48,88},{56,80},{... | collective-permute-start | bytes 786440 | tf_op jit(solution)/shard_map/ppermute | solution.py:244
  152.2 19.0 %all_to_all.31.chunks_ref = bf16[8,16,8,128]{3,2,1,0:T(8,128)(2,1)} all-to-all(bf16[8,16,8,128]{3,2,1,0:T(8,128)(2,1)} %sum_over_tensor.1), channel_id=1, replica_groups=mesh['dp'=16,'tensor'=8] {'tensor'}, dimensions={0} | all-to-all | bytes 524288 | tf_op jit(solution)/shard_map/all_to_all | solution.py:292
  171.2 1.8 %mix.1 = bf16[8,16384]{1,0:T(8,128)(2,1)} custom-call(bf16[8,16384]{1,0:T(8,128)(2,1)} %hidden_ref.3, bf16[8,16,8,128]{3,2,1,0:T(8,128)(2,1)} %all_to_all.31.chunks_ref), custom_call_target="tpu_custom_call" | custom-call | flops 131072 | bytes 786432 | tf_op jit(solution)/shard_map/mix/pallas_call | solution.py:281
  173.0 1.9 %place_parts.3 = bf16[8,16,8,2048]{3,2,1,0:T(8,128)(2,1)} custom-call(s32[8]{0:T(128)S(1)} %get-tuple-element.92.owner_ref, bf16[8,8,2048]{2,1,0:T(8,128)(2,1)S(1)} %collective-permute-done.7.refs_0_, bf16[8,8,2048]{2,1,0:T(8,128)(2,1)S(1)} %collective-permute-done.8.refs_1_, ...), custom_call_target="tpu_custom_call", output_to_operand_aliasing={{}: (9, {})} | custom-call | bytes 4194304 | tf_op jit(solution)/shard_map/place_parts/pallas_call | solution.py:212
  (33 shorter events, 0.3 us)
Async XLA Ops:
  0.6 26.5 %copy-start = (bf16[1024,1,256]{2,0,1:T(8,128)(2,1)S(1)}, bf16[1024,1,256]{2,0,1:T(8,128)(2,1)}, u32[]{:S(2)}) copy-start(bf16[1024,1,256]{2,0,1:T(8,128)(2,1)} %param.12) | copy-start | bytes 1572868
  14.9 11.4 %copy-start.5 = (bf16[8,16384]{1,0:T(8,128)(2,1)S(1)}, bf16[8,16384]{1,0:T(8,128)(2,1)}, u32[]{:S(2)}) copy-start(bf16[8,16384]{1,0:T(8,128)(2,1)} %hidden_ref.3) | copy-start | bytes 786436
  14.9 61.6 %all-to-all-start.1 = ((bf16[128,8,2048]{2,1,0:T(8,128)(2,1)}), bf16[128,8,2048]{2,1,0:T(8,128)(2,1)}, u32[]{:S(2)}, u32[]{:S(2)}) async-start(bf16[128,8,2048]{2,1,0:T(8,128)(2,1)} %bitcast.59), calls=%async_computation.1 | async-start | bytes 8388608 | tf_op jit(solution)/shard_map/all_to_all | solution.py:292
  76.4 14.0 %all-to-all-start.2 = ((bf16[16,8,2304]{2,1,0:T(8,128)(2,1)}), bf16[16,8,2304]{2,1,0:T(8,128)(2,1)}, u32[]{:S(2)}, u32[]{:S(2)}) async-start(bf16[16,8,2304]{2,1,0:T(8,128)(2,1)} %bitcast.35), calls=%async_computation.2 | async-start | bytes 1179648 | tf_op jit(solution)/shard_map/all_to_all | solution.py:292
  82.6 12.8 %collective-permute-start = (bf16[8,8,2048]{2,1,0:T(8,128)(2,1)S(1)}, bf16[8,8,2048]{2,1,0:T(8,128)(2,1)S(1)}, u32[]{:S(2)}, u32[]{:S(2)}) collective-permute-start(bf16[8,8,2048]{2,1,0:T(8,128)(2,1)S(1)} %get-tuple-element.54), channel_id=1, source_target_pairs={{0,16},{8,24},{16,32},{24,40},{32,48},{40,56},{48,0},{56,8},{64,80... | collective-permute-start | bytes 786440 | tf_op jit(solution)/shard_map/ppermute | solution.py:244
  83.9 12.3 %collective-permute-start.1 = (bf16[8,8,2048]{2,1,0:T(8,128)(2,1)S(1)}, bf16[8,8,2048]{2,1,0:T(8,128)(2,1)S(1)}, u32[]{:S(2)}, u32[]{:S(2)}) collective-permute-start(bf16[8,8,2048]{2,1,0:T(8,128)(2,1)S(1)} %get-tuple-element.55), channel_id=1, source_target_pairs={{0,120},{8,112},{16,72},{24,64},{32,88},{40,80},{48,104},{56,96},{... | collective-permute-start | bytes 786440 | tf_op jit(solution)/shard_map/ppermute | solution.py:244
  96.1 16.4 %all-to-all-start.3 = ((bf16[16,8,2048]{2,1,0:T(8,128)(2,1)}), bf16[16,8,2048]{2,1,0:T(8,128)(2,1)}, u32[]{:S(2)}, u32[]{:S(2)}) async-start(bf16[16,8,2048]{2,1,0:T(8,128)(2,1)} %attend.1), calls=%async_computation.3 | async-start | bytes 1048576 | tf_op jit(solution)/shard_map/all_to_all | solution.py:292
  102.5 14.3 %collective-permute-start.2 = (bf16[8,8,2048]{2,1,0:T(8,128)(2,1)S(1)}, bf16[8,8,2048]{2,1,0:T(8,128)(2,1)S(1)}, u32[]{:S(2)}, u32[]{:S(2)}) collective-permute-start(bf16[8,8,2048]{2,1,0:T(8,128)(2,1)S(1)} %get-tuple-element.72), channel_id=1, source_target_pairs={{0,32},{8,40},{16,48},{24,56},{32,0},{40,8},{48,16},{56,24},{64,96... | collective-permute-start | bytes 786440 | tf_op jit(solution)/shard_map/ppermute | solution.py:244
  104.3 14.7 %collective-permute-start.3 = (bf16[8,8,2048]{2,1,0:T(8,128)(2,1)S(1)}, bf16[8,8,2048]{2,1,0:T(8,128)(2,1)S(1)}, u32[]{:S(2)}, u32[]{:S(2)}) collective-permute-start(bf16[8,8,2048]{2,1,0:T(8,128)(2,1)S(1)} %get-tuple-element.73), channel_id=1, source_target_pairs={{0,64},{8,72},{16,80},{24,88},{32,96},{40,104},{48,112},{56,120},{... | collective-permute-start | bytes 786440 | tf_op jit(solution)/shard_map/ppermute | solution.py:244
  105.6 16.0 %collective-permute-start.4 = (bf16[8,8,2048]{2,1,0:T(8,128)(2,1)S(1)}, bf16[8,8,2048]{2,1,0:T(8,128)(2,1)S(1)}, u32[]{:S(2)}, u32[]{:S(2)}) collective-permute-start(bf16[8,8,2048]{2,1,0:T(8,128)(2,1)S(1)} %get-tuple-element.74), channel_id=1, source_target_pairs={{0,80},{8,88},{16,96},{24,104},{32,112},{40,120},{48,64},{56,72},{... | collective-permute-start | bytes 786440 | tf_op jit(solution)/shard_map/ppermute | solution.py:244
  108.4 28.3 %collective-permute-start.5 = (bf16[8,8,2048]{2,1,0:T(8,128)(2,1)}, bf16[8,8,2048]{2,1,0:T(8,128)(2,1)S(1)}, u32[]{:S(2)}, u32[]{:S(2)}) collective-permute-start(bf16[8,8,2048]{2,1,0:T(8,128)(2,1)} %get-tuple-element.75), channel_id=1, source_target_pairs={{0,48},{8,56},{16,0},{24,8},{32,16},{40,24},{48,32},{56,40},{64,11... | collective-permute-start | bytes 786440 | tf_op jit(solution)/shard_map/ppermute | solution.py:244
  109.8 26.8 %collective-permute-start.6 = (bf16[8,8,2048]{2,1,0:T(8,128)(2,1)}, bf16[8,8,2048]{2,1,0:T(8,128)(2,1)S(1)}, u32[]{:S(2)}, u32[]{:S(2)}) collective-permute-start(bf16[8,8,2048]{2,1,0:T(8,128)(2,1)} %get-tuple-element.76), channel_id=1, source_target_pairs={{0,40},{8,32},{16,56},{24,48},{32,8},{40,0},{48,24},{56,16},{64,10... | collective-permute-start | bytes 786440 | tf_op jit(solution)/shard_map/ppermute | solution.py:244
  116.8 31.1 %collective-permute-start.7 = (bf16[8,8,2048]{2,1,0:T(8,128)(2,1)}, bf16[8,8,2048]{2,1,0:T(8,128)(2,1)S(1)}, u32[]{:S(2)}, u32[]{:S(2)}) collective-permute-start(bf16[8,8,2048]{2,1,0:T(8,128)(2,1)} %get-tuple-element.83), channel_id=1, source_target_pairs={{0,72},{8,64},{16,88},{24,80},{32,104},{40,96},{48,120},{56,112},{... | collective-permute-start | bytes 786440 | tf_op jit(solution)/shard_map/ppermute | solution.py:244
  119.0 29.4 %collective-permute-start.8 = (bf16[8,8,2048]{2,1,0:T(8,128)(2,1)}, bf16[8,8,2048]{2,1,0:T(8,128)(2,1)S(1)}, u32[]{:S(2)}, u32[]{:S(2)}) collective-permute-start(bf16[8,8,2048]{2,1,0:T(8,128)(2,1)} %get-tuple-element.84), channel_id=1, source_target_pairs={{0,24},{8,16},{16,40},{24,32},{32,56},{40,48},{48,8},{56,0},{64,88... | collective-permute-start | bytes 786440 | tf_op jit(solution)/shard_map/ppermute | solution.py:244
  121.6 26.9 %collective-permute-start.9 = (bf16[8,8,2048]{2,1,0:T(8,128)(2,1)}, bf16[8,8,2048]{2,1,0:T(8,128)(2,1)S(1)}, u32[]{:S(2)}, u32[]{:S(2)}) collective-permute-start(bf16[8,8,2048]{2,1,0:T(8,128)(2,1)} %get-tuple-element.85), channel_id=1, source_target_pairs={{0,112},{8,120},{16,64},{24,72},{32,80},{40,88},{48,96},{56,104},{... | collective-permute-start | bytes 786440 | tf_op jit(solution)/shard_map/ppermute | solution.py:244
  124.7 19.2 %all-to-all-start.4 = ((bf16[128,8,128]{2,1,0:T(8,128)(2,1)}), bf16[128,8,128]{2,1,0:T(8,128)(2,1)}, u32[]{:S(2)}, u32[]{:S(2)}) async-start(bf16[128,8,128]{2,1,0:T(8,128)(2,1)} %bitcast.60), calls=%async_computation.4 | async-start | bytes 524288 | tf_op jit(solution)/shard_map/all_to_all | solution.py:292
  136.6 2.1 %copy-start.1 = (bf16[8,8,2048]{2,1,0:T(8,128)(2,1)}, bf16[8,8,2048]{2,1,0:T(8,128)(2,1)S(1)}, u32[]{:S(2)}) copy-start(bf16[8,8,2048]{2,1,0:T(8,128)(2,1)S(1)} %get-tuple-element.90) | copy-start | bytes 786436
  136.6 2.1 %copy-start.2 = (bf16[8,8,2048]{2,1,0:T(8,128)(2,1)}, bf16[8,8,2048]{2,1,0:T(8,128)(2,1)S(1)}, u32[]{:S(2)}) copy-start(bf16[8,8,2048]{2,1,0:T(8,128)(2,1)S(1)} %get-tuple-element.89) | copy-start | bytes 786436
  136.6 2.1 %copy-start.3 = (bf16[8,8,2048]{2,1,0:T(8,128)(2,1)}, bf16[8,8,2048]{2,1,0:T(8,128)(2,1)S(1)}, u32[]{:S(2)}) copy-start(bf16[8,8,2048]{2,1,0:T(8,128)(2,1)S(1)} %get-tuple-element.88) | copy-start | bytes 786436
  136.6 2.1 %copy-start.4 = (bf16[8,8,2048]{2,1,0:T(8,128)(2,1)}, bf16[8,8,2048]{2,1,0:T(8,128)(2,1)S(1)}, u32[]{:S(2)}) copy-start(bf16[8,8,2048]{2,1,0:T(8,128)(2,1)S(1)} %get-tuple-element.87) | copy-start | bytes 786436
  138.7 34.3 %collective-permute-start.10 = (bf16[8,8,2048]{2,1,0:T(8,128)(2,1)}, bf16[8,8,2048]{2,1,0:T(8,128)(2,1)S(1)}, u32[]{:S(2)}, u32[]{:S(2)}) collective-permute-start(bf16[8,8,2048]{2,1,0:T(8,128)(2,1)} %get-tuple-element.86), channel_id=1, source_target_pairs={{0,88},{8,80},{16,104},{24,96},{32,120},{40,112},{48,72},{56,64},{... | collective-permute-start | bytes 786440 | tf_op jit(solution)/shard_map/ppermute | solution.py:244
  145.6 27.4 %collective-permute-start.11 = (bf16[8,8,2048]{2,1,0:T(8,128)(2,1)}, bf16[8,8,2048]{2,1,0:T(8,128)(2,1)S(1)}, u32[]{:S(2)}, u32[]{:S(2)}) collective-permute-start(bf16[8,8,2048]{2,1,0:T(8,128)(2,1)} %copy-done.4), channel_id=1, source_target_pairs={{0,56},{8,48},{16,8},{24,0},{32,24},{40,16},{48,40},{56,32},{64,12... | collective-permute-start | bytes 786440 | tf_op jit(solution)/shard_map/ppermute | solution.py:244
  147.9 25.1 %collective-permute-start.12 = (bf16[8,8,2048]{2,1,0:T(8,128)(2,1)}, bf16[8,8,2048]{2,1,0:T(8,128)(2,1)S(1)}, u32[]{:S(2)}, u32[]{:S(2)}) collective-permute-start(bf16[8,8,2048]{2,1,0:T(8,128)(2,1)} %copy-done.3), channel_id=1, source_target_pairs={{0,96},{8,104},{16,112},{24,120},{32,64},{40,72},{48,80},{56,88},{... | collective-permute-start | bytes 786440 | tf_op jit(solution)/shard_map/ppermute | solution.py:244
  148.4 24.6 %collective-permute-start.13 = (bf16[8,8,2048]{2,1,0:T(8,128)(2,1)}, bf16[8,8,2048]{2,1,0:T(8,128)(2,1)S(1)}, u32[]{:S(2)}, u32[]{:S(2)}) collective-permute-start(bf16[8,8,2048]{2,1,0:T(8,128)(2,1)} %copy-done.2), channel_id=1, source_target_pairs={{0,8},{8,0},{16,24},{24,16},{32,40},{40,32},{48,56},{56,48},{64,72... | collective-permute-start | bytes 786440 | tf_op jit(solution)/shard_map/ppermute | solution.py:244
  148.4 24.6 %collective-permute-start.14 = (bf16[8,8,2048]{2,1,0:T(8,128)(2,1)}, bf16[8,8,2048]{2,1,0:T(8,128)(2,1)S(1)}, u32[]{:S(2)}, u32[]{:S(2)}) collective-permute-start(bf16[8,8,2048]{2,1,0:T(8,128)(2,1)} %copy-done.1), channel_id=1, source_target_pairs={{0,104},{8,96},{16,120},{24,112},{32,72},{40,64},{48,88},{56,80},{... | collective-permute-start | bytes 786440 | tf_op jit(solution)/shard_map/ppermute | solution.py:244

commit v4 on v3

--- a/solution.py
+++ b/solution.py
@@ -43,16 +43,11 @@
 
 def attend_kernel(
     lengths_ref, terms_ref, scale_ref, cache_ref, out_ref,
-    query_ref, held_ref, score_ref, weight_ref, sums_ref, sems,
+    query_ref, score_ref, weight_ref, sums_ref,
 ):
     copies, rows, query_cols = out_ref.shape
     length, head_dim = cache_ref.shape[1], cache_ref.shape[2] // 2
     heads = query_cols // head_dim
-    reads = [
-        pltpu.make_async_copy(cache_ref.at[r], held_ref.at[r], sems.at[r]) for r in range(rows)
-    ]
-    for read in reads:
-        read.start()
     total = terms_ref[0].astype(jnp.float32)
     for s in range(1, terms_ref.shape[0]):
         total = total + terms_ref[s].astype(jnp.float32)
@@ -64,10 +59,9 @@
     position = lax.broadcasted_iota(jnp.int32, (heads, length), 1)
     score_scale = head_dim ** (-0.5)
     for r in range(rows):
-        reads[r].wait()
         scores = lax.dot_general(
             query_ref[r].astype(jnp.bfloat16),
-            held_ref[r, :, :head_dim],
+            cache_ref[r, :, :head_dim],
             (((1,), (1,)), ((), ())),
             preferred_element_type=jnp.float32,
         )
@@ -83,7 +77,7 @@
     sums_ref[...] = self_weight * new_value[:, None, :]
     for r in range(rows):
         sums_ref[r] += jnp.dot(
-            weight_ref[r], held_ref[r, :, head_dim:], preferred_element_type=jnp.float32
+            weight_ref[r], cache_ref[r, :, head_dim:], preferred_element_type=jnp.float32
         )
     for h in range(heads):
         head = sums_ref[:, h, :].astype(out_ref.dtype)
@@ -100,67 +94,44 @@
     return pl.pallas_call(
         attend_kernel,
         out_shape=jax.ShapeDtypeStruct((copies, rows, query_cols), jnp.bfloat16),
-        in_specs=[SMEM, VMEM, VMEM, HBM],
+        in_specs=[SMEM, VMEM, VMEM, VMEM],
         out_specs=VMEM,
         scratch_shapes=[
             pltpu.VMEM((rows, heads, head_dim), jnp.float32),
-            pltpu.VMEM(cache.shape, cache.dtype),
             pltpu.VMEM((rows, heads, length), jnp.float32),
             pltpu.VMEM((rows, heads, length), jnp.bfloat16),
             pltpu.VMEM((rows, heads, head_dim), jnp.float32),
-            pltpu.SemaphoreType.DMA((rows,)),
         ],
-        compiler_params=pltpu.CompilerParams(vmem_limit_bytes=60 << 20),
+        compiler_params=pltpu.CompilerParams(vmem_limit_bytes=16 << 20),
         cost_estimate=cost(4 * cache.size * heads, 2 * cache.size),
         name="attend",
     )(lengths, terms, row_scale, cache)
 
 
-def output_kernel(heads_ref, weight_ref, out_ref, held_ref, total_ref, sems):
+def output_kernel(heads_ref, weight_ref, out_ref):
     parts, chunks, rows, chunk = out_ref.shape
-    count, depth, cols = held_ref.shape
-    reads = [
-        pltpu.make_async_copy(
-            weight_ref.at[pl.ds(k * depth, depth)], held_ref.at[k], sems.at[k]
+    step = 2 * chunk
+    for j in range(chunks // 2):
+        product = jnp.dot(
+            heads_ref[...],
+            weight_ref[:, j * step : (j + 1) * step],
+            preferred_element_type=jnp.float32,
         )
-        for k in range(count)
-    ]
-    for read in reads:
-        read.start()
-    step = 2 * chunk
-    for k, read in enumerate(reads):
-        read.wait()
-        heads = heads_ref[:, k * depth : (k + 1) * depth]
-        for j in range(0, cols, step):
-            product = jnp.dot(
-                heads, held_ref[k, :, j : j + step], preferred_element_type=jnp.float32
-            )
-            if k:
-                product = total_ref[:, j : j + step] + product
-            if k < count - 1:
-                total_ref[:, j : j + step] = product
-                continue
-            for i in range(2):
-                tile = product[:, i * chunk : (i + 1) * chunk].reshape(parts, rows, chunk)
-                out_ref[:, j // chunk + i] = tile.astype(out_ref.dtype)
+        for k in range(2):
+            tile = product[:, k * chunk : (k + 1) * chunk].reshape(parts, rows, chunk)
+            out_ref[:, 2 * j + k] = tile.astype(out_ref.dtype)
 
 
 def project_out(heads, weight, parts, chunks):
     rows, cols = heads.shape[0], weight.shape[1]
-    steps = 4
     return pl.pallas_call(
         output_kernel,
         out_shape=jax.ShapeDtypeStruct(
             (parts, chunks, rows // parts, cols // chunks), jnp.bfloat16
         ),
-        in_specs=[VMEM, HBM],
-        out_specs=VMEM,
-        scratch_shapes=[
-            pltpu.VMEM((steps, weight.shape[0] // steps, cols), weight.dtype),
-            pltpu.VMEM((rows, cols), jnp.float32),
-            pltpu.SemaphoreType.DMA((steps,)),
-        ],
-        compiler_params=pltpu.CompilerParams(vmem_limit_bytes=60 << 20),
+        in_specs=[VMEM, VMEM],
+        out_specs=VMEM,
+        compiler_params=pltpu.CompilerParams(vmem_limit_bytes=16 << 20),
         cost_estimate=cost(2 * rows * weight.size, 2 * weight.size),
         name="project_out",
     )(heads, weight)
@@ -389,9 +360,10 @@
     summed, placed = barrier((summed, placed))
     summed = start_round(3, summed)
     chunks = exchange(summed, "tensor")
+    placed = place_parts(owners[EARLY:], landed[EARLY:], dp, placed)
+    chunks, placed = barrier((chunks, placed))
     mixed = mix(hidden, chunks)
 
-    placed = place_parts(owners[EARLY:], landed[EARLY:], dp, placed)
     next_weight = placed.reshape(group * block_rows, tile_cols)
     return (mixed, next_weight)
 

time: 176 us -> 174 us (0.989)
  blocking collectives: 31.5 us -> 12.5 us
  waiting for transfers between devices: 50.5 us -> 66 us
  Pallas kernels: 27.2 us -> 22.1 us
  local copies, waits for them, and re-layouts: 1.29 us -> 5.78 us
    all_to_all x2 -> x1, blocking collectives: 31.5 us -> 12.5 us  [exchange(): return lax.all_to_all(x, axes, split_axis=0, concat_axis=0, tiled=True)]
    ppermute x15, waiting for transfers between devices: 0.95 us -> 13.1 us  [send(): lax.ppermute(part, 'dp', [(s, shifted(s, step, 1)) for s in range(16)])]
    unnamed x12 -> x20, local copies, waits for them, and re-layouts: 0.03 us -> 5.1 us
    all_to_all x4 -> x5, waiting for transfers between devices: 49.5 us -> 52.9 us  [exchange(): return lax.all_to_all(x, axes, split_axis=0, concat_axis=0, tiled=True)]
    all_to_all x4 -> x5, starting transfers between devices: 31 us -> 33.9 us  [exchange(): return lax.all_to_all(x, axes, split_axis=0, concat_axis=0, tiled=True)]
    pallas_call x1, Pallas kernels: 4.27 us -> 1.42 us  [project_out(): pl.pallas_call(output_kernel, out_shape=jax.ShapeDtypeStruct((parts, chun...]
    pallas_call x1, Pallas kernels: 5.06 us -> 2.54 us  [attend(): pl.pallas_call(attend_kernel, out_shape=jax.ShapeDtypeStruct((copies, row...]
  transfers between devices with their start and end apart: 19 -> 20, of which waited for: 5 -> 9; matrix products, arithmetic and copies ran while one was open for 4% -> 4% of each run, Pallas kernels for 13% -> 11%
where the time goes in v4:
time: 174 us; the launch traced here: 172 us
  waiting for transfers between devices  66 us (38%)
  starting transfers between devices  59.4 us (34%)
  Pallas kernels  22.1 us (13%)
  blocking collectives  12.5 us (7%)
  local copies, waits for them, and re-layouts  5.78 us (3%)
  matrix products  3.14 us (2%)
  other arithmetic  2.41 us (1%)
    all_to_all x5, waiting for transfers between devices, exchange(): return lax.all_to_all(x, axes, split_axis=0, concat_axis=0, tiled=True)  52.9 us
    all_to_all x5, starting transfers between devices, exchange(): return lax.all_to_all(x, axes, split_axis=0, concat_axis=0, tiled=True)  33.9 us
    ppermute x15, starting transfers between devices, send(): lax.ppermute(part, 'dp', [(s, shifted(s, step, 1)) for s in range(16)])  25.5 us
    ppermute x15, waiting for transfers between devices, send(): lax.ppermute(part, 'dp', [(s, shifted(s, step, 1)) for s in range(16)])  13.1 us
    all_to_all x1, blocking collectives, exchange(): return lax.all_to_all(x, axes, split_axis=0, concat_axis=0, tiled=True)  12.5 us
    pallas_call x4, Pallas kernels, pick_slabs(): pl.pallas_call(pick_kernel, out_shape=[jax.ShapeDtypeStruct(shape, slabs....  8.97 us
    unnamed x20, local copies, waits for them, and re-layouts  5.1 us
    pallas_call x2, Pallas kernels, place_parts(): pl.pallas_call(place_kernel, out_shape=jax.ShapeDtypeStruct((group, count...  3.89 us
  transfers between devices with their start and end apart: 20, of which 9 were waited for; matrix products, arithmetic and copies ran while one was open for 4% of the time, Pallas kernels for 11%

profile of v4, /device:TPU:3, one launch (start us, length us, event | category | flops | bytes accessed | tf_op | source)
XLA Modules:
  0.0 172.4 jit_solution(3503275979026963356)
XLA Ops:
  0.6 1.8 %prepare.1 = bf16[16,8,1152]{2,1,0:T(8,128)(2,1)} custom-call(s32[8]{0:T(128)} %ids_ref.1, bf16[8,16384]{1,0:T(8,128)(2,1)} %hidden_ref.3), custom_call_target="tpu_custom_call" | custom-call | bytes 524288 | tf_op jit(solution)/shard_map/prepare/pallas_call | solution.py:34
  2.4 12.5 %all_to_all.30 = bf16[16,8,1152]{2,1,0:T(8,128)(2,1)S(1)} all-to-all(bf16[16,8,1152]{2,1,0:T(8,128)(2,1)} %prepare.1), channel_id=1, replica_groups=mesh['dp'=16,'tensor'=8] {'dp'}, dimensions={0} | all-to-all | bytes 589824 | tf_op jit(solution)/shard_map/all_to_all | solution.py:263
  14.9 10.0 %all-to-all-start.1 = ((bf16[128,8,2048]{2,1,0:T(8,128)(2,1)}), bf16[128,8,2048]{2,1,0:T(8,128)(2,1)}, u32[]{:S(2)}, u32[]{:S(2)}) async-start(bf16[128,8,2048]{2,1,0:T(8,128)(2,1)} %bitcast.60), calls=%async_computation.1 | async-start | bytes 8388608 | tf_op jit(solution)/shard_map/all_to_all | solution.py:263
  25.5 0.7 dynamic-slice_convert_fusion
  26.2 0.2 multiply_reduce_fusion
  26.5 0.4 convert_reduce_fusion
  27.1 0.2 convolution_convert_fusion.1
  27.4 2.9 %convolution_convert_fusion = bf16[128,2048]{1,0:T(8,128)(2,1)S(1)} fusion(bf16[1024,2048]{1,0:T(8,128)(2,1)} %param.11, f32[1024]{0:T(1024)S(1)} %dynamic-slice_convert_fusion, bf16[16,8,1152]{2,1,0:T(8,128)(2,1)S(1)} %all_to_all.30), kind=kOutput, calls=%fused_computation | convolution fusion | flops 537526272 | bytes 4984832 | tf_op jit(solution)/shard_map/dot_general | solution.py:304
  30.3 0.9 pad_maximum_fusion
  31.1 45.3 %all-to-all-done.1.src_ref = bf16[128,8,2048]{2,1,0:T(8,128)(2,1)} async-done(((bf16[128,8,2048]{2,1,0:T(8,128)(2,1)}), bf16[128,8,2048]{2,1,0:T(8,128)(2,1)}, u32[]{:S(2)}, u32[]{:S(2)}) %all-to-all-start.1) | async-done | bytes 4194336 | tf_op jit(solution)/shard_map/all_to_all | solution.py:263
  76.4 4.5 %all-to-all-start.2 = ((bf16[16,8,2304]{2,1,0:T(8,128)(2,1)}), bf16[16,8,2304]{2,1,0:T(8,128)(2,1)S(1)}, u32[]{:S(2)}, u32[]{:S(2)}) async-start(bf16[16,8,2304]{2,1,0:T(8,128)(2,1)} %bitcast.35), calls=%async_computation.2 | async-start | bytes 1179648 | tf_op jit(solution)/shard_map/all_to_all | solution.py:263
  81.0 1.7 pick_slabs.4
  82.6 1.3 collective-permute-start
  83.9 1.7 collective-permute-start.1
  85.7 2.8 %pick_slabs.5 = (bf16[8,8,2048]{2,1,0:T(8,128)(2,1)}, bf16[8,8,2048]{2,1,0:T(8,128)(2,1)}, bf16[8,8,2048]{2,1,0:T(8,128)(2,1)S(1)}, bf16[8,8,2048]{2,1,0:T(8,128)(2,1)}, bf16[8,8,2048]{2,1,0:T(8,128)(2,1)}) custom-call(s32[40]{0:T(128)S(1)} %slice.27.table_ref, bf16[128,8,2048]{2,1,0:T(8,128)(2,1)} %all-to-all-done.1.src_ref), custom_call_target="tpu_custom_call" | custom-call | bytes 2621440 | tf_op jit(solution)/shard_map/pick_slabs/pallas_call | solution.py:155
  88.6 1.8 %all-to-all-done.2.terms_ref = bf16[16,8,2304]{2,1,0:T(8,128)(2,1)S(1)} async-done(((bf16[16,8,2304]{2,1,0:T(8,128)(2,1)}), bf16[16,8,2304]{2,1,0:T(8,128)(2,1)S(1)}, u32[]{:S(2)}, u32[]{:S(2)}) %all-to-all-start.2) | async-done | bytes 589856 | tf_op jit(solution)/shard_map/all_to_all | solution.py:263
  90.4 2.2 %copy-done.1 = bf16[8,1,1024,256]{3,2,1,0:T(8,128)(2,1)S(1)} copy-done((bf16[8,1,1024,256]{3,2,1,0:T(8,128)(2,1)S(1)}, bf16[8,1,1024,256]{3,2,1,0:T(8,128)(2,1)}, u32[]{:S(2)}) %copy-start.1) | copy-done | bytes 4194328
  92.6 2.5 %attend.1 = bf16[16,8,2048]{2,1,0:T(8,128)(2,1)} custom-call(s32[8]{0:T(128)S(1)} %copy-done.3, bf16[16,8,2304]{2,1,0:T(8,128)(2,1)S(1)} %all-to-all-done.2.terms_ref, f32[8,1]{1,0:T(8,128)S(1)} %copy.14.scale_ref, bf16[8,1024,256]{2,1,0:T(8,128)(2,1)S(1)} %bitcast.56), custom_call_target="tpu_custom_call" | custom-call | flops 134217728 | bytes 4194304 | tf_op jit(solution)/shard_map/attend/pallas_call | solution.py:94
  95.1 1.0 collective-permute-done.1.refs_2_
  96.1 8.4 %all-to-all-start.3 = ((bf16[16,8,2048]{2,1,0:T(8,128)(2,1)}), bf16[16,8,2048]{2,1,0:T(8,128)(2,1)S(1)}, u32[]{:S(2)}, u32[]{:S(2)}) async-start(bf16[16,8,2048]{2,1,0:T(8,128)(2,1)} %attend.1), calls=%async_computation.3 | async-start | bytes 1048576 | tf_op jit(solution)/shard_map/all_to_all | solution.py:263
  104.5 1.8 %collective-permute-start.2 = (bf16[8,8,2048]{2,1,0:T(8,128)(2,1)}, bf16[8,8,2048]{2,1,0:T(8,128)(2,1)S(1)}, u32[]{:S(2)}, u32[]{:S(2)}) collective-permute-start(bf16[8,8,2048]{2,1,0:T(8,128)(2,1)} %get-tuple-element.74), channel_id=1, source_target_pairs={{0,32},{8,40},{16,48},{24,56},{32,0},{40,8},{48,16},{56,24},{64,96... | collective-permute-start | bytes 786440 | tf_op jit(solution)/shard_map/ppermute | solution.py:215
  106.3 1.2 collective-permute-start.3
  107.6 2.8 %pick_slabs.6 = (bf16[8,8,2048]{2,1,0:T(8,128)(2,1)}, bf16[8,8,2048]{2,1,0:T(8,128)(2,1)}, bf16[8,8,2048]{2,1,0:T(8,128)(2,1)}, bf16[8,8,2048]{2,1,0:T(8,128)(2,1)}) custom-call(s32[32]{0:T(128)S(1)} %get-tuple-element.99.table_ref, bf16[128,8,2048]{2,1,0:T(8,128)(2,1)} %all-to-all-done.1.src_ref), custom_call_target="tpu_custom_call" | custom-call | bytes 2097152 | tf_op jit(solution)/shard_map/pick_slabs/pallas_call | solution.py:155
  110.4 1.5 collective-permute-start.5
  111.9 2.7 %collective-permute-start.6 = (bf16[8,8,2048]{2,1,0:T(8,128)(2,1)}, bf16[8,8,2048]{2,1,0:T(8,128)(2,1)S(1)}, u32[]{:S(2)}, u32[]{:S(2)}) collective-permute-start(bf16[8,8,2048]{2,1,0:T(8,128)(2,1)} %get-tuple-element.78), channel_id=1, source_target_pairs={{0,40},{8,32},{16,56},{24,48},{32,8},{40,0},{48,24},{56,16},{64,10... | collective-permute-start | bytes 786440 | tf_op jit(solution)/shard_map/ppermute | solution.py:215
  114.6 2.2 %copy-done.2 = bf16[2048,1024]{1,0:T(8,128)(2,1)S(1)} copy-done((bf16[2048,1024]{1,0:T(8,128)(2,1)S(1)}, bf16[2048,1024]{1,0:T(8,128)(2,1)}, u32[]{:S(2)}) %copy-start.2) | copy-done | bytes 4194328
  116.8 1.4 project_out.1
  118.2 0.4 collective-permute-done.2.refs_3_
  118.5 2.4 %collective-permute-start.7 = (bf16[8,8,2048]{2,1,0:T(8,128)(2,1)}, bf16[8,8,2048]{2,1,0:T(8,128)(2,1)S(1)}, u32[]{:S(2)}, u32[]{:S(2)}) collective-permute-start(bf16[8,8,2048]{2,1,0:T(8,128)(2,1)} %get-tuple-element.85), channel_id=1, source_target_pairs={{0,72},{8,64},{16,88},{24,80},{32,104},{40,96},{48,120},{56,112},{... | collective-permute-start | bytes 786440 | tf_op jit(solution)/shard_map/ppermute | solution.py:215
  121.0 1.5 collective-permute-start.8
  122.5 1.1 collective-permute-done.4.refs_5_
  123.5 2.5 %collective-permute-start.9 = (bf16[8,8,2048]{2,1,0:T(8,128)(2,1)}, bf16[8,8,2048]{2,1,0:T(8,128)(2,1)S(1)}, u32[]{:S(2)}, u32[]{:S(2)}) collective-permute-start(bf16[8,8,2048]{2,1,0:T(8,128)(2,1)} %get-tuple-element.87), channel_id=1, source_target_pairs={{0,112},{8,120},{16,64},{24,72},{32,80},{40,88},{48,96},{56,104},{... | collective-permute-start | bytes 786440 | tf_op jit(solution)/shard_map/ppermute | solution.py:215
  126.1 7.5 %all-to-all-start.4 = ((bf16[128,8,128]{2,1,0:T(8,128)(2,1)}), bf16[128,8,128]{2,1,0:T(8,128)(2,1)}, u32[]{:S(2)}, u32[]{:S(2)}) async-start(bf16[128,8,128]{2,1,0:T(8,128)(2,1)} %bitcast.38), calls=%async_computation.4 | async-start | bytes 524288 | tf_op jit(solution)/shard_map/all_to_all | solution.py:263
  133.6 1.7 %pick_slabs.7 = (bf16[8,8,2048]{2,1,0:T(8,128)(2,1)S(1)}, bf16[8,8,2048]{2,1,0:T(8,128)(2,1)S(1)}, bf16[8,8,2048]{2,1,0:T(8,128)(2,1)S(1)}, bf16[8,8,2048]{2,1,0:T(8,128)(2,1)S(1)}) custom-call(s32[32]{0:T(128)S(1)} %get-tuple-element.98.table_ref, bf16[128,8,2048]{2,1,0:T(8,128)(2,1)} %all-to-all-done.1.src_ref), custom_call_target="tpu_custom_call" | custom-call | bytes 2097152 | tf_op jit(solution)/shard_map/pick_slabs/pallas_call | solution.py:155
  135.5 2.0 %place_parts.2.refs_8_ = bf16[8,16,8,2048]{3,2,1,0:T(8,128)(2,1)} custom-call(s32[8]{0:T(128)S(1)} %get-tuple-element.97.owner_ref, bf16[8,8,2048]{2,1,0:T(8,128)(2,1)S(1)} %get-tuple-element.71.refs_0_, bf16[8,8,2048]{2,1,0:T(8,128)(2,1)S(1)} %collective-permute-done.refs_1_, bf16[8,8,2048]{2,1,0:T(8,128)(2,1)S(1)} %collective-permute-done.1.refs_2_, ...), custom_call_target="tpu_custom_call" | custom-call | bytes 4194304 | tf_op jit(solution)/shard_map/place_parts/pallas_call | solution.py:183
  137.5 2.4 %collective-permute-start.10 = (bf16[8,8,2048]{2,1,0:T(8,128)(2,1)}, bf16[8,8,2048]{2,1,0:T(8,128)(2,1)S(1)}, u32[]{:S(2)}, u32[]{:S(2)}) collective-permute-start(bf16[8,8,2048]{2,1,0:T(8,128)(2,1)} %get-tuple-element.88), channel_id=1, source_target_pairs={{0,88},{8,80},{16,104},{24,96},{32,120},{40,112},{48,72},{56,64},{... | collective-permute-start | bytes 786440 | tf_op jit(solution)/shard_map/ppermute | solution.py:215
  139.8 2.9 %all-to-all-done.4 = bf16[128,8,128]{2,1,0:T(8,128)(2,1)} async-done(((bf16[128,8,128]{2,1,0:T(8,128)(2,1)}), bf16[128,8,128]{2,1,0:T(8,128)(2,1)}, u32[]{:S(2)}, u32[]{:S(2)}) %all-to-all-start.4) | async-done | bytes 262176 | tf_op jit(solution)/shard_map/all_to_all | solution.py:263
  142.8 1.7 sum_over_tensor.1
  144.5 2.3 %collective-permute-start.11 = (bf16[8,8,2048]{2,1,0:T(8,128)(2,1)}, bf16[8,8,2048]{2,1,0:T(8,128)(2,1)S(1)}, u32[]{:S(2)}, u32[]{:S(2)}) collective-permute-start(bf16[8,8,2048]{2,1,0:T(8,128)(2,1)} %copy-done.7), channel_id=1, source_target_pairs={{0,56},{8,48},{16,8},{24,0},{32,24},{40,16},{48,40},{56,32},{64,12... | collective-permute-start | bytes 786440 | tf_op jit(solution)/shard_map/ppermute | solution.py:215
  146.7 0.5 collective-permute-start.12
  147.3 3.7 %collective-permute-start.14 = (bf16[8,8,2048]{2,1,0:T(8,128)(2,1)}, bf16[8,8,2048]{2,1,0:T(8,128)(2,1)S(1)}, u32[]{:S(2)}, u32[]{:S(2)}) collective-permute-start(bf16[8,8,2048]{2,1,0:T(8,128)(2,1)} %copy-done.4), channel_id=1, source_target_pairs={{0,104},{8,96},{16,120},{24,112},{32,72},{40,64},{48,88},{56,80},{... | collective-permute-start | bytes 786440 | tf_op jit(solution)/shard_map/ppermute | solution.py:215
  151.0 3.4 %all-to-all-start.5 = ((bf16[8,16,8,128]{3,2,1,0:T(8,128)(2,1)}), bf16[8,16,8,128]{3,2,1,0:T(8,128)(2,1)S(1)}, u32[]{:S(2)}, u32[]{:S(2)}) async-start(bf16[8,16,8,128]{3,2,1,0:T(8,128)(2,1)} %sum_over_tensor.1), calls=%async_computation.5 | async-start | bytes 524288 | tf_op jit(solution)/shard_map/all_to_all | solution.py:263
  154.5 5.5 %collective-permute-done.12.refs_5_ = bf16[8,8,2048]{2,1,0:T(8,128)(2,1)S(1)} collective-permute-done((bf16[8,8,2048]{2,1,0:T(8,128)(2,1)}, bf16[8,8,2048]{2,1,0:T(8,128)(2,1)S(1)}, u32[]{:S(2)}, u32[]{:S(2)}) %collective-permute-start.12) | collective-permute-done | bytes 262176 | tf_op jit(solution)/shard_map/ppermute | solution.py:215
  159.9 5.1 %collective-permute-done.14.refs_7_ = bf16[8,8,2048]{2,1,0:T(8,128)(2,1)S(1)} collective-permute-done((bf16[8,8,2048]{2,1,0:T(8,128)(2,1)}, bf16[8,8,2048]{2,1,0:T(8,128)(2,1)S(1)}, u32[]{:S(2)}, u32[]{:S(2)}) %collective-permute-start.14) | collective-permute-done | bytes 262176 | tf_op jit(solution)/shard_map/ppermute | solution.py:215
  165.1 1.9 %place_parts.3 = bf16[8,16,8,2048]{3,2,1,0:T(8,128)(2,1)} custom-call(s32[8]{0:T(128)S(1)} %get-tuple-element.96.owner_ref, bf16[8,8,2048]{2,1,0:T(8,128)(2,1)S(1)} %collective-permute-done.7.refs_0_, bf16[8,8,2048]{2,1,0:T(8,128)(2,1)S(1)} %collective-permute-done.8.refs_1_, ...), custom_call_target="tpu_custom_call", output_to_operand_aliasing={{}: (9, {})} | custom-call | bytes 4194304 | tf_op jit(solution)/shard_map/place_parts/pallas_call | solution.py:183
  167.0 2.9 %all-to-all-done.5.chunks_ref = bf16[8,16,8,128]{3,2,1,0:T(8,128)(2,1)S(1)} async-done(((bf16[8,16,8,128]{3,2,1,0:T(8,128)(2,1)}), bf16[8,16,8,128]{3,2,1,0:T(8,128)(2,1)S(1)}, u32[]{:S(2)}, u32[]{:S(2)}) %all-to-all-start.5) | async-done | bytes 262176 | tf_op jit(solution)/shard_map/all_to_all | solution.py:263
  169.9 0.7 copy-done.9
  170.6 1.8 %mix.1 = bf16[8,16384]{1,0:T(8,128)(2,1)} custom-call(bf16[8,16384]{1,0:T(8,128)(2,1)} %hidden_ref.3, bf16[8,16,8,128]{3,2,1,0:T(8,128)(2,1)} %copy-done.9), custom_call_target="tpu_custom_call" | custom-call | flops 131072 | bytes 786432 | tf_op jit(solution)/shard_map/mix/pallas_call | solution.py:252
  (42 shorter events, 1.0 us)
Async XLA Ops:
  0.6 26.5 %copy-start = (bf16[1024,1,256]{2,0,1:T(8,128)(2,1)S(1)}, bf16[1024,1,256]{2,0,1:T(8,128)(2,1)}, u32[]{:S(2)}) copy-start(bf16[1024,1,256]{2,0,1:T(8,128)(2,1)} %param.12) | copy-start | bytes 1572868
  14.9 11.4 %copy-start.8 = (bf16[8,16384]{1,0:T(8,128)(2,1)S(1)}, bf16[8,16384]{1,0:T(8,128)(2,1)}, u32[]{:S(2)}) copy-start(bf16[8,16384]{1,0:T(8,128)(2,1)} %hidden_ref.3) | copy-start | bytes 786436
  14.9 61.6 %all-to-all-start.1 = ((bf16[128,8,2048]{2,1,0:T(8,128)(2,1)}), bf16[128,8,2048]{2,1,0:T(8,128)(2,1)}, u32[]{:S(2)}, u32[]{:S(2)}) async-start(bf16[128,8,2048]{2,1,0:T(8,128)(2,1)} %bitcast.60), calls=%async_computation.1 | async-start | bytes 8388608 | tf_op jit(solution)/shard_map/all_to_all | solution.py:263
  76.4 14.0 %all-to-all-start.2 = ((bf16[16,8,2304]{2,1,0:T(8,128)(2,1)}), bf16[16,8,2304]{2,1,0:T(8,128)(2,1)S(1)}, u32[]{:S(2)}, u32[]{:S(2)}) async-start(bf16[16,8,2304]{2,1,0:T(8,128)(2,1)} %bitcast.35), calls=%async_computation.2 | async-start | bytes 1179648 | tf_op jit(solution)/shard_map/all_to_all | solution.py:263
  81.0 9.4 %copy-start.3 = (s32[8]{0:T(128)S(1)}, s32[8]{0:T(128)}, u32[]{:S(2)}) copy-start(s32[8]{0:T(128)} %lengths_ref.1) | copy-start | bytes 100
  82.6 12.5 %collective-permute-start = (bf16[8,8,2048]{2,1,0:T(8,128)(2,1)S(1)}, bf16[8,8,2048]{2,1,0:T(8,128)(2,1)S(1)}, u32[]{:S(2)}, u32[]{:S(2)}) collective-permute-start(bf16[8,8,2048]{2,1,0:T(8,128)(2,1)S(1)} %get-tuple-element.56), channel_id=1, source_target_pairs={{0,16},{8,24},{16,32},{24,40},{32,48},{40,56},{48,0},{56,8},{64,80... | collective-permute-start | bytes 786440 | tf_op jit(solution)/shard_map/ppermute | solution.py:215
  83.9 12.3 %collective-permute-start.1 = (bf16[8,8,2048]{2,1,0:T(8,128)(2,1)S(1)}, bf16[8,8,2048]{2,1,0:T(8,128)(2,1)S(1)}, u32[]{:S(2)}, u32[]{:S(2)}) collective-permute-start(bf16[8,8,2048]{2,1,0:T(8,128)(2,1)S(1)} %get-tuple-element.57), channel_id=1, source_target_pairs={{0,120},{8,112},{16,72},{24,64},{32,88},{40,80},{48,104},{56,96},{... | collective-permute-start | bytes 786440 | tf_op jit(solution)/shard_map/ppermute | solution.py:215
  90.4 2.2 %copy-start.1 = (bf16[8,1,1024,256]{3,2,1,0:T(8,128)(2,1)S(1)}, bf16[8,1,1024,256]{3,2,1,0:T(8,128)(2,1)}, u32[]{:S(2)}) copy-start(bf16[8,1,1024,256]{3,2,1,0:T(8,128)(2,1)} %param.14) | copy-start | bytes 12582916
  96.1 18.4 %all-to-all-start.3 = ((bf16[16,8,2048]{2,1,0:T(8,128)(2,1)}), bf16[16,8,2048]{2,1,0:T(8,128)(2,1)S(1)}, u32[]{:S(2)}, u32[]{:S(2)}) async-start(bf16[16,8,2048]{2,1,0:T(8,128)(2,1)} %attend.1), calls=%async_computation.3 | async-start | bytes 1048576 | tf_op jit(solution)/shard_map/all_to_all | solution.py:263
  104.5 14.0 %collective-permute-start.2 = (bf16[8,8,2048]{2,1,0:T(8,128)(2,1)}, bf16[8,8,2048]{2,1,0:T(8,128)(2,1)S(1)}, u32[]{:S(2)}, u32[]{:S(2)}) collective-permute-start(bf16[8,8,2048]{2,1,0:T(8,128)(2,1)} %get-tuple-element.74), channel_id=1, source_target_pairs={{0,32},{8,40},{16,48},{24,56},{32,0},{40,8},{48,16},{56,24},{64,96... | collective-permute-start | bytes 786440 | tf_op jit(solution)/shard_map/ppermute | solution.py:215
  106.3 14.6 %collective-permute-start.3 = (bf16[8,8,2048]{2,1,0:T(8,128)(2,1)}, bf16[8,8,2048]{2,1,0:T(8,128)(2,1)S(1)}, u32[]{:S(2)}, u32[]{:S(2)}) collective-permute-start(bf16[8,8,2048]{2,1,0:T(8,128)(2,1)} %get-tuple-element.75), channel_id=1, source_target_pairs={{0,64},{8,72},{16,80},{24,88},{32,96},{40,104},{48,112},{56,120},{... | collective-permute-start | bytes 786440 | tf_op jit(solution)/shard_map/ppermute | solution.py:215
  107.5 16.0 %collective-permute-start.4 = (bf16[8,8,2048]{2,1,0:T(8,128)(2,1)S(1)}, bf16[8,8,2048]{2,1,0:T(8,128)(2,1)S(1)}, u32[]{:S(2)}, u32[]{:S(2)}) collective-permute-start(bf16[8,8,2048]{2,1,0:T(8,128)(2,1)S(1)} %get-tuple-element.76), channel_id=1, source_target_pairs={{0,80},{8,88},{16,96},{24,104},{32,112},{40,120},{48,64},{56,72},{... | collective-permute-start | bytes 786440 | tf_op jit(solution)/shard_map/ppermute | solution.py:215
  110.4 25.1 %collective-permute-start.5 = (bf16[8,8,2048]{2,1,0:T(8,128)(2,1)}, bf16[8,8,2048]{2,1,0:T(8,128)(2,1)S(1)}, u32[]{:S(2)}, u32[]{:S(2)}) collective-permute-start(bf16[8,8,2048]{2,1,0:T(8,128)(2,1)} %get-tuple-element.77), channel_id=1, source_target_pairs={{0,48},{8,56},{16,0},{24,8},{32,16},{40,24},{48,32},{56,40},{64,11... | collective-permute-start | bytes 786440 | tf_op jit(solution)/shard_map/ppermute | solution.py:215
  111.9 23.6 %collective-permute-start.6 = (bf16[8,8,2048]{2,1,0:T(8,128)(2,1)}, bf16[8,8,2048]{2,1,0:T(8,128)(2,1)S(1)}, u32[]{:S(2)}, u32[]{:S(2)}) collective-permute-start(bf16[8,8,2048]{2,1,0:T(8,128)(2,1)} %get-tuple-element.78), channel_id=1, source_target_pairs={{0,40},{8,32},{16,56},{24,48},{32,8},{40,0},{48,24},{56,16},{64,10... | collective-permute-start | bytes 786440 | tf_op jit(solution)/shard_map/ppermute | solution.py:215
  114.6 2.2 %copy-start.2 = (bf16[2048,1024]{1,0:T(8,128)(2,1)S(1)}, bf16[2048,1024]{1,0:T(8,128)(2,1)}, u32[]{:S(2)}) copy-start(bf16[2048,1024]{1,0:T(8,128)(2,1)} %weight_ref.1) | copy-start | bytes 12582916
  118.5 28.2 %collective-permute-start.7 = (bf16[8,8,2048]{2,1,0:T(8,128)(2,1)}, bf16[8,8,2048]{2,1,0:T(8,128)(2,1)S(1)}, u32[]{:S(2)}, u32[]{:S(2)}) collective-permute-start(bf16[8,8,2048]{2,1,0:T(8,128)(2,1)} %get-tuple-element.85), channel_id=1, source_target_pairs={{0,72},{8,64},{16,88},{24,80},{32,104},{40,96},{48,120},{56,112},{... | collective-permute-start | bytes 786440 | tf_op jit(solution)/shard_map/ppermute | solution.py:215
  121.0 26.3 %collective-permute-start.8 = (bf16[8,8,2048]{2,1,0:T(8,128)(2,1)}, bf16[8,8,2048]{2,1,0:T(8,128)(2,1)S(1)}, u32[]{:S(2)}, u32[]{:S(2)}) collective-permute-start(bf16[8,8,2048]{2,1,0:T(8,128)(2,1)} %get-tuple-element.86), channel_id=1, source_target_pairs={{0,24},{8,16},{16,40},{24,32},{32,56},{40,48},{48,8},{56,0},{64,88... | collective-permute-start | bytes 786440 | tf_op jit(solution)/shard_map/ppermute | solution.py:215
  123.5 23.7 %collective-permute-start.9 = (bf16[8,8,2048]{2,1,0:T(8,128)(2,1)}, bf16[8,8,2048]{2,1,0:T(8,128)(2,1)S(1)}, u32[]{:S(2)}, u32[]{:S(2)}) collective-permute-start(bf16[8,8,2048]{2,1,0:T(8,128)(2,1)} %get-tuple-element.87), channel_id=1, source_target_pairs={{0,112},{8,120},{16,64},{24,72},{32,80},{40,88},{48,96},{56,104},{... | collective-permute-start | bytes 786440 | tf_op jit(solution)/shard_map/ppermute | solution.py:215
  126.1 16.7 %all-to-all-start.4 = ((bf16[128,8,128]{2,1,0:T(8,128)(2,1)}), bf16[128,8,128]{2,1,0:T(8,128)(2,1)}, u32[]{:S(2)}, u32[]{:S(2)}) async-start(bf16[128,8,128]{2,1,0:T(8,128)(2,1)} %bitcast.38), calls=%async_computation.4 | async-start | bytes 524288 | tf_op jit(solution)/shard_map/all_to_all | solution.py:263
  135.3 2.1 %copy-start.4 = (bf16[8,8,2048]{2,1,0:T(8,128)(2,1)}, bf16[8,8,2048]{2,1,0:T(8,128)(2,1)S(1)}, u32[]{:S(2)}) copy-start(bf16[8,8,2048]{2,1,0:T(8,128)(2,1)S(1)} %get-tuple-element.92) | copy-start | bytes 786436
  135.3 2.1 %copy-start.5 = (bf16[8,8,2048]{2,1,0:T(8,128)(2,1)}, bf16[8,8,2048]{2,1,0:T(8,128)(2,1)S(1)}, u32[]{:S(2)}) copy-start(bf16[8,8,2048]{2,1,0:T(8,128)(2,1)S(1)} %get-tuple-element.91) | copy-start | bytes 786436
  135.4 2.1 %copy-start.6 = (bf16[8,8,2048]{2,1,0:T(8,128)(2,1)}, bf16[8,8,2048]{2,1,0:T(8,128)(2,1)S(1)}, u32[]{:S(2)}) copy-start(bf16[8,8,2048]{2,1,0:T(8,128)(2,1)S(1)} %get-tuple-element.90) | copy-start | bytes 786436
  135.4 2.1 %copy-start.7 = (bf16[8,8,2048]{2,1,0:T(8,128)(2,1)}, bf16[8,8,2048]{2,1,0:T(8,128)(2,1)S(1)}, u32[]{:S(2)}) copy-start(bf16[8,8,2048]{2,1,0:T(8,128)(2,1)S(1)} %get-tuple-element.89) | copy-start | bytes 786436
  137.5 17.0 %collective-permute-start.10 = (bf16[8,8,2048]{2,1,0:T(8,128)(2,1)}, bf16[8,8,2048]{2,1,0:T(8,128)(2,1)S(1)}, u32[]{:S(2)}, u32[]{:S(2)}) collective-permute-start(bf16[8,8,2048]{2,1,0:T(8,128)(2,1)} %get-tuple-element.88), channel_id=1, source_target_pairs={{0,88},{8,80},{16,104},{24,96},{32,120},{40,112},{48,72},{56,64},{... | collective-permute-start | bytes 786440 | tf_op jit(solution)/shard_map/ppermute | solution.py:215
  144.5 10.0 %collective-permute-start.11 = (bf16[8,8,2048]{2,1,0:T(8,128)(2,1)}, bf16[8,8,2048]{2,1,0:T(8,128)(2,1)S(1)}, u32[]{:S(2)}, u32[]{:S(2)}) collective-permute-start(bf16[8,8,2048]{2,1,0:T(8,128)(2,1)} %copy-done.7), channel_id=1, source_target_pairs={{0,56},{8,48},{16,8},{24,0},{32,24},{40,16},{48,40},{56,32},{64,12... | collective-permute-start | bytes 786440 | tf_op jit(solution)/shard_map/ppermute | solution.py:215
  146.7 13.2 %collective-permute-start.12 = (bf16[8,8,2048]{2,1,0:T(8,128)(2,1)}, bf16[8,8,2048]{2,1,0:T(8,128)(2,1)S(1)}, u32[]{:S(2)}, u32[]{:S(2)}) collective-permute-start(bf16[8,8,2048]{2,1,0:T(8,128)(2,1)} %copy-done.6), channel_id=1, source_target_pairs={{0,96},{8,104},{16,112},{24,120},{32,64},{40,72},{48,80},{56,88},{... | collective-permute-start | bytes 786440 | tf_op jit(solution)/shard_map/ppermute | solution.py:215
  147.3 12.7 %collective-permute-start.13 = (bf16[8,8,2048]{2,1,0:T(8,128)(2,1)}, bf16[8,8,2048]{2,1,0:T(8,128)(2,1)S(1)}, u32[]{:S(2)}, u32[]{:S(2)}) collective-permute-start(bf16[8,8,2048]{2,1,0:T(8,128)(2,1)} %copy-done.5), channel_id=1, source_target_pairs={{0,8},{8,0},{16,24},{24,16},{32,40},{40,32},{48,56},{56,48},{64,72... | collective-permute-start | bytes 786440 | tf_op jit(solution)/shard_map/ppermute | solution.py:215
  147.3 17.8 %collective-permute-start.14 = (bf16[8,8,2048]{2,1,0:T(8,128)(2,1)}, bf16[8,8,2048]{2,1,0:T(8,128)(2,1)S(1)}, u32[]{:S(2)}, u32[]{:S(2)}) collective-permute-start(bf16[8,8,2048]{2,1,0:T(8,128)(2,1)} %copy-done.4), channel_id=1, source_target_pairs={{0,104},{8,96},{16,120},{24,112},{32,72},{40,64},{48,88},{56,80},{... | collective-permute-start | bytes 786440 | tf_op jit(solution)/shard_map/ppermute | solution.py:215
  151.0 18.9 %all-to-all-start.5 = ((bf16[8,16,8,128]{3,2,1,0:T(8,128)(2,1)}), bf16[8,16,8,128]{3,2,1,0:T(8,128)(2,1)S(1)}, u32[]{:S(2)}, u32[]{:S(2)}) async-start(bf16[8,16,8,128]{3,2,1,0:T(8,128)(2,1)} %sum_over_tensor.1), calls=%async_computation.5 | async-start | bytes 524288 | tf_op jit(solution)/shard_map/all_to_all | solution.py:263
  169.9 0.7 copy-start.9

commit v5 on v4

--- a/solution.py
+++ b/solution.py
@@ -197,13 +197,13 @@
 
 ROUNDS = (
     ((0, 1, 0), (1, 3, 1)),
-    ((0, 2, 0), (1, 0, 0), (1, 1, 0), (0, 3, 0), (0, 2, 1)),
+    ((0, 2, 0), (1, 0, 0), (0, 0, 1), (1, 1, 0), (0, 3, 0), (0, 2, 1)),
     ((1, 0, 1), (0, 1, 1), (1, 3, 0), (1, 1, 1)),
-    ((0, 3, 1), (1, 2, 0), (0, 0, 1), (1, 2, 1)),
+    ((0, 3, 1), (1, 2, 0), (1, 2, 1)),
 )
 STEPS = ((0, 0, 0),) + tuple(step for steps in ROUNDS for step in steps)
 FENCES = {'heads': 3}
-EARLY = 8
+EARLY = 9
 
 
 def shifted(index, step, sign):

time: 174 us -> 181 us (1.040); the launches traced: 172 us -> 177 us
  waiting for transfers between devices: 66 us -> 74 us
  starting transfers between devices: 59.4 us -> 55.8 us
    ppermute x15, waiting for transfers between devices: 13.1 us -> 19.3 us  [send(): lax.ppermute(part, 'dp', [(s, shifted(s, step, 1)) for s in range(16)])]
    ppermute x15, starting transfers between devices: 25.5 us -> 21.8 us  [send(): lax.ppermute(part, 'dp', [(s, shifted(s, step, 1)) for s in range(16)])]
    all_to_all x5, waiting for transfers between devices: 52.9 us -> 54.8 us  [exchange(): return lax.all_to_all(x, axes, split_axis=0, concat_axis=0, tiled=True)]
    unnamed x20 -> x18, local copies, waits for them, and re-layouts: 5.1 us -> 5.11 us
where the time goes in v5:
time: 181 us; the launch traced here: 177 us
  waiting for transfers between devices  74 us (41%)
  starting transfers between devices  55.8 us (31%)
  Pallas kernels  22.2 us (12%)
  blocking collectives  12.5 us (7%)
  local copies, waits for them, and re-layouts  5.85 us (3%)
  matrix products  3.14 us (2%)
  other arithmetic  2.4 us (1%)
    all_to_all x5, waiting for transfers between devices, exchange(): return lax.all_to_all(x, axes, split_axis=0, concat_axis=0, tiled=True)  54.8 us
    all_to_all x5, starting transfers between devices, exchange(): return lax.all_to_all(x, axes, split_axis=0, concat_axis=0, tiled=True)  34 us
    ppermute x15, starting transfers between devices, send(): lax.ppermute(part, 'dp', [(s, shifted(s, step, 1)) for s in range(16)])  21.8 us
    ppermute x15, waiting for transfers between devices, send(): lax.ppermute(part, 'dp', [(s, shifted(s, step, 1)) for s in range(16)])  19.3 us
    all_to_all x1, blocking collectives, exchange(): return lax.all_to_all(x, axes, split_axis=0, concat_axis=0, tiled=True)  12.5 us
    pallas_call x4, Pallas kernels, pick_slabs(): pl.pallas_call(pick_kernel, out_shape=[jax.ShapeDtypeStruct(shape, slabs....  9.04 us
    unnamed x18, local copies, waits for them, and re-layouts  5.11 us
    pallas_call x2, Pallas kernels, place_parts(): pl.pallas_call(place_kernel, out_shape=jax.ShapeDtypeStruct((group, count...  3.89 us
  transfers between devices with their start and end apart: 20, of which 9 were waited for; matrix products, arithmetic and copies ran while one was open for 4% of the time, Pallas kernels for 11%

profile of v5, /device:TPU:3, one launch (start us, length us, event | category | flops | bytes accessed | tf_op | source)
XLA Modules:
  0.0 177.0 jit_solution(17907168037150977741)
XLA Ops:
  0.6 1.8 prepare.1
  2.4 12.5 %all_to_all.30 = bf16[16,8,1152]{2,1,0:T(8,128)(2,1)S(1)} all-to-all(bf16[16,8,1152]{2,1,0:T(8,128)(2,1)} %prepare.1), channel_id=1, replica_groups=mesh['dp'=16,'tensor'=8] {'dp'}, dimensions={0} | all-to-all | bytes 589824 | tf_op jit(solution)/shard_map/all_to_all | solution.py:263
  14.9 10.0 %all-to-all-start.1 = ((bf16[128,8,2048]{2,1,0:T(8,128)(2,1)}), bf16[128,8,2048]{2,1,0:T(8,128)(2,1)}, u32[]{:S(2)}, u32[]{:S(2)}) async-start(bf16[128,8,2048]{2,1,0:T(8,128)(2,1)} %bitcast.60), calls=%async_computation.1 | async-start | bytes 8388608 | tf_op jit(solution)/shard_map/all_to_all | solution.py:263
  25.5 0.7 dynamic-slice_convert_fusion
  26.2 0.2 multiply_reduce_fusion
  26.5 0.4 convert_reduce_fusion
  27.4 2.9 %convolution_convert_fusion = bf16[128,2048]{1,0:T(8,128)(2,1)S(1)} fusion(bf16[1024,2048]{1,0:T(8,128)(2,1)} %param.11, f32[1024]{0:T(1024)S(1)} %dynamic-slice_convert_fusion, bf16[16,8,1152]{2,1,0:T(8,128)(2,1)S(1)} %all_to_all.30), kind=kOutput, calls=%fused_computation | convolution fusion | flops 537526272 | bytes 4984832 | tf_op jit(solution)/shard_map/dot_general | solution.py:304
  30.3 0.9 pad_maximum_fusion
  31.1 45.3 %all-to-all-done.1.src_ref = bf16[128,8,2048]{2,1,0:T(8,128)(2,1)} async-done(((bf16[128,8,2048]{2,1,0:T(8,128)(2,1)}), bf16[128,8,2048]{2,1,0:T(8,128)(2,1)}, u32[]{:S(2)}, u32[]{:S(2)}) %all-to-all-start.1) | async-done | bytes 4194336 | tf_op jit(solution)/shard_map/all_to_all | solution.py:263
  76.4 4.5 %all-to-all-start.2 = ((bf16[16,8,2304]{2,1,0:T(8,128)(2,1)}), bf16[16,8,2304]{2,1,0:T(8,128)(2,1)S(1)}, u32[]{:S(2)}, u32[]{:S(2)}) async-start(bf16[16,8,2304]{2,1,0:T(8,128)(2,1)} %bitcast.35), calls=%async_computation.2 | async-start | bytes 1179648 | tf_op jit(solution)/shard_map/all_to_all | solution.py:263
  81.0 1.7 pick_slabs.4
  82.7 1.3 collective-permute-start
  83.9 1.7 collective-permute-start.1
  85.8 3.0 %pick_slabs.5 = (bf16[8,8,2048]{2,1,0:T(8,128)(2,1)S(1)}, bf16[8,8,2048]{2,1,0:T(8,128)(2,1)}, bf16[8,8,2048]{2,1,0:T(8,128)(2,1)}, bf16[8,8,2048]{2,1,0:T(8,128...) custom-call(s32[48]{0:T(128)S(1)} %slice.27.table_ref, bf16[128,8,2048]{2,1,0:T(8,128)(2,1)} %all-to-all-done.1.src_ref), custom_call_target="tpu_custom_call" | custom-call | bytes 3145728 | tf_op jit(solution)/shard_map/pick_slabs/pallas_call | solution.py:155
  88.8 1.6 all-to-all-done.2.terms_ref
  90.4 2.2 %copy-done.1 = bf16[8,1,1024,256]{3,2,1,0:T(8,128)(2,1)S(1)} copy-done((bf16[8,1,1024,256]{3,2,1,0:T(8,128)(2,1)S(1)}, bf16[8,1,1024,256]{3,2,1,0:T(8,128)(2,1)}, u32[]{:S(2)}) %copy-start.1) | copy-done | bytes 4194328
  92.6 2.6 %attend.1 = bf16[16,8,2048]{2,1,0:T(8,128)(2,1)} custom-call(s32[8]{0:T(128)S(1)} %copy-done.3, bf16[16,8,2304]{2,1,0:T(8,128)(2,1)S(1)} %all-to-all-done.2.terms_ref, f32[8,1]{1,0:T(8,128)S(1)} %copy.14.scale_ref, bf16[8,1024,256]{2,1,0:T(8,128)(2,1)S(1)} %bitcast.56), custom_call_target="tpu_custom_call" | custom-call | flops 134217728 | bytes 4194304 | tf_op jit(solution)/shard_map/attend/pallas_call | solution.py:94
  95.1 1.0 collective-permute-done.1.refs_2_
  96.1 8.4 %all-to-all-start.3 = ((bf16[16,8,2048]{2,1,0:T(8,128)(2,1)}), bf16[16,8,2048]{2,1,0:T(8,128)(2,1)S(1)}, u32[]{:S(2)}, u32[]{:S(2)}) async-start(bf16[16,8,2048]{2,1,0:T(8,128)(2,1)} %attend.1), calls=%async_computation.3 | async-start | bytes 1048576 | tf_op jit(solution)/shard_map/all_to_all | solution.py:263
  104.6 1.8 %collective-permute-start.2 = (bf16[8,8,2048]{2,1,0:T(8,128)(2,1)S(1)}, bf16[8,8,2048]{2,1,0:T(8,128)(2,1)S(1)}, u32[]{:S(2)}, u32[]{:S(2)}) collective-permute-start(bf16[8,8,2048]{2,1,0:T(8,128)(2,1)S(1)} %get-tuple-element.75), channel_id=1, source_target_pairs={{0,32},{8,40},{16,48},{24,56},{32,0},{40,8},{48,16},{56,24},{64,96... | collective-permute-start | bytes 786440 | tf_op jit(solution)/shard_map/ppermute | solution.py:215
  106.4 1.2 collective-permute-start.3
  107.5 0.9 collective-permute-start.4
  108.5 2.7 %pick_slabs.6 = (bf16[8,8,2048]{2,1,0:T(8,128)(2,1)}, bf16[8,8,2048]{2,1,0:T(8,128)(2,1)}, bf16[8,8,2048]{2,1,0:T(8,128)(2,1)}, bf16[8,8,2048]{2,1,0:T(8,128)(2,1)}) custom-call(s32[32]{0:T(128)S(1)} %slice.28.table_ref, bf16[128,8,2048]{2,1,0:T(8,128)(2,1)} %all-to-all-done.1.src_ref), custom_call_target="tpu_custom_call" | custom-call | bytes 2097152 | tf_op jit(solution)/shard_map/pick_slabs/pallas_call | solution.py:155
  111.4 1.4 collective-permute-start.6
  112.8 5.7 %collective-permute-done.2.refs_3_ = bf16[8,8,2048]{2,1,0:T(8,128)(2,1)S(1)} collective-permute-done((bf16[8,8,2048]{2,1,0:T(8,128)(2,1)S(1)}, bf16[8,8,2048]{2,1,0:T(8,128)(2,1)S(1)}, u32[]{:S(2)}, u32[]{:S(2)}) %collective-permute-start.2) | collective-permute-done | bytes 262176 | tf_op jit(solution)/shard_map/ppermute | solution.py:215
  118.6 2.4 %collective-permute-start.7 = (bf16[8,8,2048]{2,1,0:T(8,128)(2,1)}, bf16[8,8,2048]{2,1,0:T(8,128)(2,1)S(1)}, u32[]{:S(2)}, u32[]{:S(2)}) collective-permute-start(bf16[8,8,2048]{2,1,0:T(8,128)(2,1)} %get-tuple-element.80), channel_id=1, source_target_pairs={{0,40},{8,32},{16,56},{24,48},{32,8},{40,0},{48,24},{56,16},{64,10... | collective-permute-start | bytes 786440 | tf_op jit(solution)/shard_map/ppermute | solution.py:215
  121.0 2.2 %copy-done.2 = bf16[2048,1024]{1,0:T(8,128)(2,1)S(1)} copy-done((bf16[2048,1024]{1,0:T(8,128)(2,1)S(1)}, bf16[2048,1024]{1,0:T(8,128)(2,1)}, u32[]{:S(2)}) %copy-start.2) | copy-done | bytes 4194328
  123.2 1.4 project_out.1
  124.6 0.2 collective-permute-start.8
  124.8 2.4 %collective-permute-start.9 = (bf16[8,8,2048]{2,1,0:T(8,128)(2,1)}, bf16[8,8,2048]{2,1,0:T(8,128)(2,1)S(1)}, u32[]{:S(2)}, u32[]{:S(2)}) collective-permute-start(bf16[8,8,2048]{2,1,0:T(8,128)(2,1)} %get-tuple-element.87), channel_id=1, source_target_pairs={{0,24},{8,16},{16,40},{24,32},{32,56},{40,48},{48,8},{56,0},{64,88... | collective-permute-start | bytes 786440 | tf_op jit(solution)/shard_map/ppermute | solution.py:215
  127.2 7.0 %all-to-all-start.4 = ((bf16[128,8,128]{2,1,0:T(8,128)(2,1)}), bf16[128,8,128]{2,1,0:T(8,128)(2,1)}, u32[]{:S(2)}, u32[]{:S(2)}) async-start(bf16[128,8,128]{2,1,0:T(8,128)(2,1)} %bitcast.38), calls=%async_computation.4 | async-start | bytes 524288 | tf_op jit(solution)/shard_map/all_to_all | solution.py:263
  134.2 1.7 pick_slabs.7
  135.9 2.1 %place_parts.2.refs_7_ = bf16[8,16,8,2048]{3,2,1,0:T(8,128)(2,1)} custom-call(s32[9]{0:T(128)S(1)} %bitcast.58, bf16[8,8,2048]{2,1,0:T(8,128)(2,1)S(1)} %get-tuple-element.72.refs_0_, bf16[8,8,2048]{2,1,0:T(8,128)(2,1)S(1)} %collective-permute-done.refs_1_, bf16[8,8,2048]{2,1,0:T(8,128)(2,1)S(1)} %collective-permute-done.1.refs_2_, ...), custom_call_target="tpu_custom_call" | custom-call | bytes 4718592 | tf_op jit(solution)/shard_map/place_parts/pallas_call | solution.py:183
  138.0 1.2 collective-permute-start.10
  139.2 1.7 collective-permute-start.11
  140.9 2.4 %all-to-all-done.4 = bf16[128,8,128]{2,1,0:T(8,128)(2,1)} async-done(((bf16[128,8,128]{2,1,0:T(8,128)(2,1)}), bf16[128,8,128]{2,1,0:T(8,128)(2,1)}, u32[]{:S(2)}, u32[]{:S(2)}) %all-to-all-start.4) | async-done | bytes 262176 | tf_op jit(solution)/shard_map/all_to_all | solution.py:263
  143.4 1.7 sum_over_tensor.1
  145.0 2.3 %collective-permute-start.12 = (bf16[8,8,2048]{2,1,0:T(8,128)(2,1)}, bf16[8,8,2048]{2,1,0:T(8,128)(2,1)S(1)}, u32[]{:S(2)}, u32[]{:S(2)}) collective-permute-start(bf16[8,8,2048]{2,1,0:T(8,128)(2,1)} %copy-done.6), channel_id=1, source_target_pairs={{0,56},{8,48},{16,8},{24,0},{32,24},{40,16},{48,40},{56,32},{64,12... | collective-permute-start | bytes 786440 | tf_op jit(solution)/shard_map/ppermute | solution.py:215
  147.3 0.5 collective-permute-start.13
  147.9 2.7 %collective-permute-start.14 = (bf16[8,8,2048]{2,1,0:T(8,128)(2,1)}, bf16[8,8,2048]{2,1,0:T(8,128)(2,1)S(1)}, u32[]{:S(2)}, u32[]{:S(2)}) collective-permute-start(bf16[8,8,2048]{2,1,0:T(8,128)(2,1)} %copy-done.4), channel_id=1, source_target_pairs={{0,104},{8,96},{16,120},{24,112},{32,72},{40,64},{48,88},{56,80},{... | collective-permute-start | bytes 786440 | tf_op jit(solution)/shard_map/ppermute | solution.py:215
  150.5 4.0 %all-to-all-start.5 = ((bf16[8,16,8,128]{3,2,1,0:T(8,128)(2,1)}), bf16[8,16,8,128]{3,2,1,0:T(8,128)(2,1)S(1)}, u32[]{:S(2)}, u32[]{:S(2)}) async-start(bf16[8,16,8,128]{3,2,1,0:T(8,128)(2,1)} %sum_over_tensor.1), calls=%async_computation.5 | async-start | bytes 524288 | tf_op jit(solution)/shard_map/all_to_all | solution.py:263
  154.6 0.7 collective-permute-done.12.refs_4_
  155.4 5.5 %collective-permute-done.13.refs_5_ = bf16[8,8,2048]{2,1,0:T(8,128)(2,1)S(1)} collective-permute-done((bf16[8,8,2048]{2,1,0:T(8,128)(2,1)}, bf16[8,8,2048]{2,1,0:T(8,128)(2,1)S(1)}, u32[]{:S(2)}, u32[]{:S(2)}) %collective-permute-start.13) | collective-permute-done | bytes 262176 | tf_op jit(solution)/shard_map/ppermute | solution.py:215
  160.9 6.3 %collective-permute-done.14.refs_6_ = bf16[8,8,2048]{2,1,0:T(8,128)(2,1)S(1)} collective-permute-done((bf16[8,8,2048]{2,1,0:T(8,128)(2,1)}, bf16[8,8,2048]{2,1,0:T(8,128)(2,1)S(1)}, u32[]{:S(2)}, u32[]{:S(2)}) %collective-permute-start.14) | collective-permute-done | bytes 262176 | tf_op jit(solution)/shard_map/ppermute | solution.py:215
  167.1 1.8 %place_parts.3 = bf16[8,16,8,2048]{3,2,1,0:T(8,128)(2,1)} custom-call(s32[7]{0:T(128)S(1)} %slice.31.owner_ref, bf16[8,8,2048]{2,1,0:T(8,128)(2,1)S(1)} %collective-permute-done.8.refs_0_, bf16[8,8,2048]{2,1,0:T(8,128)(2,1)S(1)} %collective-permute-done.9.refs_1_, ...), custom_call_target="tpu_custom_call", output_to_operand_aliasing={{}: (8, {})} | custom-call | bytes 3670016 | tf_op jit(solution)/shard_map/place_parts/pallas_call | solution.py:183
  168.9 5.5 %all-to-all-done.5.chunks_ref = bf16[8,16,8,128]{3,2,1,0:T(8,128)(2,1)S(1)} async-done(((bf16[8,16,8,128]{3,2,1,0:T(8,128)(2,1)}), bf16[8,16,8,128]{3,2,1,0:T(8,128)(2,1)S(1)}, u32[]{:S(2)}, u32[]{:S(2)}) %all-to-all-start.5) | async-done | bytes 262176 | tf_op jit(solution)/shard_map/all_to_all | solution.py:263
  174.5 0.7 copy-done.8
  175.2 1.8 %mix.1 = bf16[8,16384]{1,0:T(8,128)(2,1)} custom-call(bf16[8,16384]{1,0:T(8,128)(2,1)} %hidden_ref.3, bf16[8,16,8,128]{3,2,1,0:T(8,128)(2,1)} %copy-done.8), custom_call_target="tpu_custom_call" | custom-call | flops 131072 | bytes 786432 | tf_op jit(solution)/shard_map/mix/pallas_call | solution.py:252
  (41 shorter events, 1.4 us)
Async XLA Ops:
  0.6 26.5 %copy-start = (bf16[1024,1,256]{2,0,1:T(8,128)(2,1)S(1)}, bf16[1024,1,256]{2,0,1:T(8,128)(2,1)}, u32[]{:S(2)}) copy-start(bf16[1024,1,256]{2,0,1:T(8,128)(2,1)} %param.12) | copy-start | bytes 1572868
  14.9 11.4 %copy-start.7 = (bf16[8,16384]{1,0:T(8,128)(2,1)S(1)}, bf16[8,16384]{1,0:T(8,128)(2,1)}, u32[]{:S(2)}) copy-start(bf16[8,16384]{1,0:T(8,128)(2,1)} %hidden_ref.3) | copy-start | bytes 786436
  14.9 61.6 %all-to-all-start.1 = ((bf16[128,8,2048]{2,1,0:T(8,128)(2,1)}), bf16[128,8,2048]{2,1,0:T(8,128)(2,1)}, u32[]{:S(2)}, u32[]{:S(2)}) async-start(bf16[128,8,2048]{2,1,0:T(8,128)(2,1)} %bitcast.60), calls=%async_computation.1 | async-start | bytes 8388608 | tf_op jit(solution)/shard_map/all_to_all | solution.py:263
  76.4 14.0 %all-to-all-start.2 = ((bf16[16,8,2304]{2,1,0:T(8,128)(2,1)}), bf16[16,8,2304]{2,1,0:T(8,128)(2,1)S(1)}, u32[]{:S(2)}, u32[]{:S(2)}) async-start(bf16[16,8,2304]{2,1,0:T(8,128)(2,1)} %bitcast.35), calls=%async_computation.2 | async-start | bytes 1179648 | tf_op jit(solution)/shard_map/all_to_all | solution.py:263
  81.0 9.4 %copy-start.3 = (s32[8]{0:T(128)S(1)}, s32[8]{0:T(128)}, u32[]{:S(2)}) copy-start(s32[8]{0:T(128)} %lengths_ref.1) | copy-start | bytes 100
  82.7 12.4 %collective-permute-start = (bf16[8,8,2048]{2,1,0:T(8,128)(2,1)S(1)}, bf16[8,8,2048]{2,1,0:T(8,128)(2,1)S(1)}, u32[]{:S(2)}, u32[]{:S(2)}) collective-permute-start(bf16[8,8,2048]{2,1,0:T(8,128)(2,1)S(1)} %get-tuple-element.56), channel_id=1, source_target_pairs={{0,16},{8,24},{16,32},{24,40},{32,48},{40,56},{48,0},{56,8},{64,80... | collective-permute-start | bytes 786440 | tf_op jit(solution)/shard_map/ppermute | solution.py:215
  83.9 12.2 %collective-permute-start.1 = (bf16[8,8,2048]{2,1,0:T(8,128)(2,1)S(1)}, bf16[8,8,2048]{2,1,0:T(8,128)(2,1)S(1)}, u32[]{:S(2)}, u32[]{:S(2)}) collective-permute-start(bf16[8,8,2048]{2,1,0:T(8,128)(2,1)S(1)} %get-tuple-element.57), channel_id=1, source_target_pairs={{0,120},{8,112},{16,72},{24,64},{32,88},{40,80},{48,104},{56,96},{... | collective-permute-start | bytes 786440 | tf_op jit(solution)/shard_map/ppermute | solution.py:215
  90.4 2.2 %copy-start.1 = (bf16[8,1,1024,256]{3,2,1,0:T(8,128)(2,1)S(1)}, bf16[8,1,1024,256]{3,2,1,0:T(8,128)(2,1)}, u32[]{:S(2)}) copy-start(bf16[8,1,1024,256]{3,2,1,0:T(8,128)(2,1)} %param.14) | copy-start | bytes 12582916
  96.1 24.8 %all-to-all-start.3 = ((bf16[16,8,2048]{2,1,0:T(8,128)(2,1)}), bf16[16,8,2048]{2,1,0:T(8,128)(2,1)S(1)}, u32[]{:S(2)}, u32[]{:S(2)}) async-start(bf16[16,8,2048]{2,1,0:T(8,128)(2,1)} %attend.1), calls=%async_computation.3 | async-start | bytes 1048576 | tf_op jit(solution)/shard_map/all_to_all | solution.py:263
  104.6 14.0 %collective-permute-start.2 = (bf16[8,8,2048]{2,1,0:T(8,128)(2,1)S(1)}, bf16[8,8,2048]{2,1,0:T(8,128)(2,1)S(1)}, u32[]{:S(2)}, u32[]{:S(2)}) collective-permute-start(bf16[8,8,2048]{2,1,0:T(8,128)(2,1)S(1)} %get-tuple-element.75), channel_id=1, source_target_pairs={{0,32},{8,40},{16,48},{24,56},{32,0},{40,8},{48,16},{56,24},{64,96... | collective-permute-start | bytes 786440 | tf_op jit(solution)/shard_map/ppermute | solution.py:215
  106.4 18.2 %collective-permute-start.3 = (bf16[8,8,2048]{2,1,0:T(8,128)(2,1)}, bf16[8,8,2048]{2,1,0:T(8,128)(2,1)S(1)}, u32[]{:S(2)}, u32[]{:S(2)}) collective-permute-start(bf16[8,8,2048]{2,1,0:T(8,128)(2,1)} %get-tuple-element.76), channel_id=1, source_target_pairs={{0,64},{8,72},{16,80},{24,88},{32,96},{40,104},{48,112},{56,120},{... | collective-permute-start | bytes 786440 | tf_op jit(solution)/shard_map/ppermute | solution.py:215
  107.5 17.3 %collective-permute-start.4 = (bf16[8,8,2048]{2,1,0:T(8,128)(2,1)}, bf16[8,8,2048]{2,1,0:T(8,128)(2,1)S(1)}, u32[]{:S(2)}, u32[]{:S(2)}) collective-permute-start(bf16[8,8,2048]{2,1,0:T(8,128)(2,1)} %get-tuple-element.77), channel_id=1, source_target_pairs={{0,8},{8,0},{16,24},{24,16},{32,40},{40,32},{48,56},{56,48},{64,72... | collective-permute-start | bytes 786440 | tf_op jit(solution)/shard_map/ppermute | solution.py:215
  111.3 24.6 %collective-permute-start.5 = (bf16[8,8,2048]{2,1,0:T(8,128)(2,1)}, bf16[8,8,2048]{2,1,0:T(8,128)(2,1)S(1)}, u32[]{:S(2)}, u32[]{:S(2)}) collective-permute-start(bf16[8,8,2048]{2,1,0:T(8,128)(2,1)} %get-tuple-element.78), channel_id=1, source_target_pairs={{0,80},{8,88},{16,96},{24,104},{32,112},{40,120},{48,64},{56,72},{... | collective-permute-start | bytes 786440 | tf_op jit(solution)/shard_map/ppermute | solution.py:215
  111.4 24.6 %collective-permute-start.6 = (bf16[8,8,2048]{2,1,0:T(8,128)(2,1)}, bf16[8,8,2048]{2,1,0:T(8,128)(2,1)S(1)}, u32[]{:S(2)}, u32[]{:S(2)}) collective-permute-start(bf16[8,8,2048]{2,1,0:T(8,128)(2,1)} %get-tuple-element.79), channel_id=1, source_target_pairs={{0,48},{8,56},{16,0},{24,8},{32,16},{40,24},{48,32},{56,40},{64,11... | collective-permute-start | bytes 786440 | tf_op jit(solution)/shard_map/ppermute | solution.py:215
  118.6 17.4 %collective-permute-start.7 = (bf16[8,8,2048]{2,1,0:T(8,128)(2,1)}, bf16[8,8,2048]{2,1,0:T(8,128)(2,1)S(1)}, u32[]{:S(2)}, u32[]{:S(2)}) collective-permute-start(bf16[8,8,2048]{2,1,0:T(8,128)(2,1)} %get-tuple-element.80), channel_id=1, source_target_pairs={{0,40},{8,32},{16,56},{24,48},{32,8},{40,0},{48,24},{56,16},{64,10... | collective-permute-start | bytes 786440 | tf_op jit(solution)/shard_map/ppermute | solution.py:215
  121.0 2.2 %copy-start.2 = (bf16[2048,1024]{1,0:T(8,128)(2,1)S(1)}, bf16[2048,1024]{1,0:T(8,128)(2,1)}, u32[]{:S(2)}) copy-start(bf16[2048,1024]{1,0:T(8,128)(2,1)} %weight_ref.1) | copy-start | bytes 12582916
  124.6 22.7 %collective-permute-start.8 = (bf16[8,8,2048]{2,1,0:T(8,128)(2,1)}, bf16[8,8,2048]{2,1,0:T(8,128)(2,1)S(1)}, u32[]{:S(2)}, u32[]{:S(2)}) collective-permute-start(bf16[8,8,2048]{2,1,0:T(8,128)(2,1)} %get-tuple-element.86), channel_id=1, source_target_pairs={{0,72},{8,64},{16,88},{24,80},{32,104},{40,96},{48,120},{56,112},{... | collective-permute-start | bytes 786440 | tf_op jit(solution)/shard_map/ppermute | solution.py:215
  124.8 23.0 %collective-permute-start.9 = (bf16[8,8,2048]{2,1,0:T(8,128)(2,1)}, bf16[8,8,2048]{2,1,0:T(8,128)(2,1)S(1)}, u32[]{:S(2)}, u32[]{:S(2)}) collective-permute-start(bf16[8,8,2048]{2,1,0:T(8,128)(2,1)} %get-tuple-element.87), channel_id=1, source_target_pairs={{0,24},{8,16},{16,40},{24,32},{32,56},{40,48},{48,8},{56,0},{64,88... | collective-permute-start | bytes 786440 | tf_op jit(solution)/shard_map/ppermute | solution.py:215
  127.2 16.1 %all-to-all-start.4 = ((bf16[128,8,128]{2,1,0:T(8,128)(2,1)}), bf16[128,8,128]{2,1,0:T(8,128)(2,1)}, u32[]{:S(2)}, u32[]{:S(2)}) async-start(bf16[128,8,128]{2,1,0:T(8,128)(2,1)} %bitcast.38), calls=%async_computation.4 | async-start | bytes 524288 | tf_op jit(solution)/shard_map/all_to_all | solution.py:263
  135.9 2.1 %copy-start.4 = (bf16[8,8,2048]{2,1,0:T(8,128)(2,1)}, bf16[8,8,2048]{2,1,0:T(8,128)(2,1)S(1)}, u32[]{:S(2)}) copy-start(bf16[8,8,2048]{2,1,0:T(8,128)(2,1)S(1)} %get-tuple-element.92) | copy-start | bytes 786436
  135.9 3.3 %copy-start.5 = (bf16[8,8,2048]{2,1,0:T(8,128)(2,1)}, bf16[8,8,2048]{2,1,0:T(8,128)(2,1)S(1)}, u32[]{:S(2)}) copy-start(bf16[8,8,2048]{2,1,0:T(8,128)(2,1)S(1)} %get-tuple-element.91) | copy-start | bytes 786436
  135.9 3.3 %copy-start.6 = (bf16[8,8,2048]{2,1,0:T(8,128)(2,1)}, bf16[8,8,2048]{2,1,0:T(8,128)(2,1)S(1)}, u32[]{:S(2)}) copy-start(bf16[8,8,2048]{2,1,0:T(8,128)(2,1)S(1)} %get-tuple-element.90) | copy-start | bytes 786436
  138.0 16.6 %collective-permute-start.10 = (bf16[8,8,2048]{2,1,0:T(8,128)(2,1)}, bf16[8,8,2048]{2,1,0:T(8,128)(2,1)S(1)}, u32[]{:S(2)}, u32[]{:S(2)}) collective-permute-start(bf16[8,8,2048]{2,1,0:T(8,128)(2,1)} %get-tuple-element.88), channel_id=1, source_target_pairs={{0,112},{8,120},{16,64},{24,72},{32,80},{40,88},{48,96},{56,104},{... | collective-permute-start | bytes 786440 | tf_op jit(solution)/shard_map/ppermute | solution.py:215
  139.2 15.4 %collective-permute-start.11 = (bf16[8,8,2048]{2,1,0:T(8,128)(2,1)}, bf16[8,8,2048]{2,1,0:T(8,128)(2,1)S(1)}, u32[]{:S(2)}, u32[]{:S(2)}) collective-permute-start(bf16[8,8,2048]{2,1,0:T(8,128)(2,1)} %get-tuple-element.89), channel_id=1, source_target_pairs={{0,88},{8,80},{16,104},{24,96},{32,120},{40,112},{48,72},{56,64},{... | collective-permute-start | bytes 786440 | tf_op jit(solution)/shard_map/ppermute | solution.py:215
  145.0 10.3 %collective-permute-start.12 = (bf16[8,8,2048]{2,1,0:T(8,128)(2,1)}, bf16[8,8,2048]{2,1,0:T(8,128)(2,1)S(1)}, u32[]{:S(2)}, u32[]{:S(2)}) collective-permute-start(bf16[8,8,2048]{2,1,0:T(8,128)(2,1)} %copy-done.6), channel_id=1, source_target_pairs={{0,56},{8,48},{16,8},{24,0},{32,24},{40,16},{48,40},{56,32},{64,12... | collective-permute-start | bytes 786440 | tf_op jit(solution)/shard_map/ppermute | solution.py:215
  147.3 13.5 %collective-permute-start.13 = (bf16[8,8,2048]{2,1,0:T(8,128)(2,1)}, bf16[8,8,2048]{2,1,0:T(8,128)(2,1)S(1)}, u32[]{:S(2)}, u32[]{:S(2)}) collective-permute-start(bf16[8,8,2048]{2,1,0:T(8,128)(2,1)} %copy-done.5), channel_id=1, source_target_pairs={{0,96},{8,104},{16,112},{24,120},{32,64},{40,72},{48,80},{56,88},{... | collective-permute-start | bytes 786440 | tf_op jit(solution)/shard_map/ppermute | solution.py:215
  147.9 19.2 %collective-permute-start.14 = (bf16[8,8,2048]{2,1,0:T(8,128)(2,1)}, bf16[8,8,2048]{2,1,0:T(8,128)(2,1)S(1)}, u32[]{:S(2)}, u32[]{:S(2)}) collective-permute-start(bf16[8,8,2048]{2,1,0:T(8,128)(2,1)} %copy-done.4), channel_id=1, source_target_pairs={{0,104},{8,96},{16,120},{24,112},{32,72},{40,64},{48,88},{56,80},{... | collective-permute-start | bytes 786440 | tf_op jit(solution)/shard_map/ppermute | solution.py:215
  150.5 24.0 %all-to-all-start.5 = ((bf16[8,16,8,128]{3,2,1,0:T(8,128)(2,1)}), bf16[8,16,8,128]{3,2,1,0:T(8,128)(2,1)S(1)}, u32[]{:S(2)}, u32[]{:S(2)}) async-start(bf16[8,16,8,128]{3,2,1,0:T(8,128)(2,1)} %sum_over_tensor.1), calls=%async_computation.5 | async-start | bytes 524288 | tf_op jit(solution)/shard_map/all_to_all | solution.py:263
  174.5 0.7 copy-start.8
